TPU v7x, 32 devices: a whole 2x2x4 slice. The times are simulated.
32 devices in a mesh: dp: 16 (over z, x, core), tensor: 2 (over y).
Axes of the slice: x: 2, y: 2, z: 4, core: 2. Of those that a mesh axis runs over, the one named last changes fastest.
Arguments:
- tokens_in: bfloat16 [16, 256, 2048], P('dp'), may hold values from -6 to 6
- segment_ids: int32 [16, 256], P('dp'), may hold values from 0 to 3, never falling along the last dimension, each value on 1 to 128 neighbouring positions
- d_out: bfloat16 [16, 256, 2048], P('dp'), may hold values from -6 to 6
- qkv_weight: float32 [2048, 3, 2048], P('dp', None, 'tensor'), may hold values from -0.125 to 0.125
- qkv_bias: float32 [2, 3072], P('tensor', 'dp'), may hold values from -1.8 to 1.8
- out_weight: float32 [2048, 2048], P('tensor', 'dp'), may hold values from -0.5 to 0.5
- gating_weight: float32 [2048, 2, 5632], P('dp', None, 'tensor'), may hold values from -0.125 to 0.125
- down_weight: float32 [5632, 2048], P('tensor', 'dp'), may hold values from -0.078125 to 0.078125
- norm_params: float32 [4, 2048], P(None, 'dp'), may hold values from -1.2 to 1.5, as said below
- qkv_first: float32 [2048, 3, 2048], P('dp', None, 'tensor'), may hold values from -80 to 80
- qkv_second: float32 [2048, 3, 2048], P('dp', None, 'tensor'), may hold values from 860.16 to 3440.64
- bias_first: float32 [2, 3072], P('tensor', 'dp'), may hold values from -80 to 80
- bias_second: float32 [2, 3072], P('tensor', 'dp'), may hold values from 860.16 to 3440.64
- out_first: float32 [2048, 2048], P('tensor', 'dp'), may hold values from -16 to 16
- out_second: float32 [2048, 2048], P('tensor', 'dp'), may hold values from 34.4064 to 139.264
- gating_first: float32 [2048, 2, 5632], P('dp', None, 'tensor'), may hold values from -16 to 16
- gating_second: float32 [2048, 2, 5632], P('dp', None, 'tensor'), may hold values from 26.2144 to 106.496
- down_first: float32 [5632, 2048], P('tensor', 'dp'), may hold values from -24 to 24
- down_second: float32 [5632, 2048], P('tensor', 'dp'), may hold values from 77.824 to 311.296
- norm_first: float32 [4, 2048], P(None, 'dp'), may hold values from -64 to 64
- norm_second: float32 [4, 2048], P(None, 'dp'), may hold values from 491.52 to 1925.12
Outputs:
- block_out: float32 [16, 256, 2048], P('dp')
- input_grad: float32 [16, 256, 2048], P('dp')
- qkv_updated: float32 [2048, 3, 2048], P('dp', None, 'tensor')
- qkv_mean: float32 [2048, 3, 2048], P('dp', None, 'tensor')
- qkv_square: float32 [2048, 3, 2048], P('dp', None, 'tensor')
- bias_updated: float32 [2, 3072], P('tensor', 'dp')
- bias_mean: float32 [2, 3072], P('tensor', 'dp')
- bias_square: float32 [2, 3072], P('tensor', 'dp')
- out_updated: float32 [2048, 2048], P('tensor', 'dp')
- out_mean: float32 [2048, 2048], P('tensor', 'dp')
- out_square: float32 [2048, 2048], P('tensor', 'dp')
- gating_updated: float32 [2048, 2, 5632], P('dp', None, 'tensor')
- gating_mean: float32 [2048, 2, 5632], P('dp', None, 'tensor')
- gating_square: float32 [2048, 2, 5632], P('dp', None, 'tensor')
- down_updated: float32 [5632, 2048], P('tensor', 'dp')
- down_mean: float32 [5632, 2048], P('tensor', 'dp')
- down_square: float32 [5632, 2048], P('tensor', 'dp')
- norm_updated: float32 [4, 2048], P(None, 'dp')
- norm_mean: float32 [4, 2048], P(None, 'dp')
- norm_square: float32 [4, 2048], P(None, 'dp')
Inputs may be any that keep to these rules, and one draw needn't show every extreme that they name: `segment_ids`: along each sequence the ids never fall; a document holds 1 to 128 tokens, and some document holds exactly 128. `norm_params`: rows 0 and 2 lie between 0.5 and 1.5, rows 1 and 3 between -1.2 and 1.2.
All inputs are finite; a program needn't handle non-finite values.
Results may differ from a plain program's by a relative error of at most 0.014.
Values may be sent and summed in bfloat16 or wider, within the bound.
A program may use at most 320 MiB of HBM per device.

v0:
```python
import math

import jax
import jax.numpy as jnp
from jax import lax
from jax.sharding import PartitionSpec as P

D = 2048
H = 32
HD = 64
ROT = 16
FF = 5632
STEP = 10


def layer_norm(values, scale_row, shift_row):
    centre = values - jnp.mean(values, axis=-1, keepdims=True)
    spread = jnp.mean(centre * centre, axis=-1, keepdims=True)
    inverse = lax.rsqrt(spread + 1e-05)
    scaled = centre * inverse
    return (scaled * scale_row + shift_row, scaled, inverse)


def norm_back(grad_in, scaled, inverse, scale_row):
    grad_scaled = grad_in * scale_row
    mean_first = jnp.mean(grad_scaled, axis=-1, keepdims=True)
    mean_second = jnp.mean(grad_scaled * scaled, axis=-1, keepdims=True)
    grad_values = inverse * (grad_scaled - mean_first - scaled * mean_second)
    return (grad_values, jnp.sum(grad_in * scaled, axis=0), jnp.sum(grad_in, axis=0))


def doc_positions(segments):
    seq_len = segments.shape[-1]
    earlier = jnp.sum((segments[None, :] < segments[:, None]).astype(jnp.int32), axis=1)
    return (jnp.arange(seq_len, dtype=jnp.int32) - earlier).astype(jnp.float32)


def rotary_tables(positions):
    half_rot = ROT // 2
    frequency = 10000.0 ** (-2.0 * jnp.arange(half_rot, dtype=jnp.float32) / ROT)
    angles = positions[:, None] * frequency[None, :]
    return (jnp.cos(angles), jnp.sin(angles))


def rotate(values, cosine, sine_part):
    half_rot = ROT // 2
    first_half = values[..., :half_rot]
    second = values[..., half_rot:ROT]
    cos_wide = cosine[:, None, :]
    sin_wide = sine_part[:, None, :]
    return jnp.concatenate(
        [
            first_half * cos_wide - second * sin_wide,
            second * cos_wide + first_half * sin_wide,
            values[..., ROT:],
        ],
        axis=-1,
    )


def adamw_update(weight_old, gradient, first_old, second_old, step_rate, decay_rate):
    first_new = 0.9 * first_old + 0.1 * gradient
    second_new = 0.95 * second_old + 0.05 * gradient * gradient
    corrected = first_new / (1.0 - 0.9**STEP) / (jnp.sqrt(second_new / (1.0 - 0.95**STEP)) + 1e-08)
    return (weight_old - step_rate * (corrected + decay_rate * weight_old), first_new, second_new)


def per_device(
    tokens_in,
    segment_ids,
    d_out,
    qkv_weight,
    qkv_bias,
    out_weight,
    gating_weight,
    down_weight,
    norm_params,
    qkv_first,
    qkv_second,
    bias_first,
    bias_second,
    out_first,
    out_second,
    gating_first,
    gating_second,
    down_first,
    down_second,
    norm_first,
    norm_second,
):
    qkv_full, bias_full, norm_full, out_full = (
        lax.all_gather(qkv_weight.astype(jnp.bfloat16), "dp", axis=0, tiled=True),
        lax.all_gather(qkv_bias.astype(jnp.bfloat16), "dp", axis=1, tiled=True),
        lax.all_gather(norm_params.astype(jnp.bfloat16), "dp", axis=1, tiled=True),
        lax.all_gather(out_weight.astype(jnp.bfloat16), "dp", axis=1, tiled=True),
    )
    gating_full, down_full = (
        lax.all_gather(gating_weight.astype(jnp.bfloat16), "dp", axis=0, tiled=True),
        lax.all_gather(down_weight.astype(jnp.bfloat16), "dp", axis=1, tiled=True),
    )
    model_width = qkv_full.shape[0]
    head_local = qkv_full.shape[2]
    heads_here = head_local // HD
    hidden_local = gating_full.shape[2]
    seq_len = tokens_in.shape[1]
    scale_factor = HD ** (-0.5)
    norm_rows = norm_full.astype(jnp.float32)
    tokens = tokens_in[0].astype(jnp.float32)
    segments = segment_ids[0]
    token_order = jnp.arange(seq_len)
    allowed = (segments[:, None] == segments[None, :]) & (
        token_order[:, None] >= token_order[None, :]
    )
    cosine, sine_part = rotary_tables(doc_positions(segments))
    normed_one, scaled_one, inverse_one = layer_norm(tokens, norm_rows[0], norm_rows[1])
    normed_one = normed_one.astype(jnp.bfloat16)
    qkv_matrix = qkv_full.reshape(model_width, 3 * head_local)
    bias_row = bias_full.astype(jnp.float32).reshape(3 * head_local)
    projected = jnp.dot(normed_one, qkv_matrix, preferred_element_type=jnp.float32) + bias_row
    query_raw = projected[:, :head_local].reshape(seq_len, heads_here, HD)
    key_raw = projected[:, head_local : 2 * head_local].reshape(seq_len, heads_here, HD)
    value_raw = projected[:, 2 * head_local :].reshape(seq_len, heads_here, HD)

    def rotate_pair(query_in, key_in):
        return (rotate(query_in, cosine, sine_part), rotate(key_in, cosine, sine_part))

    (query_rot, key_rot), rotate_back = jax.vjp(rotate_pair, query_raw, key_raw)
    group_heads = math.gcd(heads_here, 4)
    group_count = heads_here // group_heads

    def to_groups(stacked):
        return stacked.transpose(1, 0, 2).reshape(group_count, group_heads, seq_len, HD)

    def from_groups(stacked):
        return stacked.reshape(heads_here, seq_len, HD).transpose(1, 0, 2)

    query_grp = to_groups(query_rot.astype(jnp.bfloat16))
    key_grp = to_groups(key_rot.astype(jnp.bfloat16))
    value_grp = to_groups(value_raw.astype(jnp.bfloat16))

    def masked_scores(query_blk, key_blk):
        raw_scores = (
            jnp.einsum("hqd,hkd->hqk", query_blk, key_blk, preferred_element_type=jnp.float32)
            * scale_factor
        )
        return jnp.where(allowed[None], raw_scores, -1e30)

    def attend_forward(block_in):
        query_blk, key_blk, value_blk = block_in
        scores = masked_scores(query_blk, key_blk)
        row_top = jnp.max(scores, axis=-1, keepdims=True)
        weights = jnp.exp(scores - row_top)
        row_total = jnp.sum(weights, axis=-1, keepdims=True)
        probability = (weights / row_total).astype(jnp.bfloat16)
        attended_blk = jnp.einsum(
            "hqk,hkd->hqd", probability, value_blk, preferred_element_type=jnp.float32
        )
        return (attended_blk, (row_top + jnp.log(row_total))[..., 0])

    attended_grp, log_totals = lax.map(attend_forward, (query_grp, key_grp, value_grp))
    attended = from_groups(attended_grp).reshape(seq_len, head_local).astype(jnp.bfloat16)
    attention_term = lax.psum(
        jnp.dot(attended, out_full, preferred_element_type=jnp.float32), "tensor"
    )
    residual = tokens + attention_term
    normed_two, scaled_two, inverse_two = layer_norm(residual, norm_rows[2], norm_rows[3])
    normed_two = normed_two.astype(jnp.bfloat16)
    gating_matrix = gating_full.reshape(model_width, 2 * hidden_local)
    gated_out = jnp.dot(normed_two, gating_matrix, preferred_element_type=jnp.float32)
    gate_part = gated_out[:, :hidden_local]
    up_part = gated_out[:, hidden_local:]
    hidden = (jax.nn.silu(gate_part) * up_part).astype(jnp.bfloat16)
    feedforward_term = lax.psum(
        jnp.dot(hidden, down_full, preferred_element_type=jnp.float32).astype(jnp.bfloat16),
        "tensor",
    ).astype(jnp.float32)
    block_out = residual + feedforward_term
    cotangent = d_out[0]
    grad_down = jnp.dot(hidden.T, cotangent, preferred_element_type=jnp.float32)
    grad_hidden = jnp.dot(cotangent, down_full.T, preferred_element_type=jnp.float32)
    sigmoid_gate = jax.nn.sigmoid(gate_part)
    grad_gate = (
        grad_hidden * up_part * sigmoid_gate * (1.0 + gate_part * (1.0 - sigmoid_gate))
    ).astype(jnp.bfloat16)
    grad_up = (grad_hidden * (gate_part * sigmoid_gate)).astype(jnp.bfloat16)
    grad_gated = jnp.concatenate([grad_gate, grad_up], axis=1)
    grad_gating_gate = jnp.dot(normed_two.T, grad_gate, preferred_element_type=jnp.float32)
    grad_gating_up = jnp.dot(normed_two.T, grad_up, preferred_element_type=jnp.float32)
    normed_grad_two = lax.psum(
        jnp.dot(grad_gated, gating_matrix.T, preferred_element_type=jnp.float32), "tensor"
    )
    residual_part, gain_two, shift_two = norm_back(
        normed_grad_two, scaled_two, inverse_two, norm_rows[2]
    )
    residual_grad = cotangent.astype(jnp.float32) + residual_part
    residual_low = residual_grad.astype(jnp.bfloat16)
    grad_out = jnp.dot(attended.T, residual_low, preferred_element_type=jnp.float32)
    grad_attended = to_groups(
        jnp.dot(residual_low, out_full.T, preferred_element_type=jnp.float32)
        .astype(jnp.bfloat16)
        .reshape(seq_len, heads_here, HD)
    )

    def attend_backward(block_in):
        query_blk, key_blk, value_blk, grad_blk, total_blk = block_in
        probability = jnp.exp(masked_scores(query_blk, key_blk) - total_blk[..., None])
        grad_value = jnp.einsum(
            "hqk,hqd->hkd",
            probability.astype(jnp.bfloat16),
            grad_blk,
            preferred_element_type=jnp.float32,
        )
        grad_prob = jnp.einsum(
            "hqd,hkd->hqk", grad_blk, value_blk, preferred_element_type=jnp.float32
        )
        centre = jnp.sum(probability * grad_prob, axis=-1, keepdims=True)
        grad_scores = (probability * (grad_prob - centre)).astype(jnp.bfloat16)
        grad_query = (
            jnp.einsum("hqk,hkd->hqd", grad_scores, key_blk, preferred_element_type=jnp.float32)
            * scale_factor
        )
        grad_key = (
            jnp.einsum("hqk,hqd->hkd", grad_scores, query_blk, preferred_element_type=jnp.float32)
            * scale_factor
        )
        return (grad_query, grad_key, grad_value)

    grad_query_grp, grad_key_grp, grad_value_grp = lax.map(
        attend_backward, (query_grp, key_grp, value_grp, grad_attended, log_totals)
    )
    grad_query_raw, grad_key_raw = rotate_back(
        (from_groups(grad_query_grp), from_groups(grad_key_grp))
    )
    grad_projected = jnp.concatenate(
        [
            grad_query_raw.reshape(seq_len, head_local),
            grad_key_raw.reshape(seq_len, head_local),
            from_groups(grad_value_grp).reshape(seq_len, head_local),
        ],
        axis=1,
    ).astype(jnp.bfloat16)
    grad_bias = jnp.sum(grad_projected, axis=0, dtype=jnp.float32).reshape(1, 3 * head_local)
    grad_qkv = jnp.dot(normed_one.T, grad_projected, preferred_element_type=jnp.float32).reshape(
        model_width, 3, head_local
    )
    normed_grad_one = lax.psum(
        jnp.dot(grad_projected, qkv_matrix.T, preferred_element_type=jnp.float32).astype(
            jnp.bfloat16
        ),
        "tensor",
    ).astype(jnp.float32)
    input_part, gain_one, shift_one = norm_back(
        normed_grad_one, scaled_one, inverse_one, norm_rows[0]
    )
    input_grad = residual_grad + input_part
    qkv_shard, bias_shard, out_shard, gate_shard, up_shard, down_shard, norm_shard = (
        lax.psum_scatter(grad_qkv, "dp", scatter_dimension=0, tiled=True),
        lax.psum_scatter(grad_bias, "dp", scatter_dimension=1, tiled=True),
        lax.psum_scatter(grad_out, "dp", scatter_dimension=1, tiled=True),
        lax.psum_scatter(grad_gating_gate, "dp", scatter_dimension=0, tiled=True),
        lax.psum_scatter(grad_gating_up, "dp", scatter_dimension=0, tiled=True),
        lax.psum_scatter(grad_down, "dp", scatter_dimension=1, tiled=True),
        lax.psum_scatter(
            jnp.stack([gain_one, shift_one, gain_two, shift_two]),
            "dp",
            scatter_dimension=1,
            tiled=True,
        ),
    )
    gating_shard = jnp.stack([gate_shard, up_shard], axis=1)
    qkv_updated, qkv_mean, qkv_square = adamw_update(
        qkv_weight, qkv_shard, qkv_first, qkv_second, D ** (-0.5), 0.1
    )
    bias_updated, bias_mean, bias_square = adamw_update(
        qkv_bias, bias_shard, bias_first, bias_second, 0.3, 0.0
    )
    out_updated, out_mean, out_square = adamw_update(
        out_weight, out_shard, out_first, out_second, (H * HD // 16) ** (-0.5), 0.1
    )
    gating_updated, gating_mean, gating_square = adamw_update(
        gating_weight, gating_shard, gating_first, gating_second, D ** (-0.5), 0.1
    )
    down_updated, down_mean, down_square = adamw_update(
        down_weight, down_shard, down_first, down_second, FF ** (-0.5), 0.1
    )
    norm_updated, norm_mean, norm_square = adamw_update(
        norm_params, norm_shard, norm_first, norm_second, 0.25, 0.0
    )
    return (
        block_out[None],
        input_grad[None],
        qkv_updated,
        qkv_mean,
        qkv_square,
        bias_updated,
        bias_mean,
        bias_square,
        out_updated,
        out_mean,
        out_square,
        gating_updated,
        gating_mean,
        gating_square,
        down_updated,
        down_mean,
        down_square,
        norm_updated,
        norm_mean,
        norm_square,
    )


def solution(mesh):
    placed = (
        P("dp", None, None),
        P("dp", None),
        P("dp", None, None),
        P("dp", None, "tensor"),
        P("tensor", "dp"),
        P("tensor", "dp"),
        P("dp", None, "tensor"),
        P("tensor", "dp"),
        P(None, "dp"),
        P("dp", None, "tensor"),
        P("dp", None, "tensor"),
        P("tensor", "dp"),
        P("tensor", "dp"),
        P("tensor", "dp"),
        P("tensor", "dp"),
        P("dp", None, "tensor"),
        P("dp", None, "tensor"),
        P("tensor", "dp"),
        P("tensor", "dp"),
        P(None, "dp"),
        P(None, "dp"),
    )
    return jax.shard_map(
        per_device,
        mesh=mesh,
        in_specs=placed,
        out_specs=(
            P("dp", None, None),
            P("dp", None, None),
            P("dp", None, "tensor"),
            P("dp", None, "tensor"),
            P("dp", None, "tensor"),
            P("tensor", "dp"),
            P("tensor", "dp"),
            P("tensor", "dp"),
            P("tensor", "dp"),
            P("tensor", "dp"),
            P("tensor", "dp"),
            P("dp", None, "tensor"),
            P("dp", None, "tensor"),
            P("dp", None, "tensor"),
            P("tensor", "dp"),
            P("tensor", "dp"),
            P("tensor", "dp"),
            P(None, "dp"),
            P(None, "dp"),
            P(None, "dp"),
        ),
        check_vma=False,
    )
```

profile of v0, /device:TPU:0, one launch (start us, length us, event | category | flops | bytes accessed | tf_op | source)
XLA Modules:
  0.0 1855.5 jit_solution(14126233544321062350)
XLA Ops:
  7.2 2.6 copy.99
  13.2 36.4 %all-reduce.6 = bf16[3072]{0:T(1024)(128)(2,1)S(1)} all-reduce(bf16[3072]{0:T(1024)(128)(2,1)S(1)} %dynamic-update-slice), channel_id=1, replica_groups=mesh['dp'=16,'tensor'=2] {'dp'}, use_global_device_ids=true, to_apply=%add.6 | all-reduce | flops 3072 | bytes 12288
  49.7 17.3 all_gather.18
  69.3 50.0 %all-gather.5.cloned.1.call-done = bf16[2048,3,1024]{0,2,1:T(8,128)(2,1)} async-done(((bf16[128,3,1024]{0,2,1:T(8,128)(2,1)}), bf16[2048,3,1024]{0,2,1:T(8,128)(2,1)}) %all-gather.5.cloned.1.call-update) | async-done | bytes 12582928 | tf_op jit(solution)/shard_map/all_gather | solution.py:92
  119.3 6.5 convolution_add_fusion
  129.9 2.0 copy.102
  133.2 12.3 while.30
  145.4 27.2 %all-gather.7.cloned.1.call-done = bf16[1024,2048]{1,0:T(8,128)(2,1)} async-done(((bf16[1024,128]{1,0:T(8,128)(2,1)}), bf16[1024,2048]{1,0:T(8,128)(2,1)}) %all-gather.7.cloned.1.call-update) | async-done | bytes 4194320 | tf_op jit(solution)/shard_map/all_gather | solution.py:95
  172.6 4.9 fusion.108
  177.6 4.0 convert_element_type.128
  183.2 55.6 %all-reduce.12.cloned.1.call-done = f32[256,2048]{1,0:T(8,128)} async-done(((f32[256,2048]{1,0:T(8,128)}), f32[256,2048]{1,0:T(8,128)}) %all-reduce.12.cloned.1.call-update) | async-done | bytes 2097168 | tf_op jit(solution)/shard_map/psum | solution.py:162
  241.1 118.6 %all-gather.9.cloned.1.call-done = bf16[2048,2,2816]{2,1,0:T(2,128)(2,1)} async-done(((bf16[128,2,2816]{2,1,0:T(2,128)(2,1)}), bf16[2048,2,2816]{2,1,0:T(2,128)(2,1)}) %all-gather.9.cloned.1.call-update) | async-done | bytes 23068688 | tf_op jit(solution)/shard_map/all_gather | solution.py:98
  359.7 24.3 %copy.122 = bf16[256,8,2,2816]{3,1,2,0:T(8,128)(2,1)} copy(bf16[256,8,2,2816]{3,2,1,0:T(2,128)(2,1)} %bitcast.238) | data formatting | bytes 46137344
  384.0 13.4 fusion.107
  397.4 62.5 %all-gather.11.cloned.1.call-done = bf16[2816,2048]{1,0:T(8,128)(2,1)} async-done(((bf16[2816,128]{1,0:T(8,128)(2,1)}), bf16[2816,2048]{1,0:T(8,128)(2,1)}) %all-gather.11.cloned.1.call-update) | async-done | bytes 11534352 | tf_op jit(solution)/shard_map/all_gather | solution.py:99
  459.9 12.4 multiply_convert_fusion.2
  472.2 12.5 fusion.52
  485.0 9.5 convolution_convert_fusion
  494.6 51.5 %all-reduce.14.cloned.1.call-done = f32[256,2048]{1,0:T(8,128)} async-done(((f32[256,2048]{1,0:T(8,128)}), f32[256,2048]{1,0:T(8,128)}) %all-reduce.14.cloned.1.call-update) | async-done | bytes 2097168 | tf_op jit(solution)/shard_map/psum | solution.py:189
  546.1 2.6 multiply_reduce_fusion.1
  551.7 2.1 convolution_convert_fusion.2
  553.8 2.0 copy.103
  555.8 37.9 %while.31 = (s32[]{:T(128)}, f32[4,4,256,64]{2,3,1,0:T(8,128)}, f32[4,4,256,64]{2,3,1,0:T(8,128)}, bf16[4,4,256,64]{2,3,1,0:T(8,128)(2,1)}, bf16[4,4,256,64]{2,3...) while((s32[]{:T(128)}, f32[4,4,256,64]{2,3,1,0:T(8,128)}, ...), condition=%wide.region_16.17_spmd.clone.clone, body=%wide.region_14.16_spmd.clone.sunk.clone | while | flops 170458112 | bytes 13920425 | solution.py:228
  589.8 1.9 fusion.179
  598.9 7.6 convolution_convert_fusion.1
  608.3 61.5 %all-reduce.16.cloned.1.call-done = (bf16[256,2048]{1,0:T(8,128)(2,1)}, bf16[256,2048]{1,0:T(8,128)(2,1)}) async-done(((bf16[256,2048]{1,0:T(8,128)(2,1)}, bf16[256,2048]{1,0:T(8,128)(2,1)}), (bf16[256,2048]{1,0:T(8,128)(2,1)}, bf16[256,2048]{1,0:T(8,128)(2,1)})) %all-reduce.16.cloned.1.call-update) | async-done | bytes 2097168 | tf_op jit(solution)/shard_map/psum | solution.py:173
  669.7 2.3 fusion.73
  673.7 6.3 fusion.84
  680.1 11.3 fusion.105
  691.5 11.2 fusion.106
  702.8 12.6 fusion.78
  716.1 11.8 fusion.76
  727.9 6.0 reduce-scatter.22.cloned.1.call-done
  735.5 3.1 add_bitcast_fusion
  738.6 2.2 fusion.66
  740.8 53.7 %reduce-scatter.24.cloned.1.call-done = f32[128,4]{1,0:T(8,128)} async-done(((f32[2048,4]{1,0:T(8,128)}), f32[128,4]{1,0:T(8,128)}) %reduce-scatter.24.cloned.1.call-update) | async-done | bytes 2064
  796.0 106.9 %reduce-scatter.14.cloned.1.call-done = f32[1024,128]{1,0:T(8,128)} async-done(((f32[1024,2048]{1,0:T(8,128)}), f32[1024,128]{1,0:T(8,128)}) %reduce-scatter.14.cloned.1.call-update) | async-done | bytes 524304 | tf_op jit(solution)/shard_map/reduce_scatter | solution.py:259
  902.9 2.9 multiply_subtract_fusion.3
  905.8 228.4 %reduce-scatter.18.cloned.1.call-done = f32[128,2816]{1,0:T(8,128)} async-done(((f32[2048,2816]{1,0:T(8,128)}), f32[128,2816]{1,0:T(8,128)}) %reduce-scatter.18.cloned.1.call-update) | async-done | bytes 1441808 | tf_op jit(solution)/shard_map/reduce_scatter | solution.py:261
  1134.2 230.5 %reduce-scatter.16.cloned.1.call-done = f32[128,2816]{1,0:T(8,128)} async-done(((f32[2048,2816]{1,0:T(8,128)}), f32[128,2816]{1,0:T(8,128)}) %reduce-scatter.16.cloned.1.call-update) | async-done | bytes 1441808 | tf_op jit(solution)/shard_map/reduce_scatter | solution.py:260
  1364.8 5.0 multiply_subtract_fusion
  1369.7 3.8 copy.109
  1373.5 4.0 copy.110
  1377.6 4.0 copy.111
  1381.5 213.9 %reduce-scatter.20.cloned.1.call-done = f32[2816,128]{1,0:T(8,128)} async-done(((f32[2816,2048]{1,0:T(8,128)}), f32[2816,128]{1,0:T(8,128)}) %reduce-scatter.20.cloned.1.call-update) | async-done | bytes 1441808 | tf_op jit(solution)/shard_map/reduce_scatter | solution.py:262
  1595.4 4.9 multiply_subtract_fusion.2
  1600.4 242.6 %reduce-scatter.12.cloned.1.call-done = f32[128,3,1024]{2,0,1:T(8,128)} async-done(((f32[2048,3,1024]{2,0,1:T(8,128)}), f32[128,3,1024]{2,0,1:T(8,128)}) %reduce-scatter.12.cloned.1.call-update) | async-done | bytes 1572880 | tf_op jit(solution)/shard_map/reduce_scatter | solution.py:257
  1842.9 5.6 multiply_subtract_fusion.1
  (237 shorter events, 77.5 us)
Async XLA Ops:
  7.2 2.8 copy-start.19
  7.2 112.1 %all-gather.5.cloned.1.call-start = ((), (), s32[]{:S(2)}) async-start(), calls=%async_computation.7 | async-start | bytes 13369344 | tf_op jit(solution)/shard_map/all_gather | solution.py:92
  9.9 39.8 %copy-start.31 = (f32[4,128]{1,0:T(4,128)S(1)}, f32[4,128]{1,0:T(4,128)}, u32[]{:S(2)}) copy-start(f32[4,128]{1,0:T(4,128)} %param.33) | copy-start | bytes 6148
  9.9 57.2 %copy-start = (bf16[1,256,2048]{2,1,0:T(8,128)(2,1)S(1)}, bf16[1,256,2048]{2,1,0:T(8,128)(2,1)}, u32[]{:S(2)}) copy-start(bf16[1,256,2048]{2,1,0:T(8,128)(2,1)} %param.25) | copy-start | bytes 3145732
  9.9 57.4 %copy-start.21 = (s32[1,256]{1,0:T(1,128)S(1)}, s32[1,256]{1,0:T(1,128)}, u32[]{:S(2)}) copy-start(s32[1,256]{1,0:T(1,128)} %param.26) | copy-start | bytes 3076
  9.9 162.7 %all-gather.7.cloned.1.call-start = ((), (), s32[]{:S(2)}) async-start(), calls=%async_computation.8 | async-start | bytes 4456448 | tf_op jit(solution)/shard_map/all_gather | solution.py:95
  10.7 228.1 %all-reduce.12.cloned.1.call-start = ((), (), s32[]{:S(2)}) async-start(), calls=%async_computation.9 | async-start | bytes 4194304 | tf_op jit(solution)/shard_map/psum | solution.py:162
  10.8 115.0 %copy-start.11 = (bf16[4,4,256,64]{2,3,1,0:T(8,128)(2,1)}, bf16[4,4,256,64]{2,3,1,0:T(8,128)(2,1)S(1)}, u32[]{:S(2)}) copy-start(bf16[4,4,256,64]{2,3,1,0:T(8,128)(2,1)S(1)} %fusion.103) | copy-start | bytes 1572868
  67.9 58.0 %copy-start.29 = (f32[256]{0:T(256)}, f32[256]{0:T(256)S(1)}, u32[]{:S(2)}) copy-start(f32[256]{0:T(256)S(1)} %add_rsqrt_fusion.1) | copy-start | bytes 3076
  69.3 56.6 %copy-start.23 = (f32[1,2048]{1,0:T(1,128)}, f32[1,2048]{1,0:T(1,128)S(1)}, u32[]{:S(2)}) copy-start(f32[1,2048]{1,0:T(1,128)S(1)} %get-tuple-element.326) | copy-start | bytes 24580
  69.3 56.6 %copy-start.27 = (f32[1,2048]{1,0:T(1,128)}, f32[1,2048]{1,0:T(1,128)S(1)}, u32[]{:S(2)}) copy-start(f32[1,2048]{1,0:T(1,128)S(1)} %get-tuple-element.327) | copy-start | bytes 24580
  145.4 32.1 %copy-start.4 = (bf16[4,4,256,64]{2,3,1,0:T(8,128)(2,1)}, bf16[4,4,256,64]{2,3,1,0:T(8,128)(2,1)S(1)}, u32[]{:S(2)}) copy-start(bf16[4,4,256,64]{2,3,1,0:T(8,128)(2,1)S(1)} %get-tuple-element.568) | copy-start | bytes 1572868
  145.4 32.1 %copy-start.5 = (bf16[4,4,256,64]{2,3,1,0:T(8,128)(2,1)}, bf16[4,4,256,64]{2,3,1,0:T(8,128)(2,1)S(1)}, u32[]{:S(2)}) copy-start(bf16[4,4,256,64]{2,3,1,0:T(8,128)(2,1)S(1)} %get-tuple-element.569) | copy-start | bytes 1572868
  177.6 4.1 copy-start.9
  177.6 182.1 %all-gather.9.cloned.1.call-start = ((), (), s32[]{:S(2)}) async-start(), calls=%async_computation.10 | async-start | bytes 24510464 | tf_op jit(solution)/shard_map/all_gather | solution.py:98
  181.7 278.2 %all-gather.11.cloned.1.call-start = ((), (), s32[]{:S(2)}) async-start(), calls=%async_computation.11 | async-start | bytes 12255232 | tf_op jit(solution)/shard_map/all_gather | solution.py:99
  182.7 363.4 %all-reduce.14.cloned.1.call-start = ((), (), s32[]{:S(2)}) async-start(), calls=%async_computation.12 | async-start | bytes 4194304 | tf_op jit(solution)/shard_map/psum | solution.py:189
  359.7 24.3 %copy-start.22 = (f32[1,2048]{1,0:T(1,128)S(1)}, f32[1,2048]{1,0:T(1,128)}, u32[]{:S(2)}) copy-start(f32[1,2048]{1,0:T(1,128)} %get-tuple-element.325) | copy-start | bytes 24580
  484.8 185.0 %all-reduce.16.cloned.1.call-start = ((), (), s32[]{:S(2)}) async-start(), calls=%async_computation.20 | async-start | bytes 4194304 | tf_op jit(solution)/shard_map/psum | solution.py:173
  546.1 2.7 copy-start.7
  546.1 2.7 copy-start.15
  548.7 2.9 copy-start.39
  555.8 39.2 %copy-start.25 = (f32[256,8]{0,1:T(8,128)S(1)}, f32[256,8]{0,1:T(8,128)}, u32[]{:S(2)}) copy-start(f32[256,8]{0,1:T(8,128)} %get-tuple-element.330) | copy-start | bytes 24580
  555.8 39.2 %copy-start.26 = (f32[256,8]{0,1:T(8,128)S(1)}, f32[256,8]{0,1:T(8,128)}, u32[]{:S(2)}) copy-start(f32[256,8]{0,1:T(8,128)} %get-tuple-element.331) | copy-start | bytes 24580
  559.4 3.9 copy-start.12
  568.9 3.9 copy-start.12
  578.3 3.9 copy-start.12
  587.8 3.9 copy-start.12
  606.5 63.3 %copy-start.24 = (f32[1,2048]{1,0:T(1,128)S(1)}, f32[1,2048]{1,0:T(1,128)}, u32[]{:S(2)}) copy-start(f32[1,2048]{1,0:T(1,128)} %copy-done.23) | copy-start | bytes 24580
  606.5 63.3 %copy-start.30 = (f32[256]{0:T(256)S(1)}, f32[256]{0:T(256)}, u32[]{:S(2)}) copy-start(f32[256]{0:T(256)} %copy-done.29) | copy-start | bytes 3076
  606.5 127.4 %reduce-scatter.22.cloned.1.call-start = ((), (), s32[]{:S(2)}) async-start(), calls=%async_computation.18 | async-start | bytes 1671168
  608.2 186.3 %reduce-scatter.24.cloned.1.call-start = ((), (), s32[]{:S(2)}) async-start(), calls=%async_computation.19 | async-start | bytes 1114112
  673.4 229.5 %reduce-scatter.14.cloned.1.call-start = ((), (), s32[]{:S(2)}) async-start(), calls=%async_computation.14 | async-start | bytes 8912896 | tf_op jit(solution)/shard_map/reduce_scatter | solution.py:259
  680.1 454.2 %reduce-scatter.18.cloned.1.call-start = ((), (), s32[]{:S(2)}) async-start(), calls=%async_computation.16 | async-start | bytes 24510464 | tf_op jit(solution)/shard_map/reduce_scatter | solution.py:261
  691.5 673.3 %reduce-scatter.16.cloned.1.call-start = ((), (), s32[]{:S(2)}) async-start(), calls=%async_computation.15 | async-start | bytes 24510464 | tf_op jit(solution)/shard_map/reduce_scatter | solution.py:260
  702.7 892.7 %reduce-scatter.20.cloned.1.call-start = ((), (), s32[]{:S(2)}) async-start(), calls=%async_computation.17 | async-start | bytes 24510464 | tf_op jit(solution)/shard_map/reduce_scatter | solution.py:262
  715.4 1127.5 %reduce-scatter.12.cloned.1.call-start = ((), (), s32[]{:S(2)}) async-start(), calls=%async_computation.13 | async-start | bytes 26738688 | tf_op jit(solution)/shard_map/reduce_scatter | solution.py:257
  727.9 7.0 copy-start.36
  727.9 7.0 copy-start.37
  727.9 7.0 copy-start.38
  735.5 3.1 copy-start.2
  735.5 3.1 copy-start.16
  738.6 56.8 %copy-start.32 = (f32[4,128]{1,0:T(4,128)S(1)}, f32[4,128]{1,0:T(4,128)}, u32[]{:S(2)}) copy-start(f32[4,128]{1,0:T(4,128)} %param.33) | copy-start | bytes 6148
  738.6 56.8 %copy-start.33 = (f32[4,128]{1,0:T(4,128)S(1)}, f32[4,128]{1,0:T(4,128)}, u32[]{:S(2)}) copy-start(f32[4,128]{1,0:T(4,128)} %param.44) | copy-start | bytes 6148
  738.6 56.8 %copy-start.34 = (f32[4,128]{1,0:T(4,128)S(1)}, f32[4,128]{1,0:T(4,128)}, u32[]{:S(2)}) copy-start(f32[4,128]{1,0:T(4,128)} %param.45) | copy-start | bytes 6148
  740.8 624.0 %copy-start.6 = (f32[128,2,2816]{2,1,0:T(2,128)S(1)}, f32[128,2,2816]{2,1,0:T(2,128)}, u32[]{:S(2)}) copy-start(f32[128,2,2816]{2,1,0:T(2,128)} %param.31) | copy-start | bytes 8650756
  1377.6 217.8 %copy-start.10 = (f32[2816,128]{1,0:T(8,128)S(1)}, f32[2816,128]{1,0:T(8,128)}, u32[]{:S(2)}) copy-start(f32[2816,128]{1,0:T(8,128)} %param.32) | copy-start | bytes 4325380
  1381.5 461.4 %copy-start.8 = (f32[128,3,1024]{2,0,1:T(8,128)S(1)}, f32[128,3,1024]{2,0,1:T(8,128)}, u32[]{:S(2)}) copy-start(f32[128,3,1024]{2,0,1:T(8,128)} %param.28) | copy-start | bytes 4718596
  (19 other events, 21.0 us)
Sparse Core Ops, SparseCore 0:
  10.8 108.5 all-gather.4
  122.0 50.5 all-gather.6
  177.7 61.0 all-reduce.11
  240.9 118.7 all-gather.8
  362.5 97.3 all-gather.10
  484.9 61.1 all-reduce.13
  606.6 63.0 all-reduce.15
  674.4 59.4 reduce-scatter.21
  738.1 56.3 reduce-scatter.23
  799.0 103.9 reduce-scatter.13
  907.6 226.5 reduce-scatter.17
  1138.8 225.9 reduce-scatter.15
  1369.4 225.9 reduce-scatter.19
  1599.9 242.9 reduce-scatter.11
where the time goes:
time: 1860 us
  waiting for transfers between devices  1510 us (81%)
  matrix products  159 us (9%)
  local copies, waits for them, and re-layouts  68.1 us (4%)
  blocking collectives  53.8 us (3%)
  other arithmetic  47.9 us (3%)
    reduce_scatter x1, waiting for transfers between devices, per_device(): lax.psum_scatter(grad_qkv, 'dp', scatter_dimension=0, tiled=True)  243 us
    reduce_scatter x1, waiting for transfers between devices, per_device(): lax.psum_scatter(grad_gating_gate, 'dp', scatter_dimension=0, tiled=True)  231 us
    reduce_scatter x1, waiting for transfers between devices, per_device(): lax.psum_scatter(grad_gating_up, 'dp', scatter_dimension=0, tiled=True)  228 us
    reduce_scatter x1, waiting for transfers between devices, per_device(): lax.psum_scatter(grad_down, 'dp', scatter_dimension=1, tiled=True)  214 us
    all_gather x1, waiting for transfers between devices, per_device(): lax.all_gather(gating_weight.astype(jnp.bfloat16), 'dp', axis=0, tiled=True)  119 us
    reduce_scatter x1, waiting for transfers between devices, per_device(): lax.psum_scatter(grad_out, 'dp', scatter_dimension=1, tiled=True)  107 us
    all_gather x1, waiting for transfers between devices, per_device(): lax.all_gather(down_weight.astype(jnp.bfloat16), 'dp', axis=1, tiled=True)  62.5 us
    psum x1, waiting for transfers between devices, per_device(): lax.psum(jnp.dot(hidden, down_full, preferred_element_type=jnp.float32).a...  61.5 us
  transfers between devices with their start and end apart: 14, of which 14 were waited for; matrix products, arithmetic and copies ran while one was open for 9% of the time, Pallas kernels for 0%

commit v1 on v0

v1 whole, which is shorter than its diff:
```python
import functools

import jax
import jax.numpy as jnp
from jax import lax
from jax.experimental import pallas as pl
from jax.experimental.pallas import tpu as pltpu
from jax.sharding import PartitionSpec as P

D = 2048
H = 32
HD = 64
ROT = 16
FF = 5632
STEP = 10
TP = 4

F32 = jnp.float32
BF16 = jnp.bfloat16


def layer_norm(values, scale_row, shift_row):
    centre = values - jnp.mean(values, axis=-1, keepdims=True)
    spread = jnp.mean(centre * centre, axis=-1, keepdims=True)
    inverse = lax.rsqrt(spread + 1e-05)
    scaled = centre * inverse
    return (scaled * scale_row + shift_row, scaled, inverse)


def norm_back(grad_in, scaled, inverse, scale_row):
    grad_scaled = grad_in * scale_row
    mean_first = jnp.mean(grad_scaled, axis=-1, keepdims=True)
    mean_second = jnp.mean(grad_scaled * scaled, axis=-1, keepdims=True)
    grad_values = inverse * (grad_scaled - mean_first - scaled * mean_second)
    return (grad_values, jnp.sum(grad_in * scaled, axis=0), jnp.sum(grad_in, axis=0))


def adamw_update(weight_old, gradient, first_old, second_old, step_rate, decay_rate):
    first_new = 0.9 * first_old + 0.1 * gradient
    second_new = 0.95 * second_old + 0.05 * gradient * gradient
    corrected = first_new / (1.0 - 0.9**STEP) / (jnp.sqrt(second_new / (1.0 - 0.95**STEP)) + 1e-08)
    return (weight_old - step_rate * (corrected + decay_rate * weight_old), first_new, second_new)


def dot(a, b, ca, cb):
    return lax.dot_general(a, b, (((ca,), (cb,)), ((), ())), preferred_element_type=F32)


def spin(values, cos_t, lower_t, upper_t):
    wide = values.shape[1]
    return (
        values * cos_t
        + pltpu.roll(values, wide - ROT // 2, 1) * lower_t
        + pltpu.roll(values, ROT // 2, 1) * upper_t
    )


def spin_back(values, cos_t, lower_t, upper_t):
    wide = values.shape[1]
    return (
        values * cos_t
        + pltpu.roll(values * lower_t, ROT // 2, 1)
        + pltpu.roll(values * upper_t, wide - ROT // 2, 1)
    )


def mask_of(seg_col, seg_row, size):
    rows = lax.broadcasted_iota(jnp.int32, (size, size), 0)
    cols = lax.broadcasted_iota(jnp.int32, (size, size), 1)
    return (seg_col == seg_row) & (cols <= rows)


def attend_kernel(proj_ref, bias_ref, cos_ref, low_ref, upp_ref, col_ref, row_ref, qkv_ref, out_ref):
    size, wide = out_ref.shape
    proj = proj_ref[...] + bias_ref[...]
    cos_t, low_t, upp_t = cos_ref[...], low_ref[...], upp_ref[...]
    query = spin(proj[:, :wide], cos_t, low_t, upp_t).astype(BF16)
    key = spin(proj[:, wide : 2 * wide], cos_t, low_t, upp_t).astype(BF16)
    value = proj[:, 2 * wide :].astype(BF16)
    qkv_ref[:, :wide] = query
    qkv_ref[:, wide : 2 * wide] = key
    qkv_ref[:, 2 * wide :] = value
    allowed = mask_of(col_ref[...], row_ref[...], size)
    head_of = lax.broadcasted_iota(jnp.int32, (size, wide), 1) // HD
    total = jnp.zeros((size, wide), F32)
    for head in range(wide // HD):
        mine = head_of == head
        scores = dot(jnp.where(mine, query, jnp.zeros_like(query)), key, 1, 1) * HD ** (-0.5)
        scores = jnp.where(allowed, scores, -1e30)
        weights = jnp.exp(scores - jnp.max(scores, axis=1, keepdims=True))
        prob = weights / jnp.sum(weights, axis=1, keepdims=True)
        total = jnp.where(mine, dot(prob.astype(BF16), value, 1, 0), total)
    out_ref[...] = total.astype(BF16)


def attend_back_kernel(qkv_ref, do_ref, cos_ref, low_ref, upp_ref, col_ref, row_ref, dp_ref, sum_ref):
    size, wide = do_ref.shape
    query, key, value = qkv_ref[:, :wide], qkv_ref[:, wide : 2 * wide], qkv_ref[:, 2 * wide :]
    grad = do_ref[...]
    allowed = mask_of(col_ref[...], row_ref[...], size)
    head_of = lax.broadcasted_iota(jnp.int32, (size, wide), 1) // HD
    zero = jnp.zeros_like(query)
    dq = jnp.zeros((size, wide), F32)
    dk = jnp.zeros((size, wide), F32)
    dv = jnp.zeros((size, wide), F32)
    for head in range(wide // HD):
        mine = head_of == head
        query_h = jnp.where(mine, query, zero)
        grad_h = jnp.where(mine, grad, zero)
        scores = dot(query_h, key, 1, 1) * HD ** (-0.5)
        scores = jnp.where(allowed, scores, -1e30)
        weights = jnp.exp(scores - jnp.max(scores, axis=1, keepdims=True))
        prob = weights / jnp.sum(weights, axis=1, keepdims=True)
        dv = dv + dot(prob.astype(BF16), grad_h, 0, 0)
        dprob = dot(grad_h, value, 1, 1)
        delta = jnp.sum(prob * dprob, axis=1, keepdims=True)
        dscore = (prob * (dprob - delta)).astype(BF16)
        dq = jnp.where(mine, dot(dscore, key, 1, 0), dq)
        dk = dk + dot(dscore, query_h, 0, 0)
    cos_t, low_t, upp_t = cos_ref[...], low_ref[...], upp_ref[...]
    dq = spin_back(dq * HD ** (-0.5), cos_t, low_t, upp_t).astype(BF16)
    dk = spin_back(dk * HD ** (-0.5), cos_t, low_t, upp_t).astype(BF16)
    dv = dv.astype(BF16)
    dp_ref[:, :wide] = dq
    dp_ref[:, wide : 2 * wide] = dk
    dp_ref[:, 2 * wide :] = dv
    for part, grad_p in enumerate((dq, dk, dv)):
        sum_ref[0, :, part * wide : (part + 1) * wide] = jnp.sum(
            grad_p.astype(F32), axis=0, keepdims=True
        )


def row_blocks(size, wide):
    return pl.BlockSpec((size, wide), lambda i: (i, 0))


def attend(proj, bias, tables, seg_col, seg_row, seqs, size, wide):
    return pl.pallas_call(
        attend_kernel,
        grid=(seqs,),
        in_specs=[
            row_blocks(size, 3 * wide),
            pl.BlockSpec((1, 3 * wide), lambda i: (0, 0)),
            row_blocks(size, wide),
            row_blocks(size, wide),
            row_blocks(size, wide),
            row_blocks(size, 1),
            pl.BlockSpec((None, 1, size), lambda i: (i, 0, 0)),
        ],
        out_specs=[row_blocks(size, 3 * wide), row_blocks(size, wide)],
        out_shape=[
            jax.ShapeDtypeStruct((seqs * size, 3 * wide), BF16),
            jax.ShapeDtypeStruct((seqs * size, wide), BF16),
        ],
        cost_estimate=pl.CostEstimate(
            flops=seqs * 8 * size * size * wide, bytes_accessed=seqs * size * wide * 32, transcendentals=seqs * size * size * 4
        ),
        name="attend",
    )(proj, bias, *tables, seg_col, seg_row)


def attend_back(qkv, grad, tables, seg_col, seg_row, seqs, size, wide):
    return pl.pallas_call(
        attend_back_kernel,
        grid=(seqs,),
        in_specs=[
            row_blocks(size, 3 * wide),
            row_blocks(size, wide),
            row_blocks(size, wide),
            row_blocks(size, wide),
            row_blocks(size, wide),
            row_blocks(size, 1),
            pl.BlockSpec((None, 1, size), lambda i: (i, 0, 0)),
        ],
        out_specs=[
            row_blocks(size, 3 * wide),
            pl.BlockSpec((1, 1, 3 * wide), lambda i: (i, 0, 0)),
        ],
        out_shape=[
            jax.ShapeDtypeStruct((seqs * size, 3 * wide), BF16),
            jax.ShapeDtypeStruct((seqs, 1, 3 * wide), F32),
        ],
        cost_estimate=pl.CostEstimate(
            flops=seqs * 20 * size * size * wide, bytes_accessed=seqs * size * wide * 32, transcendentals=seqs * size * size * 4
        ),
        name="attend_back",
    )(qkv, grad, *tables, seg_col, seg_row)


class Links:
    def __init__(self, count):
        self.count = count
        self.lines = count // TP
        self.place = lax.axis_index("dp")
        self.tensor = lax.axis_index("tensor")
        self.u = self.place // TP
        self.j = self.place % TP
        self.x = self.j // 2
        self.c = self.j % 2

    def flip(self, values, bit):
        return lax.ppermute(values, "dp", [(i, i ^ bit) for i in range(self.count)])

    def swap(self, values):
        return lax.ppermute(values, "tensor", [(0, 1), (1, 0)])

    def along(self, values, pairs):
        return lax.ppermute(
            values, "dp", [(a * TP + r, b * TP + r) for a, b in pairs for r in range(TP)]
        )

    def pair(self, mine, other, second):
        return jnp.stack([jnp.where(second, other, mine), jnp.where(second, mine, other)])

    def group_gather(self, values):
        two = self.pair(values, self.flip(values, 1), self.c == 1)
        four = self.pair(two, self.flip(two, 2), self.x == 1)
        return four.reshape((TP,) + values.shape)

    def group_swap(self, blocks):
        def block(k):
            return lax.dynamic_index_in_dim(blocks, self.j ^ k, 0, False)

        got = [block(0)] + [self.flip(block(k), k) for k in range(1, TP)]
        odd = self.c == 1
        got = [jnp.where(odd, got[k ^ 1], got[k]) for k in range(TP)]
        odd = self.x == 1
        return jnp.stack([jnp.where(odd, got[k ^ 2], got[k]) for k in range(TP)])

    def line_pieces(self, values):
        n = self.lines
        if n != 4:
            return [
                self.along(values, [(i, (i + k) % n) for i in range(n)]) for k in range(1, n)
            ]
        up = self.along(values, [(0, 1), (1, 2), (2, 3)])
        down = self.along(values, [(3, 2), (2, 1), (1, 0)])
        two = self.along(values, [(0, 2), (1, 3), (2, 0), (3, 1)])
        far = self.along(two, [(2, 3), (1, 0)])
        return [jnp.where(self.u == 0, far, up), two, jnp.where(self.u == 3, far, down)]

    def line_gather(self, values):
        out = jnp.zeros((self.lines,) + values.shape, values.dtype)
        for k, piece in enumerate([values] + self.line_pieces(values)):
            out = lax.dynamic_update_index_in_dim(out, piece, (self.u - k) % self.lines, 0)
        return out

    def line_scatter_sum(self, blocks):
        n = self.lines

        def block(k):
            return lax.dynamic_index_in_dim(blocks, (self.u + k) % n, 0, False)

        total = block(0).astype(F32)
        if n != 4:
            for k in range(1, n):
                total = total + self.along(
                    block(k), [(i, (i + k) % n) for i in range(n)]
                ).astype(F32)
            return total
        outer = jnp.where(self.u == 0, blocks[3], blocks[0])
        far = self.along(outer, [(0, 1), (3, 2)])
        up = self.along(block(1), [(0, 1), (1, 2), (2, 3)])
        down = self.along(block(3), [(3, 2), (2, 1), (1, 0)])
        two = (block(2).astype(F32) + far.astype(F32)).astype(BF16)
        two = self.along(two, [(0, 2), (1, 3), (2, 0), (3, 1)])
        return total + up.astype(F32) + down.astype(F32) + two.astype(F32)

    def line_sum(self, values):
        n = self.lines
        total = values
        for k in range(1, n):
            total = total + self.along(values, [(i, (i + k) % n) for i in range(n)])
        return total

    def scatter_sum(self, partial):
        half = partial.shape[-1] // 2

        def take(values, axis, index):
            return lax.dynamic_index_in_dim(values, index, axis, False)

        other = self.flip(take(partial, 1, 1 - self.c).astype(BF16), 1)
        here = take(partial, 1, self.c) + other.astype(F32)
        left, right = here[..., :half], here[..., half:]
        left = take(left, 0, self.x) + self.flip(take(left, 0, 1 - self.x).astype(BF16), 2).astype(F32)
        right = take(right, 1, self.tensor) + self.swap(
            take(right, 1, 1 - self.tensor).astype(BF16)
        ).astype(F32)
        left = take(left, 0, self.tensor) + self.swap(
            take(left, 0, 1 - self.tensor).astype(BF16)
        ).astype(F32)
        right = take(right, 0, self.x) + self.flip(take(right, 0, 1 - self.x).astype(BF16), 2).astype(F32)
        return jnp.concatenate([left, right], axis=-1)

    def gather(self, values):
        half = values.shape[-1] // 2
        left, right = values[:, :half], values[:, half:]
        left = self.pair(left, self.swap(left), self.tensor == 1)
        left = self.pair(left, self.flip(left, 2), self.x == 1)
        right = self.pair(right, self.flip(right, 2), self.x == 1)
        right_other = self.swap(right)
        second = self.tensor == 1
        right = jnp.stack(
            [jnp.where(second, right_other, right), jnp.where(second, right, right_other)], axis=1
        )
        here = jnp.concatenate([left, right], axis=-1)
        there = self.flip(here, 1)
        second = self.c == 1
        return jnp.stack([jnp.where(second, there, here), jnp.where(second, here, there)], axis=1)


def per_device(
    count,
    tokens_in,
    segment_ids,
    d_out,
    qkv_weight,
    qkv_bias,
    out_weight,
    gating_weight,
    down_weight,
    norm_params,
    qkv_first,
    qkv_second,
    bias_first,
    bias_second,
    out_first,
    out_second,
    gating_first,
    gating_second,
    down_first,
    down_second,
    norm_first,
    norm_second,
):
    links = Links(count)
    rows = norm_params.shape[1]
    seq_len = tokens_in.shape[1]
    head_local = qkv_weight.shape[2]
    hidden_local = gating_weight.shape[2]
    wide = head_local // TP
    hid = hidden_local // TP
    half_seq = seq_len // 2
    group_rows = TP * seq_len

    small = jnp.concatenate(
        [norm_params.astype(BF16).reshape(-1), qkv_bias.astype(BF16).reshape(-1)]
    )
    small = links.line_gather(links.group_gather(small)).reshape(count, -1)
    norm_rows = small[:, : 4 * rows].reshape(count, 4, rows).transpose(1, 0, 2).reshape(4, D).astype(F32)
    bias_full = small[:, 4 * rows :].reshape(3, TP, wide)
    bias_row = lax.dynamic_index_in_dim(bias_full, links.j, 1, False).reshape(1, 3 * wide).astype(F32)

    tokens = links.group_gather(tokens_in[0])
    segments = links.group_gather(segment_ids[0])

    def weight_chunk(shard):
        blocks = shard.astype(BF16).transpose(1, 0, 2)
        return links.group_swap(blocks).reshape(TP * shard.shape[0], shard.shape[2])

    qkv_blocks = qkv_weight.reshape(rows, 3, TP, wide).transpose(0, 2, 1, 3).reshape(rows, TP, 3 * wide)
    out_blocks = out_weight.T.reshape(rows, TP, wide)
    gating_blocks = gating_weight.reshape(rows, 2, TP, hid).transpose(0, 2, 1, 3).reshape(rows, TP, 2 * hid)
    down_blocks = down_weight.T.reshape(rows, TP, hid)
    qkv_matrix = links.line_gather(weight_chunk(qkv_blocks)).reshape(D, 3 * wide)
    out_matrix = links.line_gather(weight_chunk(out_blocks)).reshape(D, wide)
    gating_matrix = links.line_gather(weight_chunk(gating_blocks)).reshape(D, 2 * hid)
    down_matrix = links.line_gather(weight_chunk(down_blocks)).reshape(D, hid)
    cotangent = links.group_gather(d_out[0]).reshape(group_rows, D)

    def own_half(values):
        return lax.dynamic_slice_in_dim(values, links.tensor * half_seq, half_seq, 0)

    earlier = jnp.sum((segments[:, None, :] < segments[:, :, None]).astype(jnp.int32), axis=2)
    positions = (jnp.arange(seq_len, dtype=jnp.int32)[None] - earlier).astype(F32)
    frequency = 10000.0 ** (-2.0 * jnp.arange(ROT // 2, dtype=F32) / ROT)
    angles = positions.reshape(group_rows, 1) * frequency[None, :]
    cosine, sine_part = jnp.cos(angles), jnp.sin(angles)
    zeros = jnp.zeros((group_rows, HD - ROT), F32)
    heads = wide // HD
    tables = (
        jnp.tile(jnp.concatenate([cosine, cosine, zeros + 1.0], axis=1), (1, heads)),
        jnp.tile(jnp.concatenate([-sine_part, jnp.zeros_like(sine_part), zeros], axis=1), (1, heads)),
        jnp.tile(jnp.concatenate([jnp.zeros_like(sine_part), sine_part, zeros], axis=1), (1, heads)),
    )
    seg_col = segments.reshape(group_rows, 1)
    seg_row = segments.reshape(TP, 1, seq_len)

    normed_one, _, _ = layer_norm(tokens.reshape(group_rows, D).astype(F32), norm_rows[0], norm_rows[1])
    normed_one = normed_one.astype(BF16)
    projected = dot(normed_one, qkv_matrix, 1, 0)
    qkv_rot, attended = attend(projected, bias_row, tables, seg_col, seg_row, TP, seq_len, wide)

    def to_parts(partial):
        return partial.reshape(2, 2, 2, half_seq, D)

    attention_term = links.scatter_sum(to_parts(dot(attended, out_matrix, 1, 1)))
    tokens_own = own_half(tokens_in[0]).astype(F32)
    residual = tokens_own + attention_term
    normed_two, scaled_two, inverse_two = layer_norm(residual, norm_rows[2], norm_rows[3])
    normed_two = links.gather(normed_two.astype(BF16)).reshape(group_rows, D)

    gated_out = dot(normed_two, gating_matrix, 1, 0)
    gate_part, up_part = gated_out[:, :hid], gated_out[:, hid:]
    sigmoid_gate = jax.nn.sigmoid(gate_part)
    hidden = (gate_part * sigmoid_gate * up_part).astype(BF16)
    grad_down = dot(cotangent, hidden, 0, 0).astype(BF16)
    down_sum = links.line_scatter_sum(grad_down.reshape(links.lines, TP * rows, hid))
    grad_hidden = dot(cotangent, down_matrix, 1, 0)
    grad_gate = (
        grad_hidden * up_part * sigmoid_gate * (1.0 + gate_part * (1.0 - sigmoid_gate))
    ).astype(BF16)
    grad_up = (grad_hidden * (gate_part * sigmoid_gate)).astype(BF16)
    grad_gated = jnp.concatenate([grad_gate, grad_up], axis=1)
    normed_grad_two = links.scatter_sum(to_parts(dot(grad_gated, gating_matrix, 1, 1)))
    grad_gating = dot(normed_two, grad_gated, 0, 0).astype(BF16)
    gating_sum = links.line_scatter_sum(grad_gating.reshape(links.lines, TP * rows, 2 * hid))

    residual_part, gain_two, shift_two = norm_back(
        normed_grad_two, scaled_two, inverse_two, norm_rows[2]
    )
    residual_grad = own_half(d_out[0]).astype(F32) + residual_part
    residual_low = links.gather(residual_grad.astype(BF16)).reshape(group_rows, D)
    grad_attended = dot(residual_low, out_matrix, 1, 0).astype(BF16)
    grad_out = dot(residual_low, attended, 0, 0).astype(BF16)
    out_sum = links.line_scatter_sum(grad_out.reshape(links.lines, TP * rows, wide))

    feedforward_term = links.scatter_sum(to_parts(dot(hidden, down_matrix, 1, 1)))
    block_own = residual + feedforward_term
    block_out = links.pair(block_own, links.swap(block_own), links.tensor == 1).reshape(seq_len, D)

    grad_projected, bias_sums = attend_back(
        qkv_rot, grad_attended, tables, seg_col, seg_row, TP, seq_len, wide
    )
    grad_qkv = dot(normed_one, grad_projected, 0, 0).astype(BF16)
    qkv_sum = links.line_scatter_sum(grad_qkv.reshape(links.lines, TP * rows, 3 * wide))
    normed_grad_one = links.scatter_sum(to_parts(dot(grad_projected, qkv_matrix, 1, 1)))
    _, scaled_one, inverse_one = layer_norm(tokens_own, norm_rows[0], norm_rows[1])
    input_part, gain_one, shift_one = norm_back(
        normed_grad_one, scaled_one, inverse_one, norm_rows[0]
    )
    input_own = residual_grad + input_part
    input_grad = links.pair(input_own, links.swap(input_own), links.tensor == 1).reshape(seq_len, D)

    norm_small = jnp.concatenate([gain_one, shift_one, gain_two, shift_two])
    norm_small = norm_small + links.swap(norm_small)
    bias_small = jnp.sum(bias_sums, axis=0).reshape(3, 1, wide)
    bias_small = jnp.where(
        lax.broadcasted_iota(jnp.int32, (3, TP, wide), 1) == links.j, bias_small, 0.0
    ).reshape(-1)
    small_grad = jnp.concatenate([norm_small, bias_small])
    small_grad = small_grad + links.flip(small_grad, 1)
    small_grad = small_grad + links.flip(small_grad, 2)
    small_grad = links.line_sum(small_grad)
    norm_grad = lax.dynamic_slice_in_dim(small_grad[: 4 * D].reshape(4, D), links.place * rows, rows, 1)
    bias_here = qkv_bias.shape[1]
    bias_grad = lax.dynamic_slice_in_dim(
        small_grad[4 * D :].reshape(1, -1), links.place * bias_here, bias_here, 1
    )

    def to_owner(total):
        blocks = total.astype(BF16).reshape(TP, rows, total.shape[1])
        return links.group_swap(blocks).transpose(1, 0, 2).astype(F32)

    down_shard = to_owner(down_sum).reshape(rows, hidden_local).T
    gating_shard = (
        to_owner(gating_sum).reshape(rows, TP, 2, hid).transpose(0, 2, 1, 3).reshape(gating_weight.shape)
    )
    out_shard = to_owner(out_sum).reshape(rows, head_local).T
    qkv_shard = (
        to_owner(qkv_sum).reshape(rows, TP, 3, wide).transpose(0, 2, 1, 3).reshape(qkv_weight.shape)
    )
    return (
        block_out[None],
        input_grad[None],
        *adamw_update(qkv_weight, qkv_shard, qkv_first, qkv_second, D ** (-0.5), 0.1),
        *adamw_update(qkv_bias, bias_grad, bias_first, bias_second, 0.3, 0.0),
        *adamw_update(out_weight, out_shard, out_first, out_second, (H * HD // 16) ** (-0.5), 0.1),
        *adamw_update(gating_weight, gating_shard, gating_first, gating_second, D ** (-0.5), 0.1),
        *adamw_update(down_weight, down_shard, down_first, down_second, FF ** (-0.5), 0.1),
        *adamw_update(norm_params, norm_grad, norm_first, norm_second, 0.25, 0.0),
    )


def solution(mesh):
    tokens = P("dp", None, None)
    qkv = P("dp", None, "tensor")
    rest = P("tensor", "dp")
    norm = P(None, "dp")
    weights = (qkv, rest, rest, qkv, rest, norm)
    states = (qkv, qkv, rest, rest, rest, rest, qkv, qkv, rest, rest, norm, norm)
    return jax.shard_map(
        functools.partial(per_device, mesh.shape["dp"]),
        mesh=mesh,
        in_specs=(tokens, P("dp", None), tokens, *weights, *states),
        out_specs=(tokens, tokens, *(spec for spec in weights for _ in range(3))),
        check_vma=False,
    )
```

time: 1860 us -> 965 us (0.52)
  waiting for transfers between devices: 1510 us -> 413 us
  local copies, waits for them, and re-layouts: 68.1 us -> 222 us
  starting transfers between devices: 1.43 us -> 136 us
  matrix products: 159 us -> 60.1 us
  blocking collectives: 53.8 us -> 0 us
  other arithmetic: 47.9 us -> 95.8 us
  Pallas kernels: 0 us -> 19.2 us
    reduce_scatter x5 -> x0, waiting for transfers between devices: 1020 us -> none  [the longest x1 243 us: per_device(): lax.psum_scatter(grad_qkv, 'dp', scatter_dimension=0, tiled=True)]
    ppermute x0 -> x106, waiting for transfers between devices: none -> 413 us  [the longest x39 293 us: along(): lax.ppermute(values, 'dp', [(a * TP + r, b * TP + r) for a, b in pairs fo...]
    all_gather x4 -> x0, waiting for transfers between devices: 258 us -> none  [the longest x1 119 us: per_device(): lax.all_gather(gating_weight.astype(jnp.bfloat16), 'dp', axis=0, tiled=True)]
    psum x3 -> x0, waiting for transfers between devices: 169 us -> none  [the longest x1 61.5 us: per_device(): lax.psum(jnp.dot(hidden, down_full, preferred_element_type=jnp.float32).a...]
    ppermute x0 -> x106, starting transfers between devices: none -> 136 us  [the longest x39 85.7 us: along(): lax.ppermute(values, 'dp', [(a * TP + r, b * TP + r) for a, b in pairs fo...]
    dot_general x41 -> x12, matrix products: 159 us -> 60.1 us  [dot(): lax.dot_general(a, b, (((ca,), (cb,)), ((), ())), preferred_element_type=...]
    dynamic_update_slice x0 -> x13, local copies, waits for them, and re-layouts: none -> 86.1 us  [line_gather(): lax.dynamic_update_index_in_dim(out, piece, (self.u - k) % self.lines, 0)]
    unnamed x16 -> x0, waiting for transfers between devices: 60 us -> none
  transfers between devices with their start and end apart: 14 -> 106, of which waited for: 14 -> 54; matrix products, arithmetic and copies ran while one was open for 9% -> 33% of each run, Pallas kernels for 0% -> 2%
where the time goes in v1:
time: 965 us; the launch traced here: 951 us
  waiting for transfers between devices  413 us (43%)
  local copies, waits for them, and re-layouts  222 us (23%)
  starting transfers between devices  136 us (14%)
  other arithmetic  95.8 us (10%)
  matrix products  60.1 us (6%)
  Pallas kernels  19.2 us (2%)
    ppermute x39, waiting for transfers between devices, along(): lax.ppermute(values, 'dp', [(a * TP + r, b * TP + r) for a, b in pairs fo...  293 us
    dynamic_update_slice x13, local copies, waits for them, and re-layouts, line_gather(): lax.dynamic_update_index_in_dim(out, piece, (self.u - k) % self.lines, 0)  86.1 us
    ppermute x39, starting transfers between devices, along(): lax.ppermute(values, 'dp', [(a * TP + r, b * TP + r) for a, b in pairs fo...  85.7 us
    ppermute x15, waiting for transfers between devices, swap(): return lax.ppermute(values, 'tensor', [(0, 1), (1, 0)])  64.8 us
    dot_general x12, matrix products, dot(): lax.dot_general(a, b, (((ca,), (cb,)), ((), ())), preferred_element_type=...  60.1 us
    unnamed x220, local copies, waits for them, and re-layouts  58.3 us
    ppermute x52, waiting for transfers between devices, flip(): return lax.ppermute(values, 'dp', [(i, i ^ bit) for i in range(self.count)])  55.2 us
    ppermute x52, starting transfers between devices, flip(): return lax.ppermute(values, 'dp', [(i, i ^ bit) for i in range(self.count)])  32.3 us
  transfers between devices with their start and end apart: 106, of which 54 were waited for; matrix products, arithmetic and copies ran while one was open for 33% of the time, Pallas kernels for 2%

profile of v1, /device:TPU:0, one launch (start us, length us, event | category | flops | bytes accessed | tf_op | source)
XLA Modules:
  0.0 950.5 jit_solution(2833943762177606323)
XLA Ops:
  54.9 5.5 collective-permute-done.9
  66.4 19.7 %collective-permute-done.20 = bf16[512,256]{1,0:T(8,128)(2,1)S(1)} collective-permute-done((bf16[512,256]{1,0:T(8,128)(2,1)S(1)}, bf16[512,256]{1,0:T(8,128)(2,1)S(1)}, u32[]{:S(2)}, u32[]{:S(2)}) %collective-permute-start.20) | collective-permute-done | bytes 262176 | tf_op jit(solution)/shard_map/ppermute | solution.py:208
  88.1 4.6 collective-permute-start.13
  92.7 10.3 %collective-permute-done.11 = bf16[512,768]{1,0:T(8,128)(2,1)S(1)} collective-permute-done((bf16[512,768]{1,0:T(8,128)(2,1)S(1)}, bf16[512,768]{1,0:T(8,128)(2,1)S(1)}, u32[]{:S(2)}, u32[]{:S(2)}) %collective-permute-start.11) | collective-permute-done | bytes 786464 | tf_op jit(solution)/shard_map/ppermute | solution.py:208
  110.0 21.0 %collective-permute-done.23 = bf16[512,256]{1,0:T(8,128)(2,1)S(1)} collective-permute-done((bf16[512,256]{1,0:T(8,128)(2,1)S(1)}, bf16[512,256]{1,0:T(8,128)(2,1)S(1)}, u32[]{:S(2)}, u32[]{:S(2)}) %collective-permute-start.23) | collective-permute-done | bytes 262176 | tf_op jit(solution)/shard_map/ppermute | solution.py:208
  132.9 19.4 %collective-permute-done.14 = bf16[512,768]{1,0:T(8,128)(2,1)S(1)} collective-permute-done((bf16[512,768]{1,0:T(8,128)(2,1)S(1)}, bf16[512,768]{1,0:T(8,128)(2,1)S(1)}, u32[]{:S(2)}, u32[]{:S(2)}) %collective-permute-start.14) | collective-permute-done | bytes 786464 | tf_op jit(solution)/shard_map/ppermute | solution.py:208
  158.3 5.1 fusion.94.proj_ref
  163.4 7.7 attend.1
  192.5 5.6 copy.301
  198.1 6.0 copy.304
  217.8 4.6 collective-permute-start.46
  227.5 21.6 %collective-permute-done.44 = bf16[512,704]{0,1:T(8,128)(2,1)S(1)} collective-permute-done((bf16[512,704]{0,1:T(8,128)(2,1)S(1)}, bf16[512,704]{0,1:T(8,128)(2,1)S(1)}, u32[]{:S(2)}, u32[]{:S(2)}) %collective-permute-start.44) | collective-permute-done | bytes 720928 | tf_op jit(solution)/shard_map/ppermute | solution.py:208
  258.6 8.4 collective-permute-done.27
  269.8 5.3 collective-permute-start.39
  278.4 7.7 collective-permute-done.45
  292.1 26.4 %dynamic_update_slice.82 = bf16[4,512,704]{1,0,2:T(4,128)(2,1)} dynamic-update-slice(bf16[4,512,704]{1,0,2:T(4,128)(2,1)} %copy.275, bf16[1,512,704]{1,0,2:T(2,128)(2,1)} %copy.276, s32[]{:T(128)S(6)} %select_n.876, s32[]{:T(128)} %constant.491.clone.1, s32[]{:T(128)} %constant.491.clone.1) | dynamic-update-slice | bytes 1441796 | tf_op jit(solution)/shard_map/jit(dynamic_update_index_in_dim)/dynamic_update_slice | solution.py:245
  318.5 26.1 %dynamic_update_slice.83 = bf16[4,512,704]{1,0,2:T(4,128)(2,1)} dynamic-update-slice(bf16[4,512,704]{1,0,2:T(4,128)(2,1)} %dynamic_update_slice.82, bf16[1,512,704]{1,0,2:T(2,128)(2,1)S(1)} %copy.277, s32[]{:T(128)S(6)} %select_n.878, s32[]{:T(128)} %constant.491.clone.1, s32[]{:T(128)} %constant.491.clone.1) | dynamic-update-slice | bytes 1441796 | tf_op jit(solution)/shard_map/jit(dynamic_update_index_in_dim)/dynamic_update_slice | solution.py:245
  344.6 26.2 %dynamic_update_slice.84 = bf16[4,512,704]{1,0,2:T(4,128)(2,1)} dynamic-update-slice(bf16[4,512,704]{1,0,2:T(4,128)(2,1)} %dynamic_update_slice.83, bf16[1,512,704]{1,0,2:T(2,128)(2,1)} %copy.278, s32[]{:T(128)S(6)} %select_n.882, s32[]{:T(128)} %constant.491.clone.1, s32[]{:T(128)} %constant.491.clone.1) | dynamic-update-slice | bytes 1441796 | tf_op jit(solution)/shard_map/jit(dynamic_update_index_in_dim)/dynamic_update_slice | solution.py:245
  370.8 6.7 reshape.557
  406.2 50.2 %collective-permute-done.38 = bf16[512,1408]{1,0:T(8,128)(2,1)S(1)} collective-permute-done((bf16[512,1408]{1,0:T(8,128)(2,1)}, bf16[512,1408]{1,0:T(8,128)(2,1)S(1)}, u32[]{:S(2)}, u32[]{:S(2)}) %collective-permute-start.38) | collective-permute-done | bytes 1441824 | tf_op jit(solution)/shard_map/ppermute | solution.py:208
  461.6 8.4 fusion.96
  470.1 7.2 multiply_convert_fusion.1
  483.3 7.3 reshape.526
  493.1 9.5 %convolution_convert_fusion = bf16[2048,1408]{1,0:T(8,128)(2,1)S(1)} fusion(bf16[1024,2048]{1,0:T(8,128)(2,1)} %bitcast.675, bf16[1024,1408]{1,0:T(8,128)(2,1)S(1)} %pad_maximum_fusion.4), kind=kOutput, calls=%fused_computation.8 | convolution fusion | flops 5908463616 | bytes 12845056 | tf_op jit(solution)/shard_map/dot_general | solution.py:46
  502.7 6.7 fusion.97
  518.0 6.0 constant_dynamic-slice_fusion.8
  525.7 5.3 collective-permute-start.99
  539.0 13.1 %collective-permute-done.100 = bf16[512,704]{0,1:T(8,128)(2,1)S(1)} collective-permute-done((bf16[512,704]{0,1:T(8,128)(2,1)S(1)}, bf16[512,704]{0,1:T(8,128)(2,1)S(1)}, u32[]{:S(2)}, u32[]{:S(2)}) %collective-permute-start.100) | collective-permute-done | bytes 720928 | tf_op jit(solution)/shard_map/ppermute | solution.py:208
  552.0 25.1 %collective-permute-done.99 = bf16[512,704]{0,1:T(8,128)(2,1)S(1)} collective-permute-done((bf16[512,704]{0,1:T(8,128)(2,1)S(1)}, bf16[512,704]{0,1:T(8,128)(2,1)S(1)}, u32[]{:S(2)}, u32[]{:S(2)}) %collective-permute-start.99) | collective-permute-done | bytes 720928 | tf_op jit(solution)/shard_map/ppermute | solution.py:208
  577.1 14.9 %collective-permute-done.102 = bf16[512,704]{0,1:T(8,128)(2,1)S(1)} collective-permute-done((bf16[512,704]{0,1:T(8,128)(2,1)S(1)}, bf16[512,704]{0,1:T(8,128)(2,1)S(1)}, u32[]{:S(2)}, u32[]{:S(2)}) %collective-permute-start.102) | collective-permute-done | bytes 720928 | tf_op jit(solution)/shard_map/ppermute | solution.py:208
  619.7 8.5 collective-permute-done.59
  630.0 10.3 %collective-permute-done.51 = bf16[2,128,1024]{2,1,0:T(8,128)(2,1)S(1)} collective-permute-done((bf16[2,128,1024]{2,1,0:T(8,128)(2,1)S(1)}, bf16[2,128,1024]{2,1,0:T(8,128)(2,1)S(1)}, u32[]{:S(2)}, u32[]{:S(2)}) %collective-permute-start.51) | collective-permute-done | bytes 524320 | tf_op jit(solution)/shard_map/ppermute | solution.py:205
  668.4 31.2 %collective-permute-done.95 = bf16[512,1408]{1,0:T(8,128)(2,1)S(1)} collective-permute-done((bf16[512,1408]{1,0:T(8,128)(2,1)S(1)}, bf16[512,1408]{1,0:T(8,128)(2,1)S(1)}, u32[]{:S(2)}, u32[]{:S(2)}) %collective-permute-start.95) | collective-permute-done | bytes 1441824 | tf_op jit(solution)/shard_map/ppermute | solution.py:208
  705.3 11.4 %collective-permute-done.62 = bf16[2,128,1024]{2,1,0:T(8,128)(2,1)S(1)} collective-permute-done((bf16[2,128,1024]{2,1,0:T(8,128)(2,1)S(1)}, bf16[2,128,1024]{2,1,0:T(8,128)(2,1)S(1)}, u32[]{:S(2)}, u32[]{:S(2)}) %collective-permute-start.62) | collective-permute-done | bytes 524320 | tf_op jit(solution)/shard_map/ppermute | solution.py:202
  722.8 7.4 collective-permute-done.97
  739.5 5.0 multiply_subtract_fusion
  744.5 5.6 copy.316
  750.1 5.7 copy.317
  767.5 11.5 %attend_back.1 = (bf16[1024,768]{1,0:T(8,128)(2,1)}, f32[4,1,768]{2,1,0:T(1,128)}) custom-call(bf16[1024,768]{1,0:T(8,128)(2,1)} %get-tuple-element.25.qkv_ref, bf16[1024,256]{1,0:T(8,128)(2,1)} %convolution_convert_fusion.4.do_ref, f32[1024,256]{1,0:T(8,128)} %copy.257.cos_ref, f32[1024,256]{1,0:T(8,128)} %copy.258.low_ref, f32[1024,256]{1,0:T(8,128)} %copy.259.upp_ref, ...), custom_call_target="tpu_custom_call" | custom-call | flops 1342177280 | bytes 8388608 | tf_op jit(solution)/shard_map/attend_back/pallas_call | solution.py:163
  779.0 5.0 fusion.98
  785.7 6.1 collective-permute-start.87
  800.7 4.6 collective-permute-start.85
  808.5 5.2 collective-permute-done.86
  815.0 7.8 collective-permute-done.85
  822.9 5.3 collective-permute-start.72
  845.5 33.6 %collective-permute-done.75 = bf16[512,768]{1,0:T(8,128)(2,1)} collective-permute-done((bf16[512,768]{1,0:T(8,128)(2,1)}, bf16[512,768]{1,0:T(8,128)(2,1)}, u32[]{:S(2)}, u32[]{:S(2)}) %collective-permute-start.75) | collective-permute-done | bytes 786464 | tf_op jit(solution)/shard_map/ppermute | solution.py:208
  891.6 9.3 collective-permute-done.69
  936.6 10.2 %collective-permute-done.71 = f32[128,2048]{1,0:T(8,128)} collective-permute-done((f32[128,2048]{1,0:T(8,128)}, f32[128,2048]{1,0:T(8,128)}, u32[]{:S(2)}, u32[]{:S(2)}) %collective-permute-start.71) | collective-permute-done | bytes 1048608 | tf_op jit(solution)/shard_map/ppermute | solution.py:205
  (661 shorter events, 371.5 us)
Async XLA Ops:
  2.1 23.4 %collective-permute-start.2 = (bf16[704]{0:T(1024)(128)(2,1)S(1)}, bf16[704]{0:T(1024)(128)(2,1)S(1)}, u32[]{:S(2)}, u32[]{:S(2)}) collective-permute-start(bf16[704]{0:T(1024)(128)(2,1)S(1)} %pad_maximum_fusion.26), channel_id=1, source_target_pairs={{0,2},{2,0},{4,6},{6,4},{8,10},{10,8},{12,14},{14,12},{16,18},{18,... | collective-permute-start | bytes 4232 | tf_op jit(solution)/shard_map/ppermute | solution.py:202
  2.6 59.1 %collective-permute-start = (bf16[256,2048]{1,0:T(8,128)(2,1)}, bf16[256,2048]{1,0:T(8,128)(2,1)}, u32[]{:S(2)}, u32[]{:S(2)}) collective-permute-start(bf16[256,2048]{1,0:T(8,128)(2,1)} %bitcast.649), channel_id=1, source_target_pairs={{0,2},{2,0},{4,6},{6,4},{8,10},{10,8},{12,14},{14,12},{16,18},{18,... | collective-permute-start | bytes 3145736 | tf_op jit(solution)/shard_map/ppermute | solution.py:202
  7.5 47.5 %collective-permute-start.8 = (bf16[128,768]{1,0:T(8,128)(2,1)}, bf16[128,768]{1,0:T(8,128)(2,1)}, u32[]{:S(2)}, u32[]{:S(2)}) collective-permute-start(bf16[128,768]{1,0:T(8,128)(2,1)} %bitcast.19), channel_id=1, source_target_pairs={{0,6},{2,4},{4,2},{6,0},{8,14},{10,12},{12,10},{14,8},{16,22},{18,... | collective-permute-start | bytes 589832 | tf_op jit(solution)/shard_map/ppermute | solution.py:202
  12.0 40.9 %collective-permute-start.17 = (bf16[128,256]{1,0:T(8,128)(2,1)}, bf16[128,256]{1,0:T(8,128)(2,1)}, u32[]{:S(2)}, u32[]{:S(2)}) collective-permute-start(bf16[128,256]{1,0:T(8,128)(2,1)} %bitcast.45), channel_id=1, source_target_pairs={{0,6},{2,4},{4,2},{6,0},{8,14},{10,12},{12,10},{14,8},{16,22},{18,... | collective-permute-start | bytes 196616 | tf_op jit(solution)/shard_map/ppermute | solution.py:202
  54.9 31.3 %collective-permute-start.20 = (bf16[512,256]{1,0:T(8,128)(2,1)S(1)}, bf16[512,256]{1,0:T(8,128)(2,1)S(1)}, u32[]{:S(2)}, u32[]{:S(2)}) collective-permute-start(bf16[512,256]{1,0:T(8,128)(2,1)S(1)} %bitcast.701), channel_id=1, source_target_pairs={{0,16},{2,18},{4,20},{6,22},{8,24},{10,26},{12,28},{14,30},{16,0},... | collective-permute-start | bytes 786440 | tf_op jit(solution)/shard_map/ppermute | solution.py:208
  61.6 41.4 %collective-permute-start.11 = (bf16[512,768]{1,0:T(8,128)(2,1)S(1)}, bf16[512,768]{1,0:T(8,128)(2,1)S(1)}, u32[]{:S(2)}, u32[]{:S(2)}) collective-permute-start(bf16[512,768]{1,0:T(8,128)(2,1)S(1)} %bitcast.678), channel_id=1, source_target_pairs={{0,16},{2,18},{4,20},{6,22},{8,24},{10,26},{12,28},{14,30},{16,0},... | collective-permute-start | bytes 2359304 | tf_op jit(solution)/shard_map/ppermute | solution.py:208
  63.2 89.3 %collective-permute-start.1 = (bf16[2,256,2048]{2,1,0:T(8,128)(2,1)S(1)}, bf16[2,256,2048]{2,1,0:T(8,128)(2,1)S(1)}, u32[]{:S(2)}, u32[]{:S(2)}) collective-permute-start(bf16[2,256,2048]{2,1,0:T(8,128)(2,1)S(1)} %pad_maximum_fusion.5), channel_id=1, source_target_pairs={{0,4},{2,6},{4,0},{6,2},{8,12},{10,14},{12,8},{14,10},{16,20},{18,... | collective-permute-start | bytes 6291464 | tf_op jit(solution)/shard_map/ppermute | solution.py:202
  64.5 40.1 %collective-permute-start.22 = (bf16[512,256]{1,0:T(8,128)(2,1)S(1)}, bf16[512,256]{1,0:T(8,128)(2,1)S(1)}, u32[]{:S(2)}, u32[]{:S(2)}) collective-permute-start(bf16[512,256]{1,0:T(8,128)(2,1)S(1)} %bitcast.702), channel_id=1, source_target_pairs={{0,8},{2,10},{4,12},{6,14},{8,16},{10,18},{12,20},{14,22},{16,24},... | collective-permute-start | bytes 786440 | tf_op jit(solution)/shard_map/ppermute | solution.py:208
  88.1 44.5 %collective-permute-start.13 = (bf16[512,768]{1,0:T(8,128)(2,1)S(1)}, bf16[512,768]{1,0:T(8,128)(2,1)S(1)}, u32[]{:S(2)}, u32[]{:S(2)}) collective-permute-start(bf16[512,768]{1,0:T(8,128)(2,1)S(1)} %bitcast.679), channel_id=1, source_target_pairs={{0,8},{2,10},{4,12},{6,14},{8,16},{10,18},{12,20},{14,22},{16,24},... | collective-permute-start | bytes 2359304 | tf_op jit(solution)/shard_map/ppermute | solution.py:208
  103.0 29.6 %collective-permute-start.12 = (bf16[512,768]{1,0:T(8,128)(2,1)S(1)}, bf16[512,768]{1,0:T(8,128)(2,1)S(1)}, u32[]{:S(2)}, u32[]{:S(2)}) collective-permute-start(bf16[512,768]{1,0:T(8,128)(2,1)S(1)} %collective-permute-done.11), channel_id=1, source_target_pairs={{16,24},{18,26},{20,28},{22,30},{8,0},{10,2},{12,4},{14,6},{17,25}... | collective-permute-start | bytes 2359304 | tf_op jit(solution)/shard_map/ppermute | solution.py:208
  104.6 110.7 %collective-permute-start.34 = (bf16[128,1408]{1,0:T(8,128)(2,1)}, bf16[128,1408]{1,0:T(8,128)(2,1)}, u32[]{:S(2)}, u32[]{:S(2)}) collective-permute-start(bf16[128,1408]{1,0:T(8,128)(2,1)} %bitcast.88), channel_id=1, source_target_pairs={{0,6},{2,4},{4,2},{6,0},{8,14},{10,12},{12,10},{14,8},{16,22},{18,... | collective-permute-start | bytes 1081352 | tf_op jit(solution)/shard_map/ppermute | solution.py:202
  178.8 71.4 %collective-permute-start.24 = (bf16[2,2,128,2048]{3,2,1,0:T(8,128)(2,1)}, bf16[2,2,128,2048]{3,2,1,0:T(8,128)(2,1)}, u32[]{:S(2)}, u32[]{:S(2)}) collective-permute-start(bf16[2,2,128,2048]{3,2,1,0:T(8,128)(2,1)} %fusion.13), channel_id=1, source_target_pairs={{0,2},{2,0},{4,6},{6,4},{8,10},{10,8},{12,14},{14,12},{16,18},{18,... | collective-permute-start | bytes 6291464 | tf_op jit(solution)/shard_map/ppermute | solution.py:202
  179.6 25.7 %collective-permute-start.41 = (bf16[128,704]{0,1:T(8,128)(2,1)}, bf16[128,704]{0,1:T(8,128)(2,1)}, u32[]{:S(2)}, u32[]{:S(2)}) collective-permute-start(bf16[128,704]{0,1:T(8,128)(2,1)} %get-tuple-element.243), channel_id=1, source_target_pairs={{0,6},{2,4},{4,2},{6,0},{8,14},{10,12},{12,10},{14,8},{16,22},{18,... | collective-permute-start | bytes 540680 | tf_op jit(solution)/shard_map/ppermute | solution.py:202
  180.9 25.6 %collective-permute-start.42 = (bf16[128,704]{0,1:T(8,128)(2,1)}, bf16[128,704]{0,1:T(8,128)(2,1)}, u32[]{:S(2)}, u32[]{:S(2)}) collective-permute-start(bf16[128,704]{0,1:T(8,128)(2,1)} %get-tuple-element.242), channel_id=1, source_target_pairs={{0,4},{2,6},{4,0},{6,2},{8,12},{10,14},{12,8},{14,10},{16,20},{18,... | collective-permute-start | bytes 540680 | tf_op jit(solution)/shard_map/ppermute | solution.py:202
  181.7 25.0 %collective-permute-start.43 = (bf16[128,704]{0,1:T(8,128)(2,1)}, bf16[128,704]{0,1:T(8,128)(2,1)}, u32[]{:S(2)}, u32[]{:S(2)}) collective-permute-start(bf16[128,704]{0,1:T(8,128)(2,1)} %get-tuple-element.241), channel_id=1, source_target_pairs={{0,2},{2,0},{4,6},{6,4},{8,10},{10,8},{12,14},{14,12},{16,18},{18,... | collective-permute-start | bytes 540680 | tf_op jit(solution)/shard_map/ppermute | solution.py:202
  206.8 47.9 %collective-permute-start.54 = (bf16[256,2048]{1,0:T(8,128)(2,1)}, bf16[256,2048]{1,0:T(8,128)(2,1)}, u32[]{:S(2)}, u32[]{:S(2)}) collective-permute-start(bf16[256,2048]{1,0:T(8,128)(2,1)} %bitcast.692), channel_id=1, source_target_pairs={{0,2},{2,0},{4,6},{6,4},{8,10},{10,8},{12,14},{14,12},{16,18},{18,... | collective-permute-start | bytes 3145736 | tf_op jit(solution)/shard_map/ppermute | solution.py:202
  215.3 33.8 %collective-permute-start.44 = (bf16[512,704]{0,1:T(8,128)(2,1)S(1)}, bf16[512,704]{0,1:T(8,128)(2,1)S(1)}, u32[]{:S(2)}, u32[]{:S(2)}) collective-permute-start(bf16[512,704]{0,1:T(8,128)(2,1)S(1)} %bitcast.705), channel_id=1, source_target_pairs={{0,16},{2,18},{4,20},{6,22},{8,24},{10,26},{12,28},{14,30},{16,0},... | collective-permute-start | bytes 2162696 | tf_op jit(solution)/shard_map/ppermute | solution.py:208
  216.5 59.9 %collective-permute-start.47 = (bf16[512,704]{0,1:T(8,128)(2,1)S(1)}, bf16[512,704]{0,1:T(8,128)(2,1)S(1)}, u32[]{:S(2)}, u32[]{:S(2)}) collective-permute-start(bf16[512,704]{0,1:T(8,128)(2,1)S(1)} %bitcast.706), channel_id=1, source_target_pairs={{24,16},{26,18},{28,20},{30,22},{16,8},{18,10},{20,12},{22,14},{8,... | collective-permute-start | bytes 2162696 | tf_op jit(solution)/shard_map/ppermute | solution.py:208
  217.8 59.4 %collective-permute-start.46 = (bf16[512,704]{0,1:T(8,128)(2,1)S(1)}, bf16[512,704]{0,1:T(8,128)(2,1)S(1)}, u32[]{:S(2)}, u32[]{:S(2)}) collective-permute-start(bf16[512,704]{0,1:T(8,128)(2,1)S(1)} %bitcast.707), channel_id=1, source_target_pairs={{0,8},{2,10},{4,12},{6,14},{8,16},{10,18},{12,20},{14,22},{16,24},... | collective-permute-start | bytes 2162696 | tf_op jit(solution)/shard_map/ppermute | solution.py:208
  249.0 131.3 %collective-permute-start.37 = (bf16[512,1408]{1,0:T(8,128)(2,1)}, bf16[512,1408]{1,0:T(8,128)(2,1)}, u32[]{:S(2)}, u32[]{:S(2)}) collective-permute-start(bf16[512,1408]{1,0:T(8,128)(2,1)} %bitcast.97), channel_id=1, source_target_pairs={{0,16},{2,18},{4,20},{6,22},{8,24},{10,26},{12,28},{14,30},{16,0},... | collective-permute-start | bytes 4325384 | tf_op jit(solution)/shard_map/ppermute | solution.py:208
  269.8 136.4 %collective-permute-start.39 = (bf16[512,1408]{1,0:T(8,128)(2,1)}, bf16[512,1408]{1,0:T(8,128)(2,1)}, u32[]{:S(2)}, u32[]{:S(2)}) collective-permute-start(bf16[512,1408]{1,0:T(8,128)(2,1)} %bitcast.97), channel_id=1, source_target_pairs={{0,8},{2,10},{4,12},{6,14},{8,16},{10,18},{12,20},{14,22},{16,24},... | collective-permute-start | bytes 4325384 | tf_op jit(solution)/shard_map/ppermute | solution.py:208
  276.3 110.4 %collective-permute-start.55 = (bf16[2,256,2048]{2,1,0:T(8,128)(2,1)}, bf16[2,256,2048]{2,1,0:T(8,128)(2,1)}, u32[]{:S(2)}, u32[]{:S(2)}) collective-permute-start(bf16[2,256,2048]{2,1,0:T(8,128)(2,1)} %pad_maximum_fusion.7), channel_id=1, source_target_pairs={{0,4},{2,6},{4,0},{6,2},{8,12},{10,14},{12,8},{14,10},{16,20},{18,... | collective-permute-start | bytes 6291464 | tf_op jit(solution)/shard_map/ppermute | solution.py:202
  277.2 104.6 %collective-permute-start.28 = (bf16[128,1024]{1,0:T(8,128)(2,1)}, bf16[128,1024]{1,0:T(8,128)(2,1)}, u32[]{:S(2)}, u32[]{:S(2)}) collective-permute-start(bf16[128,1024]{1,0:T(8,128)(2,1)} %fusion.59), channel_id=1, source_target_pairs={{0,4},{2,6},{4,0},{6,2},{8,12},{10,14},{12,8},{14,10},{16,20},{18,... | collective-permute-start | bytes 786440 | tf_op jit(solution)/shard_map/ppermute | solution.py:202
  286.1 98.1 %collective-permute-start.26 = (bf16[128,1024]{1,0:T(8,128)(2,1)}, bf16[128,1024]{1,0:T(8,128)(2,1)}, u32[]{:S(2)}, u32[]{:S(2)}) collective-permute-start(bf16[128,1024]{1,0:T(8,128)(2,1)} %fusion.58), channel_id=1, source_target_pairs={{0,1},{1,0},{2,3},{3,2},{4,5},{5,4},{6,7},{7,6},{8,9},{9,8},{10,11... | collective-permute-start | bytes 786440 | tf_op jit(solution)/shard_map/ppermute | solution.py:205
  380.4 78.1 %collective-permute-start.40 = (bf16[512,1408]{1,0:T(8,128)(2,1)}, bf16[512,1408]{1,0:T(8,128)(2,1)S(1)}, u32[]{:S(2)}, u32[]{:S(2)}) collective-permute-start(bf16[512,1408]{1,0:T(8,128)(2,1)} %bitcast.97), channel_id=1, source_target_pairs={{24,16},{26,18},{28,20},{30,22},{16,8},{18,10},{20,12},{22,14},{8,... | collective-permute-start | bytes 4325384 | tf_op jit(solution)/shard_map/ppermute | solution.py:208
  381.8 74.6 %collective-permute-start.38 = (bf16[512,1408]{1,0:T(8,128)(2,1)}, bf16[512,1408]{1,0:T(8,128)(2,1)S(1)}, u32[]{:S(2)}, u32[]{:S(2)}) collective-permute-start(bf16[512,1408]{1,0:T(8,128)(2,1)} %collective-permute-done.37), channel_id=1, source_target_pairs={{16,24},{18,26},{20,28},{22,30},{8,0},{10,2},{12,4},{14,6},{17,25}... | collective-permute-start | bytes 4325384 | tf_op jit(solution)/shard_map/ppermute | solution.py:208
  405.7 53.8 %collective-permute-start.33 = (bf16[2,2,128,2048]{3,2,0,1:T(8,128)(2,1)S(1)}, bf16[2,2,128,2048]{3,2,0,1:T(8,128)(2,1)S(1)}, u32[]{:S(2)}, u32[]{:S(2)}) collective-permute-start(bf16[2,2,128,2048]{3,2,0,1:T(8,128)(2,1)S(1)} %maximum_maximum_fusion), channel_id=1, source_target_pairs={{0,2},{2,0},{4,6},{6,4},{8,10},{10,8},{12,14},{14,12},{16,18},{18,... | collective-permute-start | bytes 6291464 | tf_op jit(solution)/shard_map/ppermute | solution.py:202
  511.0 99.8 %collective-permute-start.56 = (bf16[2,2,128,2048]{3,2,0,1:T(8,128)(2,1)}, bf16[2,2,128,2048]{3,2,0,1:T(8,128)(2,1)}, u32[]{:S(2)}, u32[]{:S(2)}) collective-permute-start(bf16[2,2,128,2048]{3,2,0,1:T(8,128)(2,1)} %fusion.15), channel_id=1, source_target_pairs={{0,2},{2,0},{4,6},{6,4},{8,10},{10,8},{12,14},{14,12},{16,18},{18,... | collective-permute-start | bytes 6291464 | tf_op jit(solution)/shard_map/ppermute | solution.py:202
  515.6 80.0 %collective-permute-start.94 = (bf16[512,1408]{1,0:T(8,128)(2,1)}, bf16[512,1408]{1,0:T(8,128)(2,1)}, u32[]{:S(2)}, u32[]{:S(2)}) collective-permute-start(bf16[512,1408]{1,0:T(8,128)(2,1)} %slice_select_fusion), channel_id=1, source_target_pairs={{0,8},{2,10},{4,12},{6,14},{24,16},{26,18},{28,20},{30,22},{1,9},{... | collective-permute-start | bytes 4325384 | tf_op jit(solution)/shard_map/ppermute | solution.py:208
  524.2 27.8 %collective-permute-start.100 = (bf16[512,704]{0,1:T(8,128)(2,1)S(1)}, bf16[512,704]{0,1:T(8,128)(2,1)S(1)}, u32[]{:S(2)}, u32[]{:S(2)}) collective-permute-start(bf16[512,704]{0,1:T(8,128)(2,1)S(1)} %bitcast.710), channel_id=1, source_target_pairs={{24,16},{26,18},{28,20},{30,22},{16,8},{18,10},{20,12},{22,14},{8,... | collective-permute-start | bytes 2162696 | tf_op jit(solution)/shard_map/ppermute | solution.py:208
  525.7 51.4 %collective-permute-start.99 = (bf16[512,704]{0,1:T(8,128)(2,1)S(1)}, bf16[512,704]{0,1:T(8,128)(2,1)S(1)}, u32[]{:S(2)}, u32[]{:S(2)}) collective-permute-start(bf16[512,704]{0,1:T(8,128)(2,1)S(1)} %bitcast.709), channel_id=1, source_target_pairs={{0,8},{2,10},{4,12},{6,14},{8,16},{10,18},{12,20},{14,22},{16,24},... | collective-permute-start | bytes 2162696 | tf_op jit(solution)/shard_map/ppermute | solution.py:208
  531.3 60.7 %collective-permute-start.102 = (bf16[512,704]{0,1:T(8,128)(2,1)S(1)}, bf16[512,704]{0,1:T(8,128)(2,1)S(1)}, u32[]{:S(2)}, u32[]{:S(2)}) collective-permute-start(bf16[512,704]{0,1:T(8,128)(2,1)S(1)} %fusion.24), channel_id=1, source_target_pairs={{0,16},{2,18},{4,20},{6,22},{8,24},{10,26},{12,28},{14,30},{16,0},... | collective-permute-start | bytes 2162696 | tf_op jit(solution)/shard_map/ppermute | solution.py:208
  552.0 63.8 %collective-permute-start.48 = (bf16[2,2,128,2048]{3,2,0,1:T(8,128)(2,1)}, bf16[2,2,128,2048]{3,2,0,1:T(8,128)(2,1)}, u32[]{:S(2)}, u32[]{:S(2)}) collective-permute-start(bf16[2,2,128,2048]{3,2,0,1:T(8,128)(2,1)} %fusion.14), channel_id=1, source_target_pairs={{0,2},{2,0},{4,6},{6,4},{8,10},{10,8},{12,14},{14,12},{16,18},{18,... | collective-permute-start | bytes 6291464 | tf_op jit(solution)/shard_map/ppermute | solution.py:202
  601.1 67.2 %collective-permute-start.93 = (bf16[512,1408]{1,0:T(8,128)(2,1)S(1)}, bf16[512,1408]{1,0:T(8,128)(2,1)S(1)}, u32[]{:S(2)}, u32[]{:S(2)}) collective-permute-start(bf16[512,1408]{1,0:T(8,128)(2,1)S(1)} %copy-done.60), channel_id=1, source_target_pairs={{24,16},{26,18},{28,20},{30,22},{16,8},{18,10},{20,12},{22,14},{8,... | collective-permute-start | bytes 4325384 | tf_op jit(solution)/shard_map/ppermute | solution.py:208
  604.5 63.9 %collective-permute-start.92 = (bf16[512,1408]{1,0:T(8,128)(2,1)S(1)}, bf16[512,1408]{1,0:T(8,128)(2,1)S(1)}, u32[]{:S(2)}, u32[]{:S(2)}) collective-permute-start(bf16[512,1408]{1,0:T(8,128)(2,1)S(1)} %copy-done.59), channel_id=1, source_target_pairs={{0,8},{2,10},{4,12},{6,14},{8,16},{10,18},{12,20},{14,22},{16,24},... | collective-permute-start | bytes 4325384 | tf_op jit(solution)/shard_map/ppermute | solution.py:208
  607.3 92.3 %collective-permute-start.95 = (bf16[512,1408]{1,0:T(8,128)(2,1)S(1)}, bf16[512,1408]{1,0:T(8,128)(2,1)S(1)}, u32[]{:S(2)}, u32[]{:S(2)}) collective-permute-start(bf16[512,1408]{1,0:T(8,128)(2,1)S(1)} %fusion.6), channel_id=1, source_target_pairs={{0,16},{2,18},{4,20},{6,22},{8,24},{10,26},{12,28},{14,30},{16,0},... | collective-permute-start | bytes 4325384 | tf_op jit(solution)/shard_map/ppermute | solution.py:208
  665.9 38.8 %collective-permute-start.64 = (bf16[2,128,1024]{2,1,0:T(8,128)(2,1)S(1)}, bf16[2,128,1024]{2,1,0:T(8,128)(2,1)S(1)}, u32[]{:S(2)}, u32[]{:S(2)}) collective-permute-start(bf16[2,128,1024]{2,1,0:T(8,128)(2,1)S(1)} %pad_maximum_fusion.20), channel_id=1, source_target_pairs={{0,1},{1,0},{2,3},{3,2},{4,5},{5,4},{6,7},{7,6},{8,9},{9,8},{10,11... | collective-permute-start | bytes 1572872 | tf_op jit(solution)/shard_map/ppermute | solution.py:205
  702.9 27.3 %collective-permute-start.97 = (bf16[128,1408]{1,0:T(8,128)(2,1)S(1)}, bf16[128,1408]{1,0:T(8,128)(2,1)S(1)}, u32[]{:S(2)}, u32[]{:S(2)}) collective-permute-start(bf16[128,1408]{1,0:T(8,128)(2,1)S(1)} %get-tuple-element.182), channel_id=1, source_target_pairs={{0,4},{2,6},{4,0},{6,2},{8,12},{10,14},{12,8},{14,10},{16,20},{18,... | collective-permute-start | bytes 1081352 | tf_op jit(solution)/shard_map/ppermute | solution.py:202
  704.1 26.1 %collective-permute-start.98 = (bf16[128,1408]{1,0:T(8,128)(2,1)S(1)}, bf16[128,1408]{1,0:T(8,128)(2,1)S(1)}, u32[]{:S(2)}, u32[]{:S(2)}) collective-permute-start(bf16[128,1408]{1,0:T(8,128)(2,1)S(1)} %get-tuple-element.181), channel_id=1, source_target_pairs={{0,2},{2,0},{4,6},{6,4},{8,10},{10,8},{12,14},{14,12},{16,18},{18,... | collective-permute-start | bytes 1081352 | tf_op jit(solution)/shard_map/ppermute | solution.py:202
  704.7 100.6 %collective-permute-start.53 = (f32[128,2048]{1,0:T(8,128)}, f32[128,2048]{1,0:T(8,128)}, u32[]{:S(2)}, u32[]{:S(2)}) collective-permute-start(f32[128,2048]{1,0:T(8,128)} %get-tuple-element.207), channel_id=1, source_target_pairs={{0,1},{1,0},{2,3},{3,2},{4,5},{5,4},{6,7},{7,6},{8,9},{9,8},{10,11... | collective-permute-start | bytes 3145736 | tf_op jit(solution)/shard_map/ppermute | solution.py:205
  718.5 40.6 %collective-permute-start.65 = (bf16[2,2,128,2048]{3,2,0,1:T(8,128)(2,1)}, bf16[2,2,128,2048]{3,2,0,1:T(8,128)(2,1)}, u32[]{:S(2)}, u32[]{:S(2)}) collective-permute-start(bf16[2,2,128,2048]{3,2,0,1:T(8,128)(2,1)} %maximum_maximum_fusion.1), channel_id=1, source_target_pairs={{0,2},{2,0},{4,6},{6,4},{8,10},{10,8},{12,14},{14,12},{16,18},{18,... | collective-permute-start | bytes 6291464 | tf_op jit(solution)/shard_map/ppermute | solution.py:202
  785.6 97.5 %collective-permute-start.66 = (bf16[2,2,128,2048]{3,2,0,1:T(8,128)(2,1)}, bf16[2,2,128,2048]{3,2,0,1:T(8,128)(2,1)}, u32[]{:S(2)}, u32[]{:S(2)}) collective-permute-start(bf16[2,2,128,2048]{3,2,0,1:T(8,128)(2,1)} %fusion.16), channel_id=1, source_target_pairs={{0,2},{2,0},{4,6},{6,4},{8,10},{10,8},{12,14},{14,12},{16,18},{18,... | collective-permute-start | bytes 6291464 | tf_op jit(solution)/shard_map/ppermute | solution.py:202
  796.0 33.3 %collective-permute-start.74 = (bf16[512,768]{1,0:T(8,128)(2,1)S(1)}, bf16[512,768]{1,0:T(8,128)(2,1)S(1)}, u32[]{:S(2)}, u32[]{:S(2)}) collective-permute-start(bf16[512,768]{1,0:T(8,128)(2,1)S(1)} %slice_select_fusion.1), channel_id=1, source_target_pairs={{0,8},{2,10},{4,12},{6,14},{24,16},{26,18},{28,20},{30,22},{1,9},{... | collective-permute-start | bytes 2359304 | tf_op jit(solution)/shard_map/ppermute | solution.py:208
  805.3 23.1 %collective-permute-start.88 = (bf16[512,256]{1,0:T(8,128)(2,1)S(1)}, bf16[512,256]{1,0:T(8,128)(2,1)S(1)}, u32[]{:S(2)}, u32[]{:S(2)}) collective-permute-start(bf16[512,256]{1,0:T(8,128)(2,1)S(1)} %fusion.51), channel_id=1, source_target_pairs={{0,16},{2,18},{4,20},{6,22},{8,24},{10,26},{12,28},{14,30},{16,0},... | collective-permute-start | bytes 786440 | tf_op jit(solution)/shard_map/ppermute | solution.py:208
  813.7 30.5 %collective-permute-start.73 = (bf16[512,768]{1,0:T(8,128)(2,1)}, bf16[512,768]{1,0:T(8,128)(2,1)}, u32[]{:S(2)}, u32[]{:S(2)}) collective-permute-start(bf16[512,768]{1,0:T(8,128)(2,1)} %get-tuple-element.164), channel_id=1, source_target_pairs={{24,16},{26,18},{28,20},{30,22},{16,8},{18,10},{20,12},{22,14},{8,... | collective-permute-start | bytes 2359304 | tf_op jit(solution)/shard_map/ppermute | solution.py:208
  822.9 22.7 %collective-permute-start.72 = (bf16[512,768]{1,0:T(8,128)(2,1)}, bf16[512,768]{1,0:T(8,128)(2,1)}, u32[]{:S(2)}, u32[]{:S(2)}) collective-permute-start(bf16[512,768]{1,0:T(8,128)(2,1)} %get-tuple-element.163), channel_id=1, source_target_pairs={{0,8},{2,10},{4,12},{6,14},{8,16},{10,18},{12,20},{14,22},{16,24},... | collective-permute-start | bytes 2359304 | tf_op jit(solution)/shard_map/ppermute | solution.py:208
  833.1 46.0 %collective-permute-start.75 = (bf16[512,768]{1,0:T(8,128)(2,1)}, bf16[512,768]{1,0:T(8,128)(2,1)}, u32[]{:S(2)}, u32[]{:S(2)}) collective-permute-start(bf16[512,768]{1,0:T(8,128)(2,1)} %fusion.18), channel_id=1, source_target_pairs={{0,16},{2,18},{4,20},{6,22},{8,24},{10,26},{12,28},{14,30},{16,0},... | collective-permute-start | bytes 2359304 | tf_op jit(solution)/shard_map/ppermute | solution.py:208
  921.7 25.2 %collective-permute-start.71 = (f32[128,2048]{1,0:T(8,128)}, f32[128,2048]{1,0:T(8,128)}, u32[]{:S(2)}, u32[]{:S(2)}) collective-permute-start(f32[128,2048]{1,0:T(8,128)} %fusion.39), channel_id=1, source_target_pairs={{0,1},{1,0},{2,3},{3,2},{4,5},{5,4},{6,7},{7,6},{8,9},{9,8},{10,11... | collective-permute-start | bytes 3145736 | tf_op jit(solution)/shard_map/ppermute | solution.py:205
  (157 other events, 1771.3 us)

commit v2 on v1

--- a/solution.py
+++ b/solution.py
@@ -68,29 +68,6 @@
     rows = lax.broadcasted_iota(jnp.int32, (size, size), 0)
     cols = lax.broadcasted_iota(jnp.int32, (size, size), 1)
     return (seg_col == seg_row) & (cols <= rows)
-
-
-def attend_kernel(proj_ref, bias_ref, cos_ref, low_ref, upp_ref, col_ref, row_ref, qkv_ref, out_ref):
-    size, wide = out_ref.shape
-    proj = proj_ref[...] + bias_ref[...]
-    cos_t, low_t, upp_t = cos_ref[...], low_ref[...], upp_ref[...]
-    query = spin(proj[:, :wide], cos_t, low_t, upp_t).astype(BF16)
-    key = spin(proj[:, wide : 2 * wide], cos_t, low_t, upp_t).astype(BF16)
-    value = proj[:, 2 * wide :].astype(BF16)
-    qkv_ref[:, :wide] = query
-    qkv_ref[:, wide : 2 * wide] = key
-    qkv_ref[:, 2 * wide :] = value
-    allowed = mask_of(col_ref[...], row_ref[...], size)
-    head_of = lax.broadcasted_iota(jnp.int32, (size, wide), 1) // HD
-    total = jnp.zeros((size, wide), F32)
-    for head in range(wide // HD):
-        mine = head_of == head
-        scores = dot(jnp.where(mine, query, jnp.zeros_like(query)), key, 1, 1) * HD ** (-0.5)
-        scores = jnp.where(allowed, scores, -1e30)
-        weights = jnp.exp(scores - jnp.max(scores, axis=1, keepdims=True))
-        prob = weights / jnp.sum(weights, axis=1, keepdims=True)
-        total = jnp.where(mine, dot(prob.astype(BF16), value, 1, 0), total)
-    out_ref[...] = total.astype(BF16)
 
 
 def attend_back_kernel(qkv_ref, do_ref, cos_ref, low_ref, upp_ref, col_ref, row_ref, dp_ref, sum_ref):
@@ -134,31 +111,6 @@
     return pl.BlockSpec((size, wide), lambda i: (i, 0))
 
 
-def attend(proj, bias, tables, seg_col, seg_row, seqs, size, wide):
-    return pl.pallas_call(
-        attend_kernel,
-        grid=(seqs,),
-        in_specs=[
-            row_blocks(size, 3 * wide),
-            pl.BlockSpec((1, 3 * wide), lambda i: (0, 0)),
-            row_blocks(size, wide),
-            row_blocks(size, wide),
-            row_blocks(size, wide),
-            row_blocks(size, 1),
-            pl.BlockSpec((None, 1, size), lambda i: (i, 0, 0)),
-        ],
-        out_specs=[row_blocks(size, 3 * wide), row_blocks(size, wide)],
-        out_shape=[
-            jax.ShapeDtypeStruct((seqs * size, 3 * wide), BF16),
-            jax.ShapeDtypeStruct((seqs * size, wide), BF16),
-        ],
-        cost_estimate=pl.CostEstimate(
-            flops=seqs * 8 * size * size * wide, bytes_accessed=seqs * size * wide * 32, transcendentals=seqs * size * size * 4
-        ),
-        name="attend",
-    )(proj, bias, *tables, seg_col, seg_row)
-
-
 def attend_back(qkv, grad, tables, seg_col, seg_row, seqs, size, wide):
     return pl.pallas_call(
         attend_back_kernel,
@@ -185,6 +137,530 @@
         ),
         name="attend_back",
     )(qkv, grad, *tables, seg_col, seg_row)
+
+
+class Place:
+    def __init__(self, count):
+        self.count = count
+        self.lines = count // TP
+        self.me = lax.axis_index("dp")
+        self.t = lax.axis_index("tensor")
+        self.u = self.me // TP
+        self.j = self.me % TP
+        self.x = self.j // 2
+        self.c = self.j % 2
+        self.core_peer = self.me + 1 - 2 * self.c
+        self.x_peer = self.me + 2 - 4 * self.x
+
+    def group(self, k):
+        x = (self.x + k // 2) % 2
+        return self.u * TP + x * 2 + self.c, (self.t + k % 2) % 2, x
+
+
+def remote(src, dst, send_sem, recv_sem, dp, t):
+    return pltpu.make_async_remote_copy(
+        src_ref=src,
+        dst_ref=dst,
+        send_sem=send_sem,
+        recv_sem=recv_sem,
+        device_id=(dp, t),
+        device_id_type=pl.DeviceIdType.MESH,
+    )
+
+
+def wait_bytes(ref, sem):
+    pltpu.make_async_copy(ref, ref, sem).wait()
+
+
+def greet(place):
+    barrier = pltpu.get_barrier_semaphore()
+
+    @pl.loop(1, place.count)
+    def _(k):
+        pl.semaphore_signal(
+            barrier,
+            inc=1,
+            device_id=((place.me + k) % place.count, place.t),
+            device_id_type=pl.DeviceIdType.MESH,
+        )
+
+    for k in (1, 3):
+        dp, t, _ = place.group(k)
+        pl.semaphore_signal(barrier, inc=1, device_id=(dp, t), device_id_type=pl.DeviceIdType.MESH)
+    pl.semaphore_wait(barrier, place.count + 1)
+
+
+def each_dest(place, act):
+    if place.lines == 4:
+
+        @pl.loop(1, TP)
+        def _(q):
+            j = (place.j + q) % TP
+            act(place.u * TP + j, place.u, j)
+
+        @pl.loop(0, TP)
+        def _(q):
+            j = (place.j + q) % TP
+            for dz in (2, 1, 3):
+                u = (place.u + dz) % 4
+                act(u * TP + j, u, j)
+
+    else:
+
+        @pl.loop(1, place.count)
+        def _(k):
+            dest = (place.me + k) % place.count
+            act(dest, dest // TP, dest % TP)
+
+
+class WeightGather:
+    def __init__(self, place, index, src, dst, send_sem, recv_sem):
+        self.place, self.src, self.dst = place, src, dst
+        self.send_sem, self.recv_sem = send_sem.at[index], recv_sem.at[index]
+        self.rows = src.shape[1]
+
+    def copy(self, dest, u, j):
+        p = self.place
+        mine = self.dst.at[pl.ds(p.me * self.rows, self.rows)]
+        far = 0
+        if p.lines == 4:
+            far = (((p.u == 0) & (u == 2)) | ((p.u == 3) & (u == 1))).astype(jnp.int32)
+        return remote(self.src.at[j], mine, self.send_sem.at[dest], self.recv_sem.at[far], dest, p.t)
+
+    def when_sent(self, u, act):
+        p = self.place
+        if p.lines == 4:
+            pl.when(jnp.abs(p.u - u) < 3)(act)
+        else:
+            act()
+
+    def start(self):
+        p = self.place
+        mine = self.dst.at[pl.ds(p.me * self.rows, self.rows)]
+        pltpu.make_async_copy(self.src.at[p.j], mine, self.recv_sem.at[0]).start()
+        each_dest(p, lambda dest, u, j: self.when_sent(u, lambda: self.copy(dest, u, j).start()))
+
+    def forward(self):
+        p = self.place
+        size = TP * self.rows
+        chunk = self.dst.at[pl.ds(jnp.where(p.u == 2, 0, 3) * size, size)]
+        dest = p.me + jnp.where(p.u == 2, TP, -TP)
+        return remote(chunk, chunk, self.send_sem.at[p.me], self.recv_sem.at[1], dest, p.t)
+
+    def arrive(self):
+        p = self.place
+        size = TP * self.rows
+        if p.lines == 4:
+            wait_bytes(self.dst.at[pl.ds(0, size)], self.recv_sem.at[1])
+            pl.when((p.u == 1) | (p.u == 2))(lambda: self.forward().start())
+            wait_bytes(self.dst.at[pl.ds(0, 3 * size)], self.recv_sem.at[0])
+        else:
+            wait_bytes(self.dst, self.recv_sem.at[0])
+
+    def finish(self):
+        p = self.place
+        each_dest(
+            p, lambda dest, u, j: self.when_sent(u, lambda: self.copy(dest, u, j).wait_send())
+        )
+        if p.lines == 4:
+            pl.when((p.u == 1) | (p.u == 2))(lambda: self.forward().wait_send())
+
+
+class GroupSum:
+    def __init__(self, place, to_core, from_core, here, low, parts, core_sem, part_sem):
+        self.place = place
+        self.to_core, self.from_core, self.here, self.low, self.parts = to_core, from_core, here, low, parts
+        self.core_sem, self.part_sem = core_sem, part_sem
+
+    def core_copy(self, x):
+        p = self.place
+        return remote(
+            self.to_core.at[x], self.from_core.at[x], self.core_sem.at[0, x], self.core_sem.at[1, x], p.core_peer, p.t
+        )
+
+    def part_copy(self, k):
+        p = self.place
+        half = self.parts.shape[1]
+        dp, t, x = p.group(k)
+        block = self.low.at[x, pl.ds(pl.multiple_of(t * half, half), half)]
+        return remote(block, self.parts.at[k - 1], self.part_sem.at[0, k], self.part_sem.at[1, k], dp, t)
+
+    def run(self, product):
+        p = self.place
+        size, step = self.here.shape[1], min(512, D)
+        for x in range(2):
+
+            @pl.loop(0, D // step)
+            def _(n):
+                at = pl.ds(pl.multiple_of(n * step, step), step)
+                self.to_core[x, :, at] = product(x * 2 + 1 - p.c, n, step).astype(BF16)
+
+            self.core_copy(x).start()
+        for x in range(2):
+
+            @pl.loop(0, D // step)
+            def _(n):
+                at = pl.ds(pl.multiple_of(n * step, step), step)
+                self.here[x, :, at] = product(x * 2 + p.c, n, step)
+
+        for x in range(2):
+            self.core_copy(x).wait_recv()
+
+            @pl.loop(0, size // 32)
+            def _(i):
+                at = pl.ds(pl.multiple_of(i * 32, 32), 32)
+                total = self.here[x, at, :] + self.from_core[x, at, :].astype(F32)
+                self.here[x, at, :] = total
+                self.low[x, at, :] = total.astype(BF16)
+
+        for k in (3, 2, 1):
+            self.part_copy(k).start()
+        for k in (3, 2, 1):
+            self.part_copy(k).wait_recv()
+
+    def total(self, at, rows):
+        p = self.place
+        half = self.parts.shape[1]
+        value = self.here[p.x, pl.ds(pl.multiple_of(p.t * half + at, 32), rows), :]
+        for k in range(3):
+            value = value + self.parts[k, pl.ds(pl.multiple_of(at, 32), rows), :].astype(F32)
+        return value
+
+    def finish(self):
+        for x in range(2):
+            self.core_copy(x).wait_send()
+        for k in (1, 2, 3):
+            self.part_copy(k).wait_send()
+
+
+class GroupGather:
+    def __init__(self, place, out, size, part_sem, core_sem):
+        self.place, self.out, self.half = place, out, size // 2
+        self.part_sem, self.core_sem = part_sem, core_sem
+
+    def block(self, x, t):
+        p = self.place
+        start = ((x * 2 + p.c) * 2 + t) * self.half
+        return self.out.at[pl.ds(pl.multiple_of(start, self.half), self.half)]
+
+    def part_copy(self, k):
+        p = self.place
+        dp, t, _ = p.group(k)
+        mine = self.block(p.x, p.t)
+        return remote(mine, mine, self.part_sem.at[0, k], self.part_sem.at[1, k], dp, t)
+
+    def core_copy(self, k):
+        p = self.place
+        _, t, x = p.group(k)
+        block = self.block(x, t)
+        return remote(block, block, self.core_sem.at[0, k], self.core_sem.at[1, k], p.core_peer, p.t)
+
+    def run(self):
+        for k in (3, 2, 1):
+            self.part_copy(k).start()
+        self.core_copy(0).start()
+        for k in (1, 2, 3):
+            self.part_copy(k).wait_recv()
+            self.core_copy(k).start()
+        for k in range(4):
+            self.core_copy(k).wait_recv()
+
+    def finish(self):
+        for k in (1, 2, 3):
+            self.part_copy(k).wait_send()
+        for k in range(4):
+            self.core_copy(k).wait_send()
+
+
+class GroupPieces:
+    def __init__(self, place, src, out, sem):
+        self.place, self.src, self.out, self.sem = place, src, out, sem
+
+    def own(self):
+        return pltpu.make_async_copy(self.src, self.out.at[self.place.j], self.sem.at[0, 0])
+
+    def near(self, k):
+        p = self.place
+        dest = p.core_peer if k == 1 else p.x_peer
+        return remote(self.src, self.out.at[p.j], self.sem.at[0, k], self.sem.at[1, k], dest, p.t)
+
+    def relay(self):
+        p = self.place
+        block = self.out.at[(p.j + 2) % TP]
+        return remote(block, block, self.sem.at[0, 3], self.sem.at[1, 3], p.core_peer, p.t)
+
+    def start(self):
+        self.near(2).start()
+        self.near(1).start()
+        self.own().start()
+
+    def pass_on(self):
+        self.near(2).wait_recv()
+        self.relay().start()
+
+    def arrive(self):
+        self.near(1).wait_recv()
+        self.relay().wait_recv()
+        self.own().wait()
+
+    def finish(self):
+        self.near(1).wait_send()
+        self.near(2).wait_send()
+        self.relay().wait_send()
+
+
+def tables_of(aux, wide):
+    half = ROT // 2
+    line = lax.broadcasted_iota(jnp.int32, (aux.shape[1], wide), 0)
+    lane = lax.broadcasted_iota(jnp.int32, (aux.shape[1], wide), 1) % HD
+    first = lane < half
+    second = (lane >= half) & (lane < ROT)
+
+    def spread(pick, sign):
+        table = jnp.where(pick, sign, 0.0).astype(F32)
+        return lax.dot_general(
+            aux, table, (((1,), (0,)), ((), ())), precision=lax.Precision.HIGHEST, preferred_element_type=F32
+        )
+
+    rest = lax.broadcasted_iota(jnp.int32, (aux.shape[0], wide), 1) % HD >= ROT
+    cos_t = spread((line == lane % half) & (first | second), 1.0) + jnp.where(rest, 1.0, 0.0)
+    low_t = spread((line == lane + half) & first, -1.0)
+    upp_t = spread((line == lane) & second, 1.0)
+    return cos_t, low_t, upp_t
+
+
+def attend_values(query, key, value, allowed):
+    head_of = lax.broadcasted_iota(jnp.int32, query.shape, 1) // HD
+    total = jnp.zeros(query.shape, F32)
+    for head in range(query.shape[1] // HD):
+        mine = head_of == head
+        scores = dot(jnp.where(mine, query, jnp.zeros_like(query)), key, 1, 1) * HD ** (-0.5)
+        scores = jnp.where(allowed, scores, -1e30)
+        weights = jnp.exp(scores - jnp.max(scores, axis=1, keepdims=True))
+        prob = weights / jnp.sum(weights, axis=1, keepdims=True)
+        total = jnp.where(mine, dot(prob.astype(BF16), value, 1, 0), total)
+    return total
+
+
+def forward_kernel(
+    count,
+    small_src, aux_src, row_src, tok_src, cot_src, wq_src, wo_src, wg_src, wd_src,
+    wq_out, wo_out, wg_out, wd_out, h1_out, h2_out, cot_out, aux_out, row_out,
+    qkv, att, hid, slope, gain, resid, norms,
+    wq, wo, wg, wd, tok, h1, h2, small, aux_all, row_all, to_core, from_core, here, low, parts,
+    w_send, w_recv, small_sem, aux_sem, row_sem, tok_sem, cot_sem, core_sem, part_sem, part2_sem, core2_sem, out_sem,
+):
+    p = Place(count)
+    size = tok_src.shape[0]
+    half = size // 2
+    wide = att.shape[1]
+    rows = wq_src.shape[1]
+    greet(p)
+
+    auxes = GroupPieces(p, aux_src, aux_all, aux_sem)
+    rowses = GroupPieces(p, row_src, row_all, row_sem)
+    tokens = GroupPieces(p, tok_src, tok, tok_sem)
+    cots = GroupPieces(p, cot_src, cot_out, cot_sem)
+
+    def small_copy(dest):
+        return remote(small_src, small.at[p.me], small_sem.at[dest], small_sem.at[count], dest, p.t)
+
+    own_small = pltpu.make_async_copy(small_src, small.at[p.me], small_sem.at[count])
+    own_small.start()
+    each_dest(p, lambda dest, u, j: small_copy(dest).start())
+    auxes.start()
+    rowses.start()
+    tokens.start()
+    gathers = [
+        WeightGather(p, i, src, dst, w_send, w_recv)
+        for i, (src, dst) in enumerate(((wq_src, wq), (wo_src, wo), (wg_src, wg), (wd_src, wd)))
+    ]
+    gathers[0].start()
+    gathers[1].start()
+    auxes.pass_on()
+    rowses.pass_on()
+    tokens.pass_on()
+    gathers[2].start()
+
+    wait_bytes(small, small_sem.at[count])
+    per_tile = 128 // rows
+    for m in range(D // 128):
+        tile = jnp.zeros((8, 128), F32)
+        for i in range(per_tile):
+            tile = tile + small[m * per_tile + i].astype(F32)[0:8]
+        norms[0:8, m * 128 : (m + 1) * 128] = tile
+    bias_rows = small.shape[1] - 16
+    total = jnp.zeros((bias_rows, 128), F32)
+    for d in range(count):
+        total = total + small[d].astype(F32)[16:]
+    for i in range(bias_rows):
+        norms[8:9, i * 128 : (i + 1) * 128] = total[i : i + 1]
+
+    auxes.arrive()
+    rowses.arrive()
+    tokens.arrive()
+    aux_out[...] = aux_all[...]
+    row_out[...] = row_all[...]
+
+    @pl.loop(0, TP * size // 32)
+    def _(i):
+        s, at = i // (size // 32), pl.multiple_of(i % (size // 32) * 32, 32)
+        values = tok[s, pl.ds(at, 32), :].astype(F32)
+        normed, _, _ = layer_norm(values, norms[0:1, :D], norms[1:2, :D])
+        h1[pl.ds(pl.multiple_of(i * 32, 32), 32), :] = normed.astype(BF16)
+
+    h1_copy = pltpu.make_async_copy(h1, h1_out, out_sem.at[0])
+    h1_copy.start()
+    gathers[0].arrive()
+    head_wide = (bias_rows * 128) // 3
+
+    @pl.loop(0, TP)
+    def _(s):
+        at = pl.ds(pl.multiple_of(s * size, size), size)
+        proj = dot(h1[at, :], wq[...], 1, 0)
+        aux = aux_all[s]
+        tables = tables_of(aux, wide)
+
+        def part(k):
+            lanes = pl.ds(pl.multiple_of(k * head_wide + p.j * wide, 128), wide)
+            return proj[:, k * wide : (k + 1) * wide] + norms[8:9, lanes]
+
+        query = spin(part(0), *tables).astype(BF16)
+        key = spin(part(1), *tables).astype(BF16)
+        value = part(2).astype(BF16)
+        qkv[at, :wide] = query
+        qkv[at, wide : 2 * wide] = key
+        qkv[at, 2 * wide :] = value
+        allowed = mask_of(aux[:, ROT : ROT + 1], row_all[s, 0:1, :], size)
+        att[at, :] = attend_values(query, key, value, allowed).astype(BF16)
+
+    gathers[1].arrive()
+    sums = GroupSum(p, to_core, from_core, here, low, parts, core_sem, part_sem)
+
+    def attention_product(s, n, step):
+        at = pl.ds(pl.multiple_of(s * size, size), size)
+        return dot(att[at, :], wo[pl.ds(pl.multiple_of(n * step, step), step), :], 1, 1)
+
+    sums.run(attention_product)
+
+    @pl.loop(0, half // 32)
+    def _(i):
+        at = pl.multiple_of(i * 32, 32)
+        values = tok_src[pl.ds(pl.multiple_of(p.t * half + at, 32), 32), :].astype(F32)
+        values = values + sums.total(at, 32)
+        resid[pl.ds(at, 32), :] = values
+        normed, _, _ = layer_norm(values, norms[2:3, :D], norms[3:4, :D])
+        start = (p.j * 2 + p.t) * half + at
+        h2[pl.ds(pl.multiple_of(start, 32), 32), :] = normed.astype(BF16)
+
+    spread = GroupGather(p, h2, size, part2_sem, core2_sem)
+    spread.run()
+    gathers[3].start()
+    cots.start()
+    h2_copy = pltpu.make_async_copy(h2, h2_out, out_sem.at[1])
+    h2_copy.start()
+    gathers[2].arrive()
+
+    full = hid.shape[1] - 128
+
+    @pl.loop(0, TP)
+    def _(s):
+        at = pl.ds(pl.multiple_of(s * size, size), size)
+        rows_in = h2[at, :]
+        gate = dot(rows_in, wg[:, :full], 1, 0)
+        up = dot(rows_in, wg[:, full : 2 * full], 1, 0)
+        sig = jax.nn.sigmoid(gate)
+        hid[at, :full] = (gate * sig * up).astype(BF16)
+        slope[at, :full] = (up * sig * (1.0 + gate * (1.0 - sig))).astype(BF16)
+        gain[at, :full] = (gate * sig).astype(BF16)
+        gate = dot(rows_in, wg[:, 2 * full :], 1, 0)
+        up = pltpu.roll(gate, 64, 1)
+        sig = jax.nn.sigmoid(gate)
+        first = lax.broadcasted_iota(jnp.int32, gate.shape, 1) < 64
+        hid[at, full:] = jnp.where(first, gate * sig * up, 0.0).astype(BF16)
+        slope[at, full:] = jnp.where(first, up * sig * (1.0 + gate * (1.0 - sig)), 0.0).astype(BF16)
+        gain[at, full:] = jnp.where(first, gate * sig, 0.0).astype(BF16)
+
+    copies = [h1_copy, h2_copy]
+    for i, (src, dst) in enumerate(((wq, wq_out), (wo, wo_out), (wg, wg_out))):
+        copies.append(pltpu.make_async_copy(src, dst, out_sem.at[2 + i]))
+        copies[-1].start()
+    cots.pass_on()
+    cots.arrive()
+    gathers[3].arrive()
+    copies.append(pltpu.make_async_copy(wd, wd_out, out_sem.at[5]))
+    copies[-1].start()
+    for copy in copies:
+        copy.wait()
+    each_dest(p, lambda dest, u, j: small_copy(dest).wait_send())
+    for part in (auxes, rowses, tokens, cots, sums, spread, *gathers):
+        part.finish()
+
+
+def forward(count, small, aux, row, tokens, cot, wq, wo, wg, wd):
+    size = tokens.shape[0]
+    group = TP * size
+    wide, hidden = wo.shape[2], wd.shape[2]
+    any_spec = pl.BlockSpec(memory_space=pl.ANY)
+    vmem = pl.BlockSpec(memory_space=pltpu.VMEM)
+    dma = pltpu.SemaphoreType.DMA
+
+    def out(*shape, dtype=BF16):
+        return jax.ShapeDtypeStruct(shape, dtype)
+
+    pad = -(-hidden // 128) * 128
+    weights = [wq, wo, wg, wd]
+    return pl.pallas_call(
+        functools.partial(forward_kernel, count),
+        in_specs=[vmem, vmem, vmem, vmem] + [any_spec] * 5,
+        out_specs=[any_spec] * 7 + [vmem] * 9,
+        out_shape=[out(D, w.shape[2]) for w in weights]
+        + [
+            out(group, D),
+            out(group, D),
+            out(TP, size, D),
+            out(TP, size, 128, dtype=F32),
+            out(TP, 8, size, dtype=F32),
+            out(group, 3 * wide),
+            out(group, wide),
+            out(group, pad),
+            out(group, pad),
+            out(group, pad),
+            out(size // 2, D, dtype=F32),
+            out(16, max(D, 128 * (small.shape[0] - 16)), dtype=F32),
+        ],
+        scratch_shapes=[pltpu.VMEM((D, w.shape[2]), BF16) for w in weights]
+        + [
+            pltpu.VMEM((TP, size, D), BF16),
+            pltpu.VMEM((group, D), BF16),
+            pltpu.VMEM((group, D), BF16),
+            pltpu.VMEM((count,) + small.shape, BF16),
+            pltpu.VMEM((TP, size, 128), F32),
+            pltpu.VMEM((TP, 8, size), F32),
+            pltpu.VMEM((2, size, D), BF16),
+            pltpu.VMEM((2, size, D), BF16),
+            pltpu.VMEM((2, size, D), F32),
+            pltpu.VMEM((2, size, D), BF16),
+            pltpu.VMEM((3, size // 2, D), BF16),
+            dma((4, count)),
+            dma((4, 2)),
+            dma((count + 1,)),
+            dma((2, 4)),
+            dma((2, 4)),
+            dma((2, 4)),
+            dma((2, 4)),
+            dma((2, 2)),
+            dma((2, 4)),
+            dma((2, 4)),
+            dma((2, 4)),
+            dma((6,)),
+        ],
+        compiler_params=pltpu.CompilerParams(
+            collective_id=0, has_side_effects=True, vmem_limit_bytes=60 * 1024 * 1024
+        ),
+        cost_estimate=pl.CostEstimate(flops=12 * 10**9, bytes_accessed=80 * 10**6, transcendentals=10**7),
+        name="forward",
+    )(small, aux, row, tokens, cot, *weights)
 
 
 class Links:
@@ -343,75 +819,72 @@
     half_seq = seq_len // 2
     group_rows = TP * seq_len
 
-    small = jnp.concatenate(
-        [norm_params.astype(BF16).reshape(-1), qkv_bias.astype(BF16).reshape(-1)]
-    )
-    small = links.line_gather(links.group_gather(small)).reshape(count, -1)
-    norm_rows = small[:, : 4 * rows].reshape(count, 4, rows).transpose(1, 0, 2).reshape(4, D).astype(F32)
-    bias_full = small[:, 4 * rows :].reshape(3, TP, wide)
-    bias_row = lax.dynamic_index_in_dim(bias_full, links.j, 1, False).reshape(1, 3 * wide).astype(F32)
-
-    tokens = links.group_gather(tokens_in[0])
-    segments = links.group_gather(segment_ids[0])
-
-    def weight_chunk(shard):
-        blocks = shard.astype(BF16).transpose(1, 0, 2)
-        return links.group_swap(blocks).reshape(TP * shard.shape[0], shard.shape[2])
-
-    qkv_blocks = qkv_weight.reshape(rows, 3, TP, wide).transpose(0, 2, 1, 3).reshape(rows, TP, 3 * wide)
-    out_blocks = out_weight.T.reshape(rows, TP, wide)
-    gating_blocks = gating_weight.reshape(rows, 2, TP, hid).transpose(0, 2, 1, 3).reshape(rows, TP, 2 * hid)
-    down_blocks = down_weight.T.reshape(rows, TP, hid)
-    qkv_matrix = links.line_gather(weight_chunk(qkv_blocks)).reshape(D, 3 * wide)
-    out_matrix = links.line_gather(weight_chunk(out_blocks)).reshape(D, wide)
-    gating_matrix = links.line_gather(weight_chunk(gating_blocks)).reshape(D, 2 * hid)
-    down_matrix = links.line_gather(weight_chunk(down_blocks)).reshape(D, hid)
-    cotangent = links.group_gather(d_out[0]).reshape(group_rows, D)
+    def cut(shard):
+        return shard.astype(BF16).transpose(1, 0, 2)
+
+    full = hid // 128 * 128
+    gates = gating_weight.astype(BF16).reshape(rows, 2, TP, hid)
+    gates = jnp.concatenate(
+        [gates[:, 0, :, :full], gates[:, 1, :, :full], gates[:, 0, :, full:], gates[:, 1, :, full:]], axis=2
+    )
+    weights = (
+        cut(qkv_weight.reshape(rows, 3, TP, wide).transpose(0, 2, 1, 3).reshape(rows, TP, 3 * wide)),
+        cut(out_weight.T.reshape(rows, TP, wide)),
+        gates.transpose(1, 0, 2),
+        cut(down_weight.T.reshape(rows, TP, hid)),
+    )
+    bias_here = qkv_bias.shape[1]
+    small_norm = lax.dynamic_update_slice(
+        jnp.zeros((16, 128), F32), norm_params, (0, (links.place * rows) % 128)
+    )
+    small_bias = lax.dynamic_update_slice(
+        jnp.zeros((3 * head_local,), F32), qkv_bias[0], (links.place * bias_here,)
+    )
+    small = jnp.concatenate([small_norm, small_bias.reshape(-1, 128)]).astype(BF16)
+    segments = segment_ids[0]
+    earlier = jnp.sum((segments[None, :] < segments[:, None]).astype(jnp.int32), axis=1)
+    positions = (jnp.arange(seq_len, dtype=jnp.int32) - earlier).astype(F32)
+    frequency = 10000.0 ** (-2.0 * jnp.arange(ROT // 2, dtype=F32) / ROT)
+    angles = positions[:, None] * frequency[None, :]
+    aux = jnp.concatenate([jnp.cos(angles), jnp.sin(angles), segments[:, None].astype(F32)], axis=1)
+    aux = jnp.pad(aux, ((0, 0), (0, 128 - aux.shape[1])))
+    row = jnp.broadcast_to(segments.astype(F32)[None], (8, seq_len))
+
+    (
+        qkv_matrix, out_matrix, gating_matrix, down_matrix, normed_one, normed_two, cotangent, aux_all, row_all,
+        qkv_rot, attended, hidden, slope, gain, residual, norm_rows,
+    ) = forward(count, small, aux, row, tokens_in[0], d_out[0], *weights)
+    norm_rows = norm_rows[:4, :D]
+    cotangent = cotangent.reshape(group_rows, D)
+    hidden, slope, gain = hidden[:, :hid], slope[:, :hid], gain[:, :hid]
 
     def own_half(values):
         return lax.dynamic_slice_in_dim(values, links.tensor * half_seq, half_seq, 0)
 
-    earlier = jnp.sum((segments[:, None, :] < segments[:, :, None]).astype(jnp.int32), axis=2)
-    positions = (jnp.arange(seq_len, dtype=jnp.int32)[None] - earlier).astype(F32)
-    frequency = 10000.0 ** (-2.0 * jnp.arange(ROT // 2, dtype=F32) / ROT)
-    angles = positions.reshape(group_rows, 1) * frequency[None, :]
-    cosine, sine_part = jnp.cos(angles), jnp.sin(angles)
+    def to_parts(partial):
+        return partial.reshape(2, 2, 2, half_seq, D)
+
+    heads = wide // HD
+    cosine, sine_part = aux_all.reshape(group_rows, 128)[:, : ROT // 2], aux_all.reshape(group_rows, 128)[:, ROT // 2 : ROT]
     zeros = jnp.zeros((group_rows, HD - ROT), F32)
-    heads = wide // HD
     tables = (
         jnp.tile(jnp.concatenate([cosine, cosine, zeros + 1.0], axis=1), (1, heads)),
         jnp.tile(jnp.concatenate([-sine_part, jnp.zeros_like(sine_part), zeros], axis=1), (1, heads)),
         jnp.tile(jnp.concatenate([jnp.zeros_like(sine_part), sine_part, zeros], axis=1), (1, heads)),
     )
-    seg_col = segments.reshape(group_rows, 1)
-    seg_row = segments.reshape(TP, 1, seq_len)
-
-    normed_one, _, _ = layer_norm(tokens.reshape(group_rows, D).astype(F32), norm_rows[0], norm_rows[1])
-    normed_one = normed_one.astype(BF16)
-    projected = dot(normed_one, qkv_matrix, 1, 0)
-    qkv_rot, attended = attend(projected, bias_row, tables, seg_col, seg_row, TP, seq_len, wide)
-
-    def to_parts(partial):
-        return partial.reshape(2, 2, 2, half_seq, D)
-
-    attention_term = links.scatter_sum(to_parts(dot(attended, out_matrix, 1, 1)))
+    seg_col = aux_all.reshape(group_rows, 128)[:, ROT : ROT + 1].astype(jnp.int32)
+    seg_row = row_all[:, 0:1, :].astype(jnp.int32)
     tokens_own = own_half(tokens_in[0]).astype(F32)
-    residual = tokens_own + attention_term
-    normed_two, scaled_two, inverse_two = layer_norm(residual, norm_rows[2], norm_rows[3])
-    normed_two = links.gather(normed_two.astype(BF16)).reshape(group_rows, D)
-
-    gated_out = dot(normed_two, gating_matrix, 1, 0)
-    gate_part, up_part = gated_out[:, :hid], gated_out[:, hid:]
-    sigmoid_gate = jax.nn.sigmoid(gate_part)
-    hidden = (gate_part * sigmoid_gate * up_part).astype(BF16)
+    _, scaled_two, inverse_two = layer_norm(residual, norm_rows[2], norm_rows[3])
+
     grad_down = dot(cotangent, hidden, 0, 0).astype(BF16)
     down_sum = links.line_scatter_sum(grad_down.reshape(links.lines, TP * rows, hid))
     grad_hidden = dot(cotangent, down_matrix, 1, 0)
-    grad_gate = (
-        grad_hidden * up_part * sigmoid_gate * (1.0 + gate_part * (1.0 - sigmoid_gate))
-    ).astype(BF16)
-    grad_up = (grad_hidden * (gate_part * sigmoid_gate)).astype(BF16)
-    grad_gated = jnp.concatenate([grad_gate, grad_up], axis=1)
+    grad_gate = (grad_hidden * slope.astype(F32)).astype(BF16)
+    grad_up = (grad_hidden * gain.astype(F32)).astype(BF16)
+    grad_gated = jnp.concatenate(
+        [grad_gate[:, :full], grad_up[:, :full], grad_gate[:, full:], grad_up[:, full:]], axis=1
+    )
     normed_grad_two = links.scatter_sum(to_parts(dot(grad_gated, gating_matrix, 1, 1)))
     grad_gating = dot(normed_two, grad_gated, 0, 0).astype(BF16)
     gating_sum = links.line_scatter_sum(grad_gating.reshape(links.lines, TP * rows, 2 * hid))
@@ -453,7 +926,6 @@
     small_grad = small_grad + links.flip(small_grad, 2)
     small_grad = links.line_sum(small_grad)
     norm_grad = lax.dynamic_slice_in_dim(small_grad[: 4 * D].reshape(4, D), links.place * rows, rows, 1)
-    bias_here = qkv_bias.shape[1]
     bias_grad = lax.dynamic_slice_in_dim(
         small_grad[4 * D :].reshape(1, -1), links.place * bias_here, bias_here, 1
     )
@@ -463,9 +935,10 @@
         return links.group_swap(blocks).transpose(1, 0, 2).astype(F32)
 
     down_shard = to_owner(down_sum).reshape(rows, hidden_local).T
-    gating_shard = (
-        to_owner(gating_sum).reshape(rows, TP, 2, hid).transpose(0, 2, 1, 3).reshape(gating_weight.shape)
-    )
+    gating_parts = to_owner(gating_sum)
+    gate_parts = jnp.concatenate([gating_parts[..., :full], gating_parts[..., 2 * full : full + hid]], axis=2)
+    up_parts = jnp.concatenate([gating_parts[..., full : 2 * full], gating_parts[..., full + hid :]], axis=2)
+    gating_shard = jnp.stack([gate_parts, up_parts], axis=1).reshape(gating_weight.shape)
     out_shard = to_owner(out_sum).reshape(rows, head_local).T
     qkv_shard = (
         to_owner(qkv_sum).reshape(rows, TP, 3, wide).transpose(0, 2, 1, 3).reshape(qkv_weight.shape)

time: 965 us -> 870 us (0.902)
  Pallas kernels: 19.2 us -> 297 us
  waiting for transfers between devices: 413 us -> 204 us
  local copies, waits for them, and re-layouts: 222 us -> 151 us
  starting transfers between devices: 136 us -> 75.2 us
  other arithmetic: 95.8 us -> 78.8 us
    pallas_call x1, Pallas kernels: 7.73 us -> 286 us  [forward(): pl.pallas_call(functools.partial(forward_kernel, count), in_specs=[vmem,...]
    ppermute x39 -> x19, waiting for transfers between devices: 293 us -> 117 us  [along(): lax.ppermute(values, 'dp', [(a * TP + r, b * TP + r) for a, b in pairs fo...]
    dynamic_update_slice x13 -> x1, local copies, waits for them, and re-layouts: 86.1 us -> 0.86 us  [per_device(): lax.dynamic_update_slice(jnp.zeros((3 * head_local,), F32), qkv_bias[0],...]
    ppermute x39 -> x19, starting transfers between devices: 85.7 us -> 41.7 us  [along(): lax.ppermute(values, 'dp', [(a * TP + r, b * TP + r) for a, b in pairs fo...]
    ppermute x15 -> x11, waiting for transfers between devices: 64.8 us -> 39.1 us  [swap(): return lax.ppermute(values, 'tensor', [(0, 1), (1, 0)])]
    concatenate x0 -> x5, local copies, waits for them, and re-layouts: none -> 15.9 us  [the longest x1 5.36 us: per_device(): jnp.concatenate([grad_gate[:, :full], grad_up[:, :full], grad_gate[:, ful...]
    another operation x21 -> x1, local copies, waits for them, and re-layouts: 15.6 us -> 0.01 us
    reshape x7 -> x0, local copies, waits for them, and re-layouts: 12.8 us -> none  [the longest x1 6.66 us: per_device(): down_matrix = links.line_gather(weight_chunk(down_blocks)).reshape(D, hid)]
  transfers between devices with their start and end apart: 106 -> 56, of which waited for: 54 -> 29; matrix products, arithmetic and copies ran while one was open for 33% -> 23% of each run, Pallas kernels for 2% -> 1%
where the time goes in v2:
time: 870 us; the launch traced here: 860 us
  Pallas kernels  297 us (34%)
  waiting for transfers between devices  204 us (23%)
  local copies, waits for them, and re-layouts  151 us (17%)
  other arithmetic  78.8 us (9%)
  starting transfers between devices  75.2 us (9%)
  matrix products  51.5 us (6%)
    pallas_call x1, Pallas kernels, forward(): pl.pallas_call(functools.partial(forward_kernel, count), in_specs=[vmem,...  286 us
    ppermute x19, waiting for transfers between devices, along(): lax.ppermute(values, 'dp', [(a * TP + r, b * TP + r) for a, b in pairs fo...  117 us
    unnamed x130, local copies, waits for them, and re-layouts  64.1 us
    dot_general x9, matrix products, dot(): lax.dot_general(a, b, (((ca,), (cb,)), ((), ())), preferred_element_type=...  51.5 us
    ppermute x26, waiting for transfers between devices, flip(): return lax.ppermute(values, 'dp', [(i, i ^ bit) for i in range(self.count)])  47.8 us
    ppermute x19, starting transfers between devices, along(): lax.ppermute(values, 'dp', [(a * TP + r, b * TP + r) for a, b in pairs fo...  41.7 us
    ppermute x11, waiting for transfers between devices, swap(): return lax.ppermute(values, 'tensor', [(0, 1), (1, 0)])  39.1 us
    ppermute x26, starting transfers between devices, flip(): return lax.ppermute(values, 'dp', [(i, i ^ bit) for i in range(self.count)])  20.9 us
  transfers between devices with their start and end apart: 56, of which 29 were waited for; matrix products, arithmetic and copies ran while one was open for 23% of the time, Pallas kernels for 1%

profile of v2, /device:TPU:0, one launch (start us, length us, event | category | flops | bytes accessed | tf_op | source)
XLA Modules:
  0.0 860.3 jit_solution(7608396454699341782)
XLA Ops:
  1.2 4.1 copy.266
  35.7 3.1 concatenate.49
  39.4 286.0 %forward.1 = (bf16[2048,768]{1,0:T(8,128)(2,1)}, bf16[2048,256]{1,0:T(8,128)(2,1)}, bf16[2048,1408]{1,0:T(8,128)(2,1)}, bf16[2048,704]{1,0:T(8,128)(2,1)}, bf16[...) custom-call(bf16[40,128]{1,0:T(8,128)(2,1)} %fusion.56.small_src, ...), custom_call_target="tpu_custom_call" | custom-call | flops 12000000000 | bytes 80000000 | tf_op jit(solution)/shard_map/forward/pallas_call | solution.py:613
  325.4 7.5 multiply_convert_fusion
  335.3 5.4 concatenate.51
  340.7 11.7 %fusion.80 = f32[1024,2048]{1,0:T(8,128)} fusion(bf16[1024,1408]{1,0:T(8,128)(2,1)} %concatenate.51, bf16[2048,1408]{1,0:T(8,128)(2,1)} %get-tuple-element.44), kind=kOutput, calls=%fused_computation.279 | convolution fusion | flops 5905580032 | bytes 17039360 | tf_op jit(solution)/shard_map/dot_general | solution.py:46
  352.3 3.8 fusion.6
  356.2 9.5 %convolution_convert_fusion = bf16[2048,1408]{1,0:T(8,128)(2,1)S(1)} fusion(bf16[1024,2048]{1,0:T(8,128)(2,1)} %get-tuple-element.55, bf16[1024,1408]{1,0:T(8,128)(2,1)} %concatenate.51), kind=kOutput, calls=%fused_computation | convolution fusion | flops 5908463616 | bytes 12845056 | tf_op jit(solution)/shard_map/dot_general | solution.py:46
  371.0 3.5 convolution_convert_fusion.2
  378.5 7.3 reshape.287
  385.8 11.1 %constant_dynamic-slice_fusion.8 = (bf16[1,512,704]{1,0,2:T(2,128)(2,1)}, bf16[1,512,704]{1,0,2:T(2,128)(2,1)S(1)}, bf16[1,512,704]{1,0,2:T(2,128)(2,1)S(1)}, bf16[1,512,704]{1,0,2:T(2,128)(2,1)}) fusion(bf16[4,512,704]{1,0,2:T(4,128)(2,1)} %reshape.287, s32[]{:T(128)S(6)} %select_n.477, s32[]{:T(128)S(6)} %select_n.481, s32[]{:T(128)S(6)} %select_n.479, ...), kind=kLoop, calls=%fused_computation.226 | loop fusion | bytes 5767184 | tf_op jit(solution)/shard_map/jit(dynamic_index_in_dim)/dynamic_slice | solution.py:728
  400.3 5.4 collective-permute-start.49
  433.8 3.6 dynamic-slice_bitcast_fusion.1
  437.4 6.0 copy.299
  443.4 5.6 copy.302
  449.0 5.9 fusion.21
  460.9 29.3 %collective-permute-done.52 = bf16[512,704]{0,1:T(8,128)(2,1)S(1)} collective-permute-done((bf16[512,704]{0,1:T(8,128)(2,1)S(1)}, bf16[512,704]{0,1:T(8,128)(2,1)S(1)}, u32[]{:S(2)}, u32[]{:S(2)}) %collective-permute-start.52) | collective-permute-done | bytes 720928 | tf_op jit(solution)/shard_map/ppermute | solution.py:684
  495.2 3.6 constant_dynamic-slice_fusion.1
  526.4 6.5 collective-permute-done.9
  537.1 8.3 collective-permute-done.3
  549.6 3.3 collective-permute-done.10
  567.0 33.7 %collective-permute-done.45 = bf16[512,1408]{1,0:T(8,128)(2,1)S(1)} collective-permute-done((bf16[512,1408]{1,0:T(8,128)(2,1)S(1)}, bf16[512,1408]{1,0:T(8,128)(2,1)S(1)}, u32[]{:S(2)}, u32[]{:S(2)}) %collective-permute-start.45) | collective-permute-done | bytes 1441824 | tf_op jit(solution)/shard_map/ppermute | solution.py:684
  606.3 7.5 collective-permute-done.46
  613.9 7.4 collective-permute-done.47
  621.6 10.9 %collective-permute-done.12 = bf16[2,128,1024]{2,1,0:T(8,128)(2,1)S(1)} collective-permute-done((bf16[2,128,1024]{2,1,0:T(8,128)(2,1)S(1)}, bf16[2,128,1024]{2,1,0:T(8,128)(2,1)S(1)}, u32[]{:S(2)}, u32[]{:S(2)}) %collective-permute-start.12) | collective-permute-done | bytes 524320 | tf_op jit(solution)/shard_map/ppermute | solution.py:678
  642.9 6.9 multiply_subtract_fusion
  649.8 5.6 copy.314
  655.4 5.7 copy.315
  661.1 3.3 copy.316
  670.6 11.4 %attend_back.1 = (bf16[1024,768]{1,0:T(8,128)(2,1)}, f32[4,1,768]{2,1,0:T(1,128)}) custom-call(bf16[1024,768]{1,0:T(8,128)(2,1)} %get-tuple-element.46.qkv_ref, bf16[1024,256]{1,0:T(8,128)(2,1)} %convolution_convert_fusion.4.do_ref, f32[1024,256]{1,0:T(8,128)} %copy.284.cos_ref, f32[1024,256]{1,0:T(8,128)} %copy.285.low_ref, f32[1024,256]{1,0:T(8,128)} %copy.286.upp_ref, ...), custom_call_target="tpu_custom_call" | custom-call | flops 1342177280 | bytes 8388608 | tf_op jit(solution)/shard_map/attend_back/pallas_call | solution.py:115
  681.9 5.9 fusion.81
  689.8 3.2 copy-done.22
  694.5 5.0 collective-permute-start.37
  699.6 4.1 convolution_convert_fusion.1
  706.4 4.6 collective-permute-start.35
  714.3 7.1 collective-permute-done.36
  722.7 5.8 collective-permute-done.35
  728.6 5.3 collective-permute-start.22
  738.7 4.3 collective-permute-start.25
  746.3 4.9 collective-permute-done.22
  751.2 35.8 %collective-permute-done.25 = bf16[512,768]{1,0:T(8,128)(2,1)} collective-permute-done((bf16[512,768]{1,0:T(8,128)(2,1)}, bf16[512,768]{1,0:T(8,128)(2,1)}, u32[]{:S(2)}, u32[]{:S(2)}) %collective-permute-start.25) | collective-permute-done | bytes 786464 | tf_op jit(solution)/shard_map/ppermute | solution.py:684
  793.6 3.4 bitcast_add_fusion
  803.1 9.8 %collective-permute-done.19 = bf16[2,128,1024]{2,1,0:T(8,128)(2,1)} collective-permute-done((bf16[2,128,1024]{2,1,0:T(8,128)(2,1)}, bf16[2,128,1024]{2,1,0:T(8,128)(2,1)}, u32[]{:S(2)}, u32[]{:S(2)}) %collective-permute-start.19) | collective-permute-done | bytes 524320 | tf_op jit(solution)/shard_map/ppermute | solution.py:681
  816.6 5.3 collective-permute-done.20
  824.8 3.3 collective-permute-done.29
  836.3 3.0 multiply_subtract_fusion.1
  842.4 3.1 copy.312
  848.5 7.9 collective-permute-done.21
  (379 shorter events, 213.1 us)
Async XLA Ops:
  356.2 159.2 %collective-permute-start.6 = (bf16[2,2,128,2048]{3,2,0,1:T(8,128)(2,1)}, bf16[2,2,128,2048]{3,2,0,1:T(8,128)(2,1)}, u32[]{:S(2)}, u32[]{:S(2)}) collective-permute-start(bf16[2,2,128,2048]{3,2,0,1:T(8,128)(2,1)} %fusion.6), channel_id=1, source_target_pairs={{0,2},{2,0},{4,6},{6,4},{8,10},{10,8},{12,14},{14,12},{16,18},{18,... | collective-permute-start | bytes 6291464 | tf_op jit(solution)/shard_map/ppermute | solution.py:678
  367.0 133.7 %collective-permute-start.44 = (bf16[512,1408]{1,0:T(8,128)(2,1)}, bf16[512,1408]{1,0:T(8,128)(2,1)}, u32[]{:S(2)}, u32[]{:S(2)}) collective-permute-start(bf16[512,1408]{1,0:T(8,128)(2,1)} %slice_select_fusion), channel_id=1, source_target_pairs={{0,8},{2,10},{4,12},{6,14},{24,16},{26,18},{28,20},{30,22},{1,9},{... | collective-permute-start | bytes 4325384 | tf_op jit(solution)/shard_map/ppermute | solution.py:684
  376.3 78.6 %collective-permute-start.51 = (bf16[512,704]{0,1:T(8,128)(2,1)}, bf16[512,704]{0,1:T(8,128)(2,1)}, u32[]{:S(2)}, u32[]{:S(2)}) collective-permute-start(bf16[512,704]{0,1:T(8,128)(2,1)} %slice_select_fusion.2), channel_id=1, source_target_pairs={{0,8},{2,10},{4,12},{6,14},{24,16},{26,18},{28,20},{30,22},{1,9},{... | collective-permute-start | bytes 2162696 | tf_op jit(solution)/shard_map/ppermute | solution.py:684
  397.9 62.8 %collective-permute-start.50 = (bf16[512,704]{0,1:T(8,128)(2,1)}, bf16[512,704]{0,1:T(8,128)(2,1)}, u32[]{:S(2)}, u32[]{:S(2)}) collective-permute-start(bf16[512,704]{0,1:T(8,128)(2,1)} %bitcast.369), channel_id=1, source_target_pairs={{24,16},{26,18},{28,20},{30,22},{16,8},{18,10},{20,12},{22,14},{8,... | collective-permute-start | bytes 2162696 | tf_op jit(solution)/shard_map/ppermute | solution.py:684
  400.3 60.6 %collective-permute-start.49 = (bf16[512,704]{0,1:T(8,128)(2,1)}, bf16[512,704]{0,1:T(8,128)(2,1)}, u32[]{:S(2)}, u32[]{:S(2)}) collective-permute-start(bf16[512,704]{0,1:T(8,128)(2,1)} %bitcast.370), channel_id=1, source_target_pairs={{0,8},{2,10},{4,12},{6,14},{8,16},{10,18},{12,20},{14,22},{16,24},... | collective-permute-start | bytes 2162696 | tf_op jit(solution)/shard_map/ppermute | solution.py:684
  456.8 33.3 %collective-permute-start.52 = (bf16[512,704]{0,1:T(8,128)(2,1)S(1)}, bf16[512,704]{0,1:T(8,128)(2,1)S(1)}, u32[]{:S(2)}, u32[]{:S(2)}) collective-permute-start(bf16[512,704]{0,1:T(8,128)(2,1)S(1)} %fusion.15), channel_id=1, source_target_pairs={{0,16},{2,18},{4,20},{6,22},{8,24},{10,26},{12,28},{14,30},{16,0},... | collective-permute-start | bytes 2162696 | tf_op jit(solution)/shard_map/ppermute | solution.py:684
  460.8 60.3 %collective-permute-start = (bf16[2,2,128,2048]{3,2,0,1:T(8,128)(2,1)}, bf16[2,2,128,2048]{3,2,0,1:T(8,128)(2,1)}, u32[]{:S(2)}, u32[]{:S(2)}) collective-permute-start(bf16[2,2,128,2048]{3,2,0,1:T(8,128)(2,1)} %fusion.5), channel_id=1, source_target_pairs={{0,2},{2,0},{4,6},{6,4},{8,10},{10,8},{12,14},{14,12},{16,18},{18,... | collective-permute-start | bytes 6291464 | tf_op jit(solution)/shard_map/ppermute | solution.py:678
  499.0 10.7 %collective-permute-start.54 = (bf16[128,704]{0,1:T(8,128)(2,1)S(1)}, bf16[128,704]{0,1:T(8,128)(2,1)S(1)}, u32[]{:S(2)}, u32[]{:S(2)}) collective-permute-start(bf16[128,704]{0,1:T(8,128)(2,1)S(1)} %bitcast.427), channel_id=1, source_target_pairs={{0,4},{2,6},{4,0},{6,2},{8,12},{10,14},{12,8},{14,10},{16,20},{18,... | collective-permute-start | bytes 540680 | tf_op jit(solution)/shard_map/ppermute | solution.py:678
  500.7 11.0 %collective-permute-start.55 = (bf16[128,704]{0,1:T(8,128)(2,1)S(1)}, bf16[128,704]{0,1:T(8,128)(2,1)S(1)}, u32[]{:S(2)}, u32[]{:S(2)}) collective-permute-start(bf16[128,704]{0,1:T(8,128)(2,1)S(1)} %bitcast.426), channel_id=1, source_target_pairs={{0,2},{2,0},{4,6},{6,4},{8,10},{10,8},{12,14},{14,12},{16,18},{18,... | collective-permute-start | bytes 540680 | tf_op jit(solution)/shard_map/ppermute | solution.py:678
  505.6 59.7 %collective-permute-start.43 = (bf16[512,1408]{1,0:T(8,128)(2,1)S(1)}, bf16[512,1408]{1,0:T(8,128)(2,1)S(1)}, u32[]{:S(2)}, u32[]{:S(2)}) collective-permute-start(bf16[512,1408]{1,0:T(8,128)(2,1)S(1)} %copy-done.31), channel_id=1, source_target_pairs={{24,16},{26,18},{28,20},{30,22},{16,8},{18,10},{20,12},{22,14},{8,... | collective-permute-start | bytes 4325384 | tf_op jit(solution)/shard_map/ppermute | solution.py:684
  509.6 57.4 %collective-permute-start.42 = (bf16[512,1408]{1,0:T(8,128)(2,1)S(1)}, bf16[512,1408]{1,0:T(8,128)(2,1)S(1)}, u32[]{:S(2)}, u32[]{:S(2)}) collective-permute-start(bf16[512,1408]{1,0:T(8,128)(2,1)S(1)} %copy-done.30), channel_id=1, source_target_pairs={{0,8},{2,10},{4,12},{6,14},{8,16},{10,18},{12,20},{14,22},{16,24},... | collective-permute-start | bytes 4325384 | tf_op jit(solution)/shard_map/ppermute | solution.py:684
  511.7 89.1 %collective-permute-start.45 = (bf16[512,1408]{1,0:T(8,128)(2,1)S(1)}, bf16[512,1408]{1,0:T(8,128)(2,1)S(1)}, u32[]{:S(2)}, u32[]{:S(2)}) collective-permute-start(bf16[512,1408]{1,0:T(8,128)(2,1)S(1)} %fusion.1), channel_id=1, source_target_pairs={{0,16},{2,18},{4,20},{6,22},{8,24},{10,26},{12,28},{14,30},{16,0},... | collective-permute-start | bytes 4325384 | tf_op jit(solution)/shard_map/ppermute | solution.py:684
  519.4 13.5 %collective-permute-start.9 = (bf16[2,128,1024]{2,1,0:T(8,128)(2,1)S(1)}, bf16[2,128,1024]{2,1,0:T(8,128)(2,1)S(1)}, u32[]{:S(2)}, u32[]{:S(2)}) collective-permute-start(bf16[2,128,1024]{2,1,0:T(8,128)(2,1)S(1)} %fusion.39), channel_id=1, source_target_pairs={{0,1},{1,0},{2,3},{3,2},{4,5},{5,4},{6,7},{7,6},{8,9},{9,8},{10,11... | collective-permute-start | bytes 1572872 | tf_op jit(solution)/shard_map/ppermute | solution.py:681
  521.1 13.6 %collective-permute-start.7 = (bf16[2,128,1024]{2,1,0:T(8,128)(2,1)S(1)}, bf16[2,128,1024]{2,1,0:T(8,128)(2,1)S(1)}, u32[]{:S(2)}, u32[]{:S(2)}) collective-permute-start(bf16[2,128,1024]{2,1,0:T(8,128)(2,1)S(1)} %fusion.38), channel_id=1, source_target_pairs={{0,4},{2,6},{4,0},{6,2},{8,12},{10,14},{12,8},{14,10},{16,20},{18,... | collective-permute-start | bytes 1572872 | tf_op jit(solution)/shard_map/ppermute | solution.py:678
  532.9 12.5 %collective-permute-start.3 = (bf16[2,128,1024]{2,1,0:T(8,128)(2,1)S(1)}, bf16[2,128,1024]{2,1,0:T(8,128)(2,1)S(1)}, u32[]{:S(2)}, u32[]{:S(2)}) collective-permute-start(bf16[2,128,1024]{2,1,0:T(8,128)(2,1)S(1)} %fusion.37), channel_id=1, source_target_pairs={{0,1},{1,0},{2,3},{3,2},{4,5},{5,4},{6,7},{7,6},{8,9},{9,8},{10,11... | collective-permute-start | bytes 1572872 | tf_op jit(solution)/shard_map/ppermute | solution.py:681
  534.8 13.2 %collective-permute-start.1 = (bf16[2,128,1024]{2,1,0:T(8,128)(2,1)S(1)}, bf16[2,128,1024]{2,1,0:T(8,128)(2,1)S(1)}, u32[]{:S(2)}, u32[]{:S(2)}) collective-permute-start(bf16[2,128,1024]{2,1,0:T(8,128)(2,1)S(1)} %fusion.36), channel_id=1, source_target_pairs={{0,4},{2,6},{4,0},{6,2},{8,12},{10,14},{12,8},{14,10},{16,20},{18,... | collective-permute-start | bytes 1572872 | tf_op jit(solution)/shard_map/ppermute | solution.py:678
  545.3 7.6 collective-permute-start.10
  547.9 6.8 collective-permute-start.8
  563.2 147.9 %collective-permute-start.5 = (f32[128,2048]{1,0:T(8,128)}, f32[128,2048]{1,0:T(8,128)}, u32[]{:S(2)}, u32[]{:S(2)}) collective-permute-start(f32[128,2048]{1,0:T(8,128)} %get-tuple-element.231), channel_id=1, source_target_pairs={{0,1},{1,0},{2,3},{3,2},{4,5},{5,4},{6,7},{7,6},{8,9},{9,8},{10,11... | collective-permute-start | bytes 3145736 | tf_op jit(solution)/shard_map/ppermute | solution.py:681
  564.5 39.9 %collective-permute-start.11 = (bf16[128,1024]{1,0:T(8,128)(2,1)S(1)}, bf16[128,1024]{1,0:T(8,128)(2,1)S(1)}, u32[]{:S(2)}, u32[]{:S(2)}) collective-permute-start(bf16[128,1024]{1,0:T(8,128)(2,1)S(1)} %get-tuple-element.255), channel_id=1, source_target_pairs={{0,1},{1,0},{2,3},{3,2},{4,5},{5,4},{6,7},{7,6},{8,9},{9,8},{10,11... | collective-permute-start | bytes 786440 | tf_op jit(solution)/shard_map/ppermute | solution.py:681
  565.3 39.6 %collective-permute-start.13 = (bf16[128,1024]{1,0:T(8,128)(2,1)S(1)}, bf16[128,1024]{1,0:T(8,128)(2,1)S(1)}, u32[]{:S(2)}, u32[]{:S(2)}) collective-permute-start(bf16[128,1024]{1,0:T(8,128)(2,1)S(1)} %get-tuple-element.256), channel_id=1, source_target_pairs={{0,4},{2,6},{4,0},{6,2},{8,12},{10,14},{12,8},{14,10},{16,20},{18,... | collective-permute-start | bytes 786440 | tf_op jit(solution)/shard_map/ppermute | solution.py:678
  603.0 10.8 %collective-permute-start.46 = (bf16[128,1408]{1,0:T(8,128)(2,1)S(1)}, bf16[128,1408]{1,0:T(8,128)(2,1)S(1)}, u32[]{:S(2)}, u32[]{:S(2)}) collective-permute-start(bf16[128,1408]{1,0:T(8,128)(2,1)S(1)} %get-tuple-element.220), channel_id=1, source_target_pairs={{0,6},{2,4},{4,2},{6,0},{8,14},{10,12},{12,10},{14,8},{16,22},{18,... | collective-permute-start | bytes 1081352 | tf_op jit(solution)/shard_map/ppermute | solution.py:678
  603.1 18.2 %collective-permute-start.47 = (bf16[128,1408]{1,0:T(8,128)(2,1)S(1)}, bf16[128,1408]{1,0:T(8,128)(2,1)S(1)}, u32[]{:S(2)}, u32[]{:S(2)}) collective-permute-start(bf16[128,1408]{1,0:T(8,128)(2,1)S(1)} %get-tuple-element.219), channel_id=1, source_target_pairs={{0,4},{2,6},{4,0},{6,2},{8,12},{10,14},{12,8},{14,10},{16,20},{18,... | collective-permute-start | bytes 1081352 | tf_op jit(solution)/shard_map/ppermute | solution.py:678
  604.4 16.9 %collective-permute-start.48 = (bf16[128,1408]{1,0:T(8,128)(2,1)S(1)}, bf16[128,1408]{1,0:T(8,128)(2,1)S(1)}, u32[]{:S(2)}, u32[]{:S(2)}) collective-permute-start(bf16[128,1408]{1,0:T(8,128)(2,1)S(1)} %get-tuple-element.218), channel_id=1, source_target_pairs={{0,2},{2,0},{4,6},{6,4},{8,10},{10,8},{12,14},{14,12},{16,18},{18,... | collective-permute-start | bytes 1081352 | tf_op jit(solution)/shard_map/ppermute | solution.py:678
  605.1 16.4 %collective-permute-start.14 = (bf16[2,128,1024]{2,1,0:T(8,128)(2,1)S(1)}, bf16[2,128,1024]{2,1,0:T(8,128)(2,1)S(1)}, u32[]{:S(2)}, u32[]{:S(2)}) collective-permute-start(bf16[2,128,1024]{2,1,0:T(8,128)(2,1)S(1)} %pad_maximum_fusion.10), channel_id=1, source_target_pairs={{0,1},{1,0},{2,3},{3,2},{4,5},{5,4},{6,7},{7,6},{8,9},{9,8},{10,11... | collective-permute-start | bytes 1572872 | tf_op jit(solution)/shard_map/ppermute | solution.py:681
  613.8 18.7 %collective-permute-start.12 = (bf16[2,128,1024]{2,1,0:T(8,128)(2,1)S(1)}, bf16[2,128,1024]{2,1,0:T(8,128)(2,1)S(1)}, u32[]{:S(2)}, u32[]{:S(2)}) collective-permute-start(bf16[2,128,1024]{2,1,0:T(8,128)(2,1)S(1)} %pad_maximum_fusion.9), channel_id=1, source_target_pairs={{0,4},{2,6},{4,0},{6,2},{8,12},{10,14},{12,8},{14,10},{16,20},{18,... | collective-permute-start | bytes 1572872 | tf_op jit(solution)/shard_map/ppermute | solution.py:678
  634.3 30.2 %collective-permute-start.15 = (bf16[2,2,128,2048]{3,2,0,1:T(8,128)(2,1)}, bf16[2,2,128,2048]{3,2,0,1:T(8,128)(2,1)}, u32[]{:S(2)}, u32[]{:S(2)}) collective-permute-start(bf16[2,2,128,2048]{3,2,0,1:T(8,128)(2,1)} %maximum_maximum_fusion), channel_id=1, source_target_pairs={{0,2},{2,0},{4,6},{6,4},{8,10},{10,8},{12,14},{14,12},{16,18},{18,... | collective-permute-start | bytes 6291464 | tf_op jit(solution)/shard_map/ppermute | solution.py:678
  689.5 104.2 %collective-permute-start.16 = (bf16[2,2,128,2048]{3,2,0,1:T(8,128)(2,1)}, bf16[2,2,128,2048]{3,2,0,1:T(8,128)(2,1)}, u32[]{:S(2)}, u32[]{:S(2)}) collective-permute-start(bf16[2,2,128,2048]{3,2,0,1:T(8,128)(2,1)} %fusion.7), channel_id=1, source_target_pairs={{0,2},{2,0},{4,6},{6,4},{8,10},{10,8},{12,14},{14,12},{16,18},{18,... | collective-permute-start | bytes 6291464 | tf_op jit(solution)/shard_map/ppermute | solution.py:678
  694.5 11.9 %collective-permute-start.37 = (bf16[512,256]{1,0:T(8,128)(2,1)S(1)}, bf16[512,256]{1,0:T(8,128)(2,1)S(1)}, u32[]{:S(2)}, u32[]{:S(2)}) collective-permute-start(bf16[512,256]{1,0:T(8,128)(2,1)S(1)} %slice_select_fusion.3), channel_id=1, source_target_pairs={{0,8},{2,10},{4,12},{6,14},{24,16},{26,18},{28,20},{30,22},{1,9},{... | collective-permute-start | bytes 786440 | tf_op jit(solution)/shard_map/ppermute | solution.py:684
  703.7 30.9 %collective-permute-start.24 = (bf16[512,768]{1,0:T(8,128)(2,1)S(1)}, bf16[512,768]{1,0:T(8,128)(2,1)S(1)}, u32[]{:S(2)}, u32[]{:S(2)}) collective-permute-start(bf16[512,768]{1,0:T(8,128)(2,1)S(1)} %slice_select_fusion.1), channel_id=1, source_target_pairs={{0,8},{2,10},{4,12},{6,14},{24,16},{26,18},{28,20},{30,22},{1,9},{... | collective-permute-start | bytes 2359304 | tf_op jit(solution)/shard_map/ppermute | solution.py:684
  705.1 16.3 %collective-permute-start.36 = (bf16[512,256]{1,0:T(8,128)(2,1)S(1)}, bf16[512,256]{1,0:T(8,128)(2,1)S(1)}, u32[]{:S(2)}, u32[]{:S(2)}) collective-permute-start(bf16[512,256]{1,0:T(8,128)(2,1)S(1)} %get-tuple-element.226), channel_id=1, source_target_pairs={{24,16},{26,18},{28,20},{30,22},{16,8},{18,10},{20,12},{22,14},{8,... | collective-permute-start | bytes 786440 | tf_op jit(solution)/shard_map/ppermute | solution.py:684
  706.4 22.1 %collective-permute-start.35 = (bf16[512,256]{1,0:T(8,128)(2,1)S(1)}, bf16[512,256]{1,0:T(8,128)(2,1)S(1)}, u32[]{:S(2)}, u32[]{:S(2)}) collective-permute-start(bf16[512,256]{1,0:T(8,128)(2,1)S(1)} %get-tuple-element.225), channel_id=1, source_target_pairs={{0,8},{2,10},{4,12},{6,14},{8,16},{10,18},{12,20},{14,22},{16,24},... | collective-permute-start | bytes 786440 | tf_op jit(solution)/shard_map/ppermute | solution.py:684
  711.1 23.1 %collective-permute-start.38 = (bf16[512,256]{1,0:T(8,128)(2,1)S(1)}, bf16[512,256]{1,0:T(8,128)(2,1)S(1)}, u32[]{:S(2)}, u32[]{:S(2)}) collective-permute-start(bf16[512,256]{1,0:T(8,128)(2,1)S(1)} %fusion.42), channel_id=1, source_target_pairs={{0,16},{2,18},{4,20},{6,22},{8,24},{10,26},{12,28},{14,30},{16,0},... | collective-permute-start | bytes 786440 | tf_op jit(solution)/shard_map/ppermute | solution.py:684
  721.4 24.9 %collective-permute-start.23 = (bf16[512,768]{1,0:T(8,128)(2,1)}, bf16[512,768]{1,0:T(8,128)(2,1)}, u32[]{:S(2)}, u32[]{:S(2)}) collective-permute-start(bf16[512,768]{1,0:T(8,128)(2,1)} %get-tuple-element.199), channel_id=1, source_target_pairs={{24,16},{26,18},{28,20},{30,22},{16,8},{18,10},{20,12},{22,14},{8,... | collective-permute-start | bytes 2359304 | tf_op jit(solution)/shard_map/ppermute | solution.py:684
  728.6 22.7 %collective-permute-start.22 = (bf16[512,768]{1,0:T(8,128)(2,1)}, bf16[512,768]{1,0:T(8,128)(2,1)}, u32[]{:S(2)}, u32[]{:S(2)}) collective-permute-start(bf16[512,768]{1,0:T(8,128)(2,1)} %get-tuple-element.198), channel_id=1, source_target_pairs={{0,8},{2,10},{4,12},{6,14},{8,16},{10,18},{12,20},{14,22},{16,24},... | collective-permute-start | bytes 2359304 | tf_op jit(solution)/shard_map/ppermute | solution.py:684
  734.7 10.0 %collective-permute-start.40 = (bf16[128,256]{1,0:T(8,128)(2,1)S(1)}, bf16[128,256]{1,0:T(8,128)(2,1)S(1)}, u32[]{:S(2)}, u32[]{:S(2)}) collective-permute-start(bf16[128,256]{1,0:T(8,128)(2,1)S(1)} %get-tuple-element.264), channel_id=1, source_target_pairs={{0,4},{2,6},{4,0},{6,2},{8,12},{10,14},{12,8},{14,10},{16,20},{18,... | collective-permute-start | bytes 196616 | tf_op jit(solution)/shard_map/ppermute | solution.py:678
  738.7 48.3 %collective-permute-start.25 = (bf16[512,768]{1,0:T(8,128)(2,1)}, bf16[512,768]{1,0:T(8,128)(2,1)}, u32[]{:S(2)}, u32[]{:S(2)}) collective-permute-start(bf16[512,768]{1,0:T(8,128)(2,1)} %fusion.9), channel_id=1, source_target_pairs={{0,16},{2,18},{4,20},{6,22},{8,24},{10,26},{12,28},{14,30},{16,0},... | collective-permute-start | bytes 2359304 | tf_op jit(solution)/shard_map/ppermute | solution.py:684
  790.1 11.6 %collective-permute-start.26 = (bf16[128,768]{0,1:T(8,128)(2,1)}, bf16[128,768]{0,1:T(8,128)(2,1)}, u32[]{:S(2)}, u32[]{:S(2)}) collective-permute-start(bf16[128,768]{0,1:T(8,128)(2,1)} %bitcast.89), channel_id=1, source_target_pairs={{0,6},{2,4},{4,2},{6,0},{8,14},{10,12},{12,10},{14,8},{16,22},{18,... | collective-permute-start | bytes 589832 | tf_op jit(solution)/shard_map/ppermute | solution.py:678
  792.2 9.7 %collective-permute-start.27 = (bf16[128,768]{0,1:T(8,128)(2,1)}, bf16[128,768]{0,1:T(8,128)(2,1)}, u32[]{:S(2)}, u32[]{:S(2)}) collective-permute-start(bf16[128,768]{0,1:T(8,128)(2,1)} %bitcast.90), channel_id=1, source_target_pairs={{0,4},{2,6},{4,0},{6,2},{8,12},{10,14},{12,8},{14,10},{16,20},{18,... | collective-permute-start | bytes 589832 | tf_op jit(solution)/shard_map/ppermute | solution.py:678
  793.4 8.5 collective-permute-start.28
  798.4 14.4 %collective-permute-start.19 = (bf16[2,128,1024]{2,1,0:T(8,128)(2,1)}, bf16[2,128,1024]{2,1,0:T(8,128)(2,1)}, u32[]{:S(2)}, u32[]{:S(2)}) collective-permute-start(bf16[2,128,1024]{2,1,0:T(8,128)(2,1)} %fusion.41), channel_id=1, source_target_pairs={{0,1},{1,0},{2,3},{3,2},{4,5},{5,4},{6,7},{7,6},{8,9},{9,8},{10,11... | collective-permute-start | bytes 1572872 | tf_op jit(solution)/shard_map/ppermute | solution.py:681
  801.1 14.7 %collective-permute-start.17 = (bf16[2,128,1024]{2,1,0:T(8,128)(2,1)S(1)}, bf16[2,128,1024]{2,1,0:T(8,128)(2,1)S(1)}, u32[]{:S(2)}, u32[]{:S(2)}) collective-permute-start(bf16[2,128,1024]{2,1,0:T(8,128)(2,1)S(1)} %fusion.40), channel_id=1, source_target_pairs={{0,4},{2,6},{4,0},{6,2},{8,12},{10,14},{12,8},{14,10},{16,20},{18,... | collective-permute-start | bytes 1572872 | tf_op jit(solution)/shard_map/ppermute | solution.py:678
  814.1 7.8 collective-permute-start.20
  816.0 7.5 collective-permute-start.18
  831.2 25.2 %collective-permute-start.21 = (f32[128,2048]{1,0:T(8,128)}, f32[128,2048]{1,0:T(8,128)}, u32[]{:S(2)}, u32[]{:S(2)}) collective-permute-start(f32[128,2048]{1,0:T(8,128)} %fusion.32), channel_id=1, source_target_pairs={{0,1},{1,0},{2,3},{3,2},{4,5},{5,4},{6,7},{7,6},{8,9},{9,8},{10,11... | collective-permute-start | bytes 3145736 | tf_op jit(solution)/shard_map/ppermute | solution.py:681
  833.5 13.6 %collective-permute-start.34 = (f32[11264]{0:T(1024)S(1)}, f32[11264]{0:T(1024)S(1)}, u32[]{:S(2)}, u32[]{:S(2)}) collective-permute-start(f32[11264]{0:T(1024)S(1)} %add.459), channel_id=1, source_target_pairs={{0,24},{2,26},{4,28},{6,30},{8,0},{10,2},{12,4},{14,6},{16,8},{18,... | collective-permute-start | bytes 135176 | tf_op jit(solution)/shard_map/ppermute | solution.py:684
  835.4 11.8 %collective-permute-start.33 = (f32[11264]{0:T(1024)S(1)}, f32[11264]{0:T(1024)S(1)}, u32[]{:S(2)}, u32[]{:S(2)}) collective-permute-start(f32[11264]{0:T(1024)S(1)} %add.459), channel_id=1, source_target_pairs={{0,16},{2,18},{4,20},{6,22},{8,24},{10,26},{12,28},{14,30},{16,0},... | collective-permute-start | bytes 135176 | tf_op jit(solution)/shard_map/ppermute | solution.py:684
  835.4 11.8 %collective-permute-start.32 = (f32[11264]{0:T(1024)S(1)}, f32[11264]{0:T(1024)S(1)}, u32[]{:S(2)}, u32[]{:S(2)}) collective-permute-start(f32[11264]{0:T(1024)S(1)} %add.459), channel_id=1, source_target_pairs={{0,8},{2,10},{4,12},{6,14},{8,16},{10,18},{12,20},{14,22},{16,24},... | collective-permute-start | bytes 135176 | tf_op jit(solution)/shard_map/ppermute | solution.py:684
  (62 other events, 418.6 us)

commit v3 on v2

--- a/solution.py
+++ b/solution.py
@@ -70,17 +70,13 @@
     return (seg_col == seg_row) & (cols <= rows)
 
 
-def attend_back_kernel(qkv_ref, do_ref, cos_ref, low_ref, upp_ref, col_ref, row_ref, dp_ref, sum_ref):
-    size, wide = do_ref.shape
-    query, key, value = qkv_ref[:, :wide], qkv_ref[:, wide : 2 * wide], qkv_ref[:, 2 * wide :]
-    grad = do_ref[...]
-    allowed = mask_of(col_ref[...], row_ref[...], size)
-    head_of = lax.broadcasted_iota(jnp.int32, (size, wide), 1) // HD
+def attend_back_values(query, key, value, grad, allowed, tables):
+    head_of = lax.broadcasted_iota(jnp.int32, query.shape, 1) // HD
     zero = jnp.zeros_like(query)
-    dq = jnp.zeros((size, wide), F32)
-    dk = jnp.zeros((size, wide), F32)
-    dv = jnp.zeros((size, wide), F32)
-    for head in range(wide // HD):
+    dq = jnp.zeros(query.shape, F32)
+    dk = jnp.zeros(query.shape, F32)
+    dv = jnp.zeros(query.shape, F32)
+    for head in range(query.shape[1] // HD):
         mine = head_of == head
         query_h = jnp.where(mine, query, zero)
         grad_h = jnp.where(mine, grad, zero)
@@ -94,49 +90,9 @@
         dscore = (prob * (dprob - delta)).astype(BF16)
         dq = jnp.where(mine, dot(dscore, key, 1, 0), dq)
         dk = dk + dot(dscore, query_h, 0, 0)
-    cos_t, low_t, upp_t = cos_ref[...], low_ref[...], upp_ref[...]
-    dq = spin_back(dq * HD ** (-0.5), cos_t, low_t, upp_t).astype(BF16)
-    dk = spin_back(dk * HD ** (-0.5), cos_t, low_t, upp_t).astype(BF16)
-    dv = dv.astype(BF16)
-    dp_ref[:, :wide] = dq
-    dp_ref[:, wide : 2 * wide] = dk
-    dp_ref[:, 2 * wide :] = dv
-    for part, grad_p in enumerate((dq, dk, dv)):
-        sum_ref[0, :, part * wide : (part + 1) * wide] = jnp.sum(
-            grad_p.astype(F32), axis=0, keepdims=True
-        )
-
-
-def row_blocks(size, wide):
-    return pl.BlockSpec((size, wide), lambda i: (i, 0))
-
-
-def attend_back(qkv, grad, tables, seg_col, seg_row, seqs, size, wide):
-    return pl.pallas_call(
-        attend_back_kernel,
-        grid=(seqs,),
-        in_specs=[
-            row_blocks(size, 3 * wide),
-            row_blocks(size, wide),
-            row_blocks(size, wide),
-            row_blocks(size, wide),
-            row_blocks(size, wide),
-            row_blocks(size, 1),
-            pl.BlockSpec((None, 1, size), lambda i: (i, 0, 0)),
-        ],
-        out_specs=[
-            row_blocks(size, 3 * wide),
-            pl.BlockSpec((1, 1, 3 * wide), lambda i: (i, 0, 0)),
-        ],
-        out_shape=[
-            jax.ShapeDtypeStruct((seqs * size, 3 * wide), BF16),
-            jax.ShapeDtypeStruct((seqs, 1, 3 * wide), F32),
-        ],
-        cost_estimate=pl.CostEstimate(
-            flops=seqs * 20 * size * size * wide, bytes_accessed=seqs * size * wide * 32, transcendentals=seqs * size * size * 4
-        ),
-        name="attend_back",
-    )(qkv, grad, *tables, seg_col, seg_row)
+    dq = spin_back(dq * HD ** (-0.5), *tables).astype(BF16)
+    dk = spin_back(dk * HD ** (-0.5), *tables).astype(BF16)
+    return dq, dk, dv.astype(BF16)
 
 
 class Place:
@@ -267,70 +223,83 @@
 
 
 class GroupSum:
-    def __init__(self, place, to_core, from_core, here, low, parts, core_sem, part_sem):
+    def __init__(self, place, to_core, from_core, low, own, parts, core_sem, part_sem, free_sem=None):
         self.place = place
-        self.to_core, self.from_core, self.here, self.low, self.parts = to_core, from_core, here, low, parts
-        self.core_sem, self.part_sem = core_sem, part_sem
-
-    def core_copy(self, x):
+        self.to_core, self.from_core, self.low, self.own, self.parts = to_core, from_core, low, own, parts
+        self.core_sem, self.part_sem, self.free_sem = core_sem, part_sem, free_sem
+
+    def core_copy(self, i):
         p = self.place
         return remote(
-            self.to_core.at[x], self.from_core.at[x], self.core_sem.at[0, x], self.core_sem.at[1, x], p.core_peer, p.t
+            self.to_core.at[i], self.from_core.at[i], self.core_sem.at[0, i], self.core_sem.at[1, i], p.core_peer, p.t
         )
 
     def part_copy(self, k):
         p = self.place
         half = self.parts.shape[1]
-        dp, t, x = p.group(k)
-        block = self.low.at[x, pl.ds(pl.multiple_of(t * half, half), half)]
+        dp, t, _ = p.group(k)
+        block = self.low.at[0 if k >= 2 else 1, pl.ds(pl.multiple_of(t * half, half), half)]
         return remote(block, self.parts.at[k - 1], self.part_sem.at[0, k], self.part_sem.at[1, k], dp, t)
 
-    def run(self, product):
-        p = self.place
-        size, step = self.here.shape[1], min(512, D)
-        for x in range(2):
+    def start(self, product):
+        p = self.place
+        step = min(512, D)
+        other = [(p.x + 1) % 2, p.x]
+        for i in range(2):
 
             @pl.loop(0, D // step)
             def _(n):
                 at = pl.ds(pl.multiple_of(n * step, step), step)
-                self.to_core[x, :, at] = product(x * 2 + 1 - p.c, n, step).astype(BF16)
-
-            self.core_copy(x).start()
-        for x in range(2):
+                self.to_core[i, :, at] = product(other[i] * 2 + 1 - p.c, n, step).astype(BF16)
+
+            self.core_copy(i).start()
+        for i in range(2):
+            self.core_copy(i).wait_recv()
 
             @pl.loop(0, D // step)
             def _(n):
                 at = pl.ds(pl.multiple_of(n * step, step), step)
-                self.here[x, :, at] = product(x * 2 + p.c, n, step)
-
-        for x in range(2):
-            self.core_copy(x).wait_recv()
-
-            @pl.loop(0, size // 32)
-            def _(i):
-                at = pl.ds(pl.multiple_of(i * 32, 32), 32)
-                total = self.here[x, at, :] + self.from_core[x, at, :].astype(F32)
-                self.here[x, at, :] = total
-                self.low[x, at, :] = total.astype(BF16)
-
-        for k in (3, 2, 1):
-            self.part_copy(k).start()
+                total = product(other[i] * 2 + p.c, n, step) + self.from_core[i, :, at].astype(F32)
+                self.low[i, :, at] = total.astype(BF16)
+                if i == 1:
+                    self.own[:, at] = total
+
+            for k in (3, 2) if i == 0 else (1,):
+                self.part_copy(k).start()
+
+    def arrive(self):
         for k in (3, 2, 1):
             self.part_copy(k).wait_recv()
 
     def total(self, at, rows):
         p = self.place
         half = self.parts.shape[1]
-        value = self.here[p.x, pl.ds(pl.multiple_of(p.t * half + at, 32), rows), :]
+        value = self.own[pl.ds(pl.multiple_of(p.t * half + at, 32), rows), :]
         for k in range(3):
             value = value + self.parts[k, pl.ds(pl.multiple_of(at, 32), rows), :].astype(F32)
         return value
 
     def finish(self):
-        for x in range(2):
-            self.core_copy(x).wait_send()
+        for i in range(2):
+            self.core_copy(i).wait_send()
         for k in (1, 2, 3):
             self.part_copy(k).wait_send()
+
+    def release(self):
+        p = self.place
+        pl.semaphore_signal(
+            self.free_sem.at[0], inc=1, device_id=(p.core_peer, p.t), device_id_type=pl.DeviceIdType.MESH
+        )
+        for k in (1, 2, 3):
+            dp, t, _ = p.group(k)
+            pl.semaphore_signal(
+                self.free_sem.at[k], inc=1, device_id=(dp, t), device_id_type=pl.DeviceIdType.MESH
+            )
+
+    def acquire(self):
+        self.finish()
+        for k in range(4):
+            pl.semaphore_wait(self.free_sem.at[k], 1)
 
 
 class GroupGather:
@@ -446,8 +415,8 @@
     count,
     small_src, aux_src, row_src, tok_src, cot_src, wq_src, wo_src, wg_src, wd_src,
     wq_out, wo_out, wg_out, wd_out, h1_out, h2_out, cot_out, aux_out, row_out,
-    qkv, att, hid, slope, gain, resid, norms,
-    wq, wo, wg, wd, tok, h1, h2, small, aux_all, row_all, to_core, from_core, here, low, parts,
+    qkv, att, hid, slopes, resid, norms,
+    wq, wo, wg, wd, tok, h1, h2, small, aux_all, row_all, to_core, from_core, low, own, parts,
     w_send, w_recv, small_sem, aux_sem, row_sem, tok_sem, cot_sem, core_sem, part_sem, part2_sem, core2_sem, out_sem,
 ):
     p = Place(count)
@@ -535,13 +504,14 @@
         att[at, :] = attend_values(query, key, value, allowed).astype(BF16)
 
     gathers[1].arrive()
-    sums = GroupSum(p, to_core, from_core, here, low, parts, core_sem, part_sem)
+    sums = GroupSum(p, to_core, from_core, low, own, parts, core_sem, part_sem)
 
     def attention_product(s, n, step):
         at = pl.ds(pl.multiple_of(s * size, size), size)
         return dot(att[at, :], wo[pl.ds(pl.multiple_of(n * step, step), step), :], 1, 1)
 
-    sums.run(attention_product)
+    sums.start(attention_product)
+    sums.arrive()
 
     @pl.loop(0, half // 32)
     def _(i):
@@ -562,6 +532,7 @@
     gathers[2].arrive()
 
     full = hid.shape[1] - 128
+    slope, gain = slopes.at[: TP * size], slopes.at[TP * size :]
 
     @pl.loop(0, TP)
     def _(s):
@@ -600,7 +571,7 @@
 def forward(count, small, aux, row, tokens, cot, wq, wo, wg, wd):
     size = tokens.shape[0]
     group = TP * size
-    wide, hidden = wo.shape[2], wd.shape[2]
+    wide, pad = wo.shape[2], wd.shape[2]
     any_spec = pl.BlockSpec(memory_space=pl.ANY)
     vmem = pl.BlockSpec(memory_space=pltpu.VMEM)
     dma = pltpu.SemaphoreType.DMA
@@ -608,12 +579,11 @@
     def out(*shape, dtype=BF16):
         return jax.ShapeDtypeStruct(shape, dtype)
 
-    pad = -(-hidden // 128) * 128
     weights = [wq, wo, wg, wd]
     return pl.pallas_call(
         functools.partial(forward_kernel, count),
         in_specs=[vmem, vmem, vmem, vmem] + [any_spec] * 5,
-        out_specs=[any_spec] * 7 + [vmem] * 9,
+        out_specs=[any_spec] * 7 + [vmem] * 8,
         out_shape=[out(D, w.shape[2]) for w in weights]
         + [
             out(group, D),
@@ -624,8 +594,7 @@
             out(group, 3 * wide),
             out(group, wide),
             out(group, pad),
-            out(group, pad),
-            out(group, pad),
+            out(2 * group, pad),
             out(size // 2, D, dtype=F32),
             out(16, max(D, 128 * (small.shape[0] - 16)), dtype=F32),
         ],
@@ -639,8 +608,8 @@
             pltpu.VMEM((TP, 8, size), F32),
             pltpu.VMEM((2, size, D), BF16),
             pltpu.VMEM((2, size, D), BF16),
-            pltpu.VMEM((2, size, D), F32),
             pltpu.VMEM((2, size, D), BF16),
+            pltpu.VMEM((size, D), F32),
             pltpu.VMEM((3, size // 2, D), BF16),
             dma((4, count)),
             dma((4, 2)),
@@ -663,126 +632,404 @@
     )(small, aux, row, tokens, cot, *weights)
 
 
-class Links:
-    def __init__(self, count):
-        self.count = count
-        self.lines = count // TP
-        self.place = lax.axis_index("dp")
-        self.tensor = lax.axis_index("tensor")
-        self.u = self.place // TP
-        self.j = self.place % TP
-        self.x = self.j // 2
-        self.c = self.j % 2
-
-    def flip(self, values, bit):
-        return lax.ppermute(values, "dp", [(i, i ^ bit) for i in range(self.count)])
-
-    def swap(self, values):
-        return lax.ppermute(values, "tensor", [(0, 1), (1, 0)])
-
-    def along(self, values, pairs):
-        return lax.ppermute(
-            values, "dp", [(a * TP + r, b * TP + r) for a, b in pairs for r in range(TP)]
+class GradScatter:
+    def __init__(self, place, index, grad, out, far, send_sem, recv_sem, far_sem):
+        self.place, self.grad, self.out, self.far = place, grad, out, far
+        self.send_sem, self.recv_sem, self.far_sem = send_sem.at[index], recv_sem.at[index], far_sem.at[index]
+        self.rows = out.shape[2]
+
+    def copy(self, dest, u, j):
+        p = self.place
+        block = self.grad.at[pl.ds(dest * self.rows, self.rows)]
+        far = 0
+        if p.lines == 4:
+            far = (((p.u == 0) & (u == 2)) | ((p.u == 3) & (u == 1))).astype(jnp.int32)
+        return remote(block, self.out.at[p.u, p.j], self.send_sem.at[dest], self.recv_sem.at[far], dest, p.t)
+
+    def outer(self):
+        p = self.place
+        size = TP * self.rows
+        chunk = self.grad.at[pl.ds(jnp.where(p.u == 0, 3, 0) * size, size)]
+        dest = p.me + jnp.where(p.u == 0, TP, -TP)
+        return remote(chunk, self.far, self.send_sem.at[p.me], self.far_sem, dest, p.t)
+
+    def ends(self):
+        return (self.place.u == 0) | (self.place.u == 3)
+
+    def later(self, u):
+        p = self.place
+        return ((p.u == 1) & (u == 3)) | ((p.u == 2) & (u == 0))
+
+    def start(self):
+        p = self.place
+        if p.lines == 4:
+            pl.when(self.ends())(lambda: self.outer().start())
+        own = self.grad.at[pl.ds(p.me * self.rows, self.rows)]
+
+        def act(dest, u, j):
+            if p.lines == 4:
+                pl.when((jnp.abs(p.u - u) < 3) & ~self.later(u))(lambda: self.copy(dest, u, j).start())
+            else:
+                self.copy(dest, u, j).start()
+
+        each_dest(p, act)
+        pltpu.make_async_copy(own, self.out.at[p.u, p.j], self.recv_sem.at[0]).start()
+
+    def combine(self):
+        p = self.place
+        if p.lines != 4:
+            return
+        size = TP * self.rows
+
+        @pl.when(~self.ends())
+        def _():
+            u = jnp.where(p.u == 1, 3, 0)
+            wait_bytes(self.far, self.far_sem)
+
+            @pl.loop(0, size // 32)
+            def _(i):
+                here = pl.ds(pl.multiple_of(i * 32, 32), 32)
+                at = pl.ds(pl.multiple_of(u * size + i * 32, 32), 32)
+                total = self.grad[at, :].astype(F32) + self.far[here, :].astype(F32)
+                self.grad[at, :] = total.astype(BF16)
+
+            @pl.loop(0, TP)
+            def _(q):
+                j = (p.j + q) % TP
+                self.copy(u * TP + j, u, j).start()
+
+    def arrive(self):
+        p = self.place
+        if p.lines == 4:
+            wait_bytes(self.out.at[pl.ds(0, 3)], self.recv_sem.at[0])
+            pl.when(~self.ends())(lambda: wait_bytes(self.out.at[0], self.recv_sem.at[1]))
+        else:
+            wait_bytes(self.out, self.recv_sem.at[0])
+
+    def finish(self):
+        p = self.place
+
+        def act(dest, u, j):
+            if p.lines == 4:
+                pl.when(jnp.abs(p.u - u) < 3)(lambda: self.copy(dest, u, j).wait_send())
+            else:
+                self.copy(dest, u, j).wait_send()
+
+        each_dest(p, act)
+        if p.lines == 4:
+            pl.when(self.ends())(lambda: self.outer().wait_send())
+
+
+def norm_stats(values):
+    centre = values - jnp.mean(values, axis=-1, keepdims=True)
+    inverse = lax.rsqrt(jnp.mean(centre * centre, axis=-1, keepdims=True) + 1e-05)
+    return centre * inverse, inverse
+
+
+def backward_kernel(
+    count,
+    aux, row, tok, resid, norms, hid_in, cot_in, slopes_in, wd_in, wg_in, wo_in, wq_in, h2_in, h1_in, qkv_in, att_in,
+    rs_q, rs_o, rs_g, rs_d, block_out, input_out, norm_out, bias_out,
+    wd, wg, wo, cot, hid, slopes, hh, qkv, att, dgate, gd, gg, go, far_d, far_g, far_o, far_q,
+    to_core, from_core, low, own, parts, grad, block, gains, biases, small_all, bias_all, small_t,
+    load_sem, rs_send, rs_recv, rs_far, core_sem, part_sem, free_sem, part2_sem, core2_sem,
+    swap_sem, small_sem, bias_sem, rank_sem, t_sem,
+):
+    p = Place(count)
+    size = tok.shape[0]
+    half = size // 2
+    group = TP * size
+    wide = att.shape[1]
+    full = hid.shape[1] - 128
+    loads = {}
+    for i, (name, src, dst) in enumerate(
+        (
+            ("wd", wd_in, wd), ("cot", cot_in, cot), ("slopes", slopes_in, slopes.at[: 2 * group, : hid.shape[1]]),
+            ("hid", hid_in, hid), ("wg", wg_in, wg), ("h2", h2_in, hh), ("wo", wo_in, wo), ("att", att_in, att),
+            ("qkv", qkv_in, qkv),
         )
-
-    def pair(self, mine, other, second):
-        return jnp.stack([jnp.where(second, other, mine), jnp.where(second, mine, other)])
-
-    def group_gather(self, values):
-        two = self.pair(values, self.flip(values, 1), self.c == 1)
-        four = self.pair(two, self.flip(two, 2), self.x == 1)
-        return four.reshape((TP,) + values.shape)
-
-    def group_swap(self, blocks):
-        def block(k):
-            return lax.dynamic_index_in_dim(blocks, self.j ^ k, 0, False)
-
-        got = [block(0)] + [self.flip(block(k), k) for k in range(1, TP)]
-        odd = self.c == 1
-        got = [jnp.where(odd, got[k ^ 1], got[k]) for k in range(TP)]
-        odd = self.x == 1
-        return jnp.stack([jnp.where(odd, got[k ^ 2], got[k]) for k in range(TP)])
-
-    def line_pieces(self, values):
-        n = self.lines
-        if n != 4:
-            return [
-                self.along(values, [(i, (i + k) % n) for i in range(n)]) for k in range(1, n)
-            ]
-        up = self.along(values, [(0, 1), (1, 2), (2, 3)])
-        down = self.along(values, [(3, 2), (2, 1), (1, 0)])
-        two = self.along(values, [(0, 2), (1, 3), (2, 0), (3, 1)])
-        far = self.along(two, [(2, 3), (1, 0)])
-        return [jnp.where(self.u == 0, far, up), two, jnp.where(self.u == 3, far, down)]
-
-    def line_gather(self, values):
-        out = jnp.zeros((self.lines,) + values.shape, values.dtype)
-        for k, piece in enumerate([values] + self.line_pieces(values)):
-            out = lax.dynamic_update_index_in_dim(out, piece, (self.u - k) % self.lines, 0)
-        return out
-
-    def line_scatter_sum(self, blocks):
-        n = self.lines
-
-        def block(k):
-            return lax.dynamic_index_in_dim(blocks, (self.u + k) % n, 0, False)
-
-        total = block(0).astype(F32)
-        if n != 4:
-            for k in range(1, n):
-                total = total + self.along(
-                    block(k), [(i, (i + k) % n) for i in range(n)]
-                ).astype(F32)
-            return total
-        outer = jnp.where(self.u == 0, blocks[3], blocks[0])
-        far = self.along(outer, [(0, 1), (3, 2)])
-        up = self.along(block(1), [(0, 1), (1, 2), (2, 3)])
-        down = self.along(block(3), [(3, 2), (2, 1), (1, 0)])
-        two = (block(2).astype(F32) + far.astype(F32)).astype(BF16)
-        two = self.along(two, [(0, 2), (1, 3), (2, 0), (3, 1)])
-        return total + up.astype(F32) + down.astype(F32) + two.astype(F32)
-
-    def line_sum(self, values):
-        n = self.lines
-        total = values
-        for k in range(1, n):
-            total = total + self.along(values, [(i, (i + k) % n) for i in range(n)])
-        return total
-
-    def scatter_sum(self, partial):
-        half = partial.shape[-1] // 2
-
-        def take(values, axis, index):
-            return lax.dynamic_index_in_dim(values, index, axis, False)
-
-        other = self.flip(take(partial, 1, 1 - self.c).astype(BF16), 1)
-        here = take(partial, 1, self.c) + other.astype(F32)
-        left, right = here[..., :half], here[..., half:]
-        left = take(left, 0, self.x) + self.flip(take(left, 0, 1 - self.x).astype(BF16), 2).astype(F32)
-        right = take(right, 1, self.tensor) + self.swap(
-            take(right, 1, 1 - self.tensor).astype(BF16)
-        ).astype(F32)
-        left = take(left, 0, self.tensor) + self.swap(
-            take(left, 0, 1 - self.tensor).astype(BF16)
-        ).astype(F32)
-        right = take(right, 0, self.x) + self.flip(take(right, 0, 1 - self.x).astype(BF16), 2).astype(F32)
-        return jnp.concatenate([left, right], axis=-1)
-
-    def gather(self, values):
-        half = values.shape[-1] // 2
-        left, right = values[:, :half], values[:, half:]
-        left = self.pair(left, self.swap(left), self.tensor == 1)
-        left = self.pair(left, self.flip(left, 2), self.x == 1)
-        right = self.pair(right, self.flip(right, 2), self.x == 1)
-        right_other = self.swap(right)
-        second = self.tensor == 1
-        right = jnp.stack(
-            [jnp.where(second, right_other, right), jnp.where(second, right, right_other)], axis=1
+    ):
+        loads[name] = pltpu.make_async_copy(src, dst, load_sem.at[i])
+        loads[name].start()
+    greet(p)
+    gq = slopes.at[:D, : 3 * wide]
+    wq = wg.at[:, : 3 * wide]
+    scatter_q, scatter_o, scatter_g, scatter_d = [
+        GradScatter(p, i, g, out, far, rs_send, rs_recv, rs_far)
+        for i, (g, out, far) in enumerate(
+            ((gq, rs_q, far_q), (go, rs_o, far_o), (gg, rs_g, far_g), (gd, rs_d, far_d))
         )
-        here = jnp.concatenate([left, right], axis=-1)
-        there = self.flip(here, 1)
-        second = self.c == 1
-        return jnp.stack([jnp.where(second, there, here), jnp.where(second, here, there)], axis=1)
+    ]
+    sums = GroupSum(p, to_core, from_core, low, own, parts, core_sem, part_sem, free_sem)
+
+    def rows_of(s):
+        return pl.ds(pl.multiple_of(s * size, size), size)
+
+    for name in ("wd", "cot", "slopes"):
+        loads[name].wait()
+
+    @pl.loop(0, TP)
+    def _(s):
+        at = rows_of(s)
+        dhid = dot(cot[at, :], wd[...], 1, 0)
+        slope = dhid * slopes[at, : hid.shape[1]].astype(F32)
+        gain = dhid * slopes[pl.ds(pl.multiple_of(group + s * size, size), size), : hid.shape[1]].astype(F32)
+        dgate[at, :full] = slope[:, :full].astype(BF16)
+        dgate[at, full : 2 * full] = gain[:, :full].astype(BF16)
+        last = slope[:, full:] + pltpu.roll(gain[:, full:], 64, 1)
+        dgate[at, 2 * full :] = last.astype(BF16)
+
+    step = min(256, D)
+
+    def weight_grad(left, right, out):
+        @pl.loop(0, D // step)
+        def _(n):
+            at = pl.ds(pl.multiple_of(n * step, step), step)
+            out[at, :] = dot(left[:, at], right[...], 0, 0).astype(BF16)
+
+    loads["hid"].wait()
+    weight_grad(cot, hid, gd)
+    scatter_d.start()
+
+    loads["wg"].wait()
+    sums.start(
+        lambda s, n, step: dot(dgate[rows_of(s), :], wg[pl.ds(pl.multiple_of(n * step, step), step), :], 1, 1)
+    )
+    load_wq = pltpu.make_async_copy(wq_in, wq, load_sem.at[9])
+    load_wq.start()
+    loads["h2"].wait()
+    weight_grad(hh, dgate, gg)
+    scatter_g.start()
+    load_h1 = pltpu.make_async_copy(h1_in, hh, load_sem.at[10])
+    load_h1.start()
+    scatter_d.combine()
+    sums.arrive()
+
+    gains[...] = jnp.zeros_like(gains)
+
+    @pl.loop(0, half // 32)
+    def _(i):
+        at = pl.multiple_of(i * 32, 32)
+        scaled, inverse = norm_stats(resid[pl.ds(at, 32), :])
+        grad_in = sums.total(at, 32)
+        part, gain, shift = norm_back(grad_in, scaled, inverse, norms[2:3, :D])
+        gains[2:3, :] += gain[None]
+        gains[3:4, :] += shift[None]
+        mine = pl.ds(pl.multiple_of((p.j * 2 + p.t) * half + at, 32), 32)
+        total = cot[mine, :].astype(F32) + part
+        grad[pl.ds(at, 32), :] = total
+        cot[mine, :] = total.astype(BF16)
+
+    sums.release()
+    spread = GroupGather(p, cot, size, part2_sem, core2_sem)
+    spread.run()
+    scatter_g.combine()
+
+    for name in ("wo", "att", "qkv"):
+        loads[name].wait()
+    biases[...] = jnp.zeros_like(biases)
+
+    @pl.loop(0, TP)
+    def _(s):
+        at = rows_of(s)
+        grad_out = dot(cot[at, :], wo[...], 1, 0).astype(BF16)
+        allowed = mask_of(aux[s][:, ROT : ROT + 1], row[s, 0:1, :], size)
+        tables = tables_of(aux[s], wide)
+        three = attend_back_values(
+            qkv[at, :wide], qkv[at, wide : 2 * wide], qkv[at, 2 * wide :], grad_out, allowed, tables
+        )
+        for k, value in enumerate(three):
+            lanes = slice(k * wide, (k + 1) * wide)
+            qkv[at, lanes] = value
+            biases[0:1, lanes] += jnp.sum(value.astype(F32), axis=0, keepdims=True)
+
+    load_h1.wait()
+    weight_grad(hh, qkv, gq)
+    scatter_q.start()
+    weight_grad(cot, att, go)
+    scatter_o.start()
+
+    bias_all[p.u] = biases[...]
+
+    def bias_copy(k):
+        u = (p.u + k) % p.lines
+        return remote(biases, bias_all.at[p.u], bias_sem.at[k], bias_sem.at[p.lines + k], u * TP + p.j, p.t)
+
+    for k in range(1, p.lines):
+        bias_copy(k).start()
+
+    load_wq.wait()
+    sums.acquire()
+    sums.start(
+        lambda s, n, step: dot(qkv[rows_of(s), :], wq[pl.ds(pl.multiple_of(n * step, step), step), :], 1, 1)
+    )
+    scatter_q.combine()
+    scatter_o.combine()
+    sums.arrive()
+
+    @pl.loop(0, half // 32)
+    def _(i):
+        at = pl.multiple_of(i * 32, 32)
+        values = tok[pl.ds(pl.multiple_of(p.t * half + at, 32), 32), :].astype(F32)
+        scaled, inverse = norm_stats(values)
+        part, gain, shift = norm_back(sums.total(at, 32), scaled, inverse, norms[0:1, :D])
+        gains[0:1, :] += gain[None]
+        gains[1:2, :] += shift[None]
+        grad[pl.ds(at, 32), :] += part
+
+    sums.release()
+    mine = pl.ds(pl.multiple_of(p.t * half, half), half)
+
+    def give(index, value, out):
+        here = pltpu.make_async_copy(value, out.at[mine], swap_sem.at[index, 0])
+        there = remote(value, out.at[mine], swap_sem.at[index, 1], swap_sem.at[index, 2], p.me, 1 - p.t)
+        here.start()
+        there.start()
+        return here, there
+
+    gives = [*give(0, grad, input_out)]
+
+    rows = rs_q.shape[2]
+
+    def tile_of(d):
+        return pl.ds(pl.multiple_of(d * rows // 128 * 128, 128), 128)
+
+    def small_copy(dest):
+        return remote(gains.at[:, tile_of(dest)], small_all.at[p.me], small_sem.at[dest], small_sem.at[count], dest, p.t)
+
+    own_small = pltpu.make_async_copy(gains.at[:, tile_of(p.me)], small_all.at[p.me], small_sem.at[count])
+    own_small.start()
+    each_dest(p, lambda dest, u, j: small_copy(dest).start())
+
+    for k in range(1, p.lines):
+        bias_copy(k).wait_recv()
+    total = bias_all[0]
+    for k in range(1, p.lines):
+        total = total + bias_all[k]
+    bias_out[p.j] = total
+
+    def rank_copy(q):
+        j = (p.j + q) % TP
+        return remote(bias_out.at[p.j], bias_out.at[p.j], rank_sem.at[q], rank_sem.at[TP + q], p.u * TP + j, p.t)
+
+    for q in range(1, TP):
+        rank_copy(q).start()
+
+    sums.acquire()
+    sums.start(lambda s, n, step: dot(hid[rows_of(s), :], wd[pl.ds(pl.multiple_of(n * step, step), step), :], 1, 1))
+    sums.arrive()
+
+    @pl.loop(0, half // 32)
+    def _(i):
+        at = pl.multiple_of(i * 32, 32)
+        block[pl.ds(at, 32), :] = resid[pl.ds(at, 32), :] + sums.total(at, 32)
+
+    gives += give(1, block, block_out)
+
+    wait_bytes(small_all, small_sem.at[count])
+    total = small_all[0]
+    for d in range(1, count):
+        total = total + small_all[d]
+    small_t[0] = total
+    swap = remote(small_t.at[0], small_t.at[1], t_sem.at[0], t_sem.at[1], p.me, 1 - p.t)
+    swap.start()
+    swap.wait()
+    norm_out[...] = small_t[0] + small_t[1]
+    for q in range(1, TP):
+        rank_copy(q).wait()
+    for k in range(1, p.lines):
+        bias_copy(k).wait_send()
+    each_dest(p, lambda dest, u, j: small_copy(dest).wait_send())
+    for copy in gives:
+        copy.wait()
+    sums.finish()
+    spread.finish()
+    for scatter in (scatter_d, scatter_g, scatter_q, scatter_o):
+        scatter.arrive()
+        scatter.finish()
+
+
+def backward(count, aux, row, tok, resid, norms, hid, cot, slopes, wd, wg, wo, wq, h2, h1, qkv, att):
+    size = tok.shape[0]
+    half = size // 2
+    group = TP * size
+    wide, pad = wo.shape[1], wd.shape[1]
+    lines, rows = count // TP, D // count
+    any_spec = pl.BlockSpec(memory_space=pl.ANY)
+    vmem = pl.BlockSpec(memory_space=pltpu.VMEM)
+    dma = pltpu.SemaphoreType.DMA
+
+    def out(*shape, dtype=BF16):
+        return jax.ShapeDtypeStruct(shape, dtype)
+
+    def far(width):
+        return pltpu.VMEM((TP * rows if lines == 4 else 16, width), BF16)
+
+    return pl.pallas_call(
+        functools.partial(backward_kernel, count),
+        in_specs=[vmem] * 5 + [any_spec] * 11,
+        out_specs=[any_spec] * 6 + [vmem] * 2,
+        out_shape=[
+            out(lines, TP, rows, 3 * wide),
+            out(lines, TP, rows, wide),
+            out(lines, TP, rows, wg.shape[1]),
+            out(lines, TP, rows, pad),
+            out(size, D, dtype=F32),
+            out(size, D, dtype=F32),
+            out(8, 128, dtype=F32),
+            out(TP, 8, 3 * wide, dtype=F32),
+        ],
+        scratch_shapes=[
+            pltpu.VMEM((D, pad), BF16),
+            pltpu.VMEM((D, wg.shape[1]), BF16),
+            pltpu.VMEM((D, wide), BF16),
+            pltpu.VMEM((group, D), BF16),
+            pltpu.VMEM((group, pad), BF16),
+            pltpu.VMEM((max(2 * group, D), max(pad, 3 * wide)), BF16),
+            pltpu.VMEM((group, D), BF16),
+            pltpu.VMEM((group, 3 * wide), BF16),
+            pltpu.VMEM((group, wide), BF16),
+            pltpu.VMEM((group, wg.shape[1]), BF16),
+            pltpu.VMEM((D, pad), BF16),
+            pltpu.VMEM((D, wg.shape[1]), BF16),
+            pltpu.VMEM((D, wide), BF16),
+            far(pad),
+            far(wg.shape[1]),
+            far(wide),
+            far(3 * wide),
+            pltpu.VMEM((2, size, D), BF16),
+            pltpu.VMEM((2, size, D), BF16),
+            pltpu.VMEM((2, size, D), BF16),
+            pltpu.VMEM((size, D), F32),
+            pltpu.VMEM((3, half, D), BF16),
+            pltpu.VMEM((half, D), F32),
+            pltpu.VMEM((half, D), F32),
+            pltpu.VMEM((8, D), F32),
+            pltpu.VMEM((8, 3 * wide), F32),
+            pltpu.VMEM((count, 8, 128), F32),
+            pltpu.VMEM((lines, 8, 3 * wide), F32),
+            pltpu.VMEM((2, 8, 128), F32),
+            dma((11,)),
+            dma((4, count)),
+            dma((4, 2)),
+            dma((4,)),
+            dma((2, 2)),
+            dma((2, 4)),
+            pltpu.SemaphoreType.REGULAR((4,)),
+            dma((2, 4)),
+            dma((2, 4)),
+            dma((2, 3)),
+            dma((count + 1,)),
+            dma((2 * lines,)),
+            dma((2 * TP,)),
+            dma((2,)),
+        ],
+        compiler_params=pltpu.CompilerParams(
+            collective_id=1, has_side_effects=True, vmem_limit_bytes=62 * 1024 * 1024
+        ),
+        cost_estimate=pl.CostEstimate(flops=27 * 10**9, bytes_accessed=120 * 10**6, transcendentals=10**7),
+        name="backward",
+    )(aux, row, tok, resid, norms, hid, cot, slopes, wd, wg, wo, wq, h2, h1, qkv, att)
 
 
 def per_device(
@@ -809,37 +1056,32 @@
     norm_first,
     norm_second,
 ):
-    links = Links(count)
+    place = lax.axis_index("dp")
     rows = norm_params.shape[1]
     seq_len = tokens_in.shape[1]
     head_local = qkv_weight.shape[2]
     hidden_local = gating_weight.shape[2]
     wide = head_local // TP
     hid = hidden_local // TP
-    half_seq = seq_len // 2
-    group_rows = TP * seq_len
+    full = hid // 128 * 128
 
     def cut(shard):
         return shard.astype(BF16).transpose(1, 0, 2)
 
-    full = hid // 128 * 128
     gates = gating_weight.astype(BF16).reshape(rows, 2, TP, hid)
     gates = jnp.concatenate(
         [gates[:, 0, :, :full], gates[:, 1, :, :full], gates[:, 0, :, full:], gates[:, 1, :, full:]], axis=2
     )
+    downs = jnp.pad(down_weight.T.reshape(rows, TP, hid), ((0, 0), (0, 0), (0, -hid % 128)))
     weights = (
         cut(qkv_weight.reshape(rows, 3, TP, wide).transpose(0, 2, 1, 3).reshape(rows, TP, 3 * wide)),
         cut(out_weight.T.reshape(rows, TP, wide)),
         gates.transpose(1, 0, 2),
-        cut(down_weight.T.reshape(rows, TP, hid)),
+        cut(downs),
     )
     bias_here = qkv_bias.shape[1]
-    small_norm = lax.dynamic_update_slice(
-        jnp.zeros((16, 128), F32), norm_params, (0, (links.place * rows) % 128)
-    )
-    small_bias = lax.dynamic_update_slice(
-        jnp.zeros((3 * head_local,), F32), qkv_bias[0], (links.place * bias_here,)
-    )
+    small_norm = lax.dynamic_update_slice(jnp.zeros((16, 128), F32), norm_params, (0, (place * rows) % 128))
+    small_bias = lax.dynamic_update_slice(jnp.zeros((3 * head_local,), F32), qkv_bias[0], (place * bias_here,))
     small = jnp.concatenate([small_norm, small_bias.reshape(-1, 128)]).astype(BF16)
     segments = segment_ids[0]
     earlier = jnp.sum((segments[None, :] < segments[:, None]).astype(jnp.int32), axis=1)
@@ -850,99 +1092,36 @@
     aux = jnp.pad(aux, ((0, 0), (0, 128 - aux.shape[1])))
     row = jnp.broadcast_to(segments.astype(F32)[None], (8, seq_len))
 
-    (
-        qkv_matrix, out_matrix, gating_matrix, down_matrix, normed_one, normed_two, cotangent, aux_all, row_all,
-        qkv_rot, attended, hidden, slope, gain, residual, norm_rows,
-    ) = forward(count, small, aux, row, tokens_in[0], d_out[0], *weights)
-    norm_rows = norm_rows[:4, :D]
-    cotangent = cotangent.reshape(group_rows, D)
-    hidden, slope, gain = hidden[:, :hid], slope[:, :hid], gain[:, :hid]
-
-    def own_half(values):
-        return lax.dynamic_slice_in_dim(values, links.tensor * half_seq, half_seq, 0)
-
-    def to_parts(partial):
-        return partial.reshape(2, 2, 2, half_seq, D)
-
-    heads = wide // HD
-    cosine, sine_part = aux_all.reshape(group_rows, 128)[:, : ROT // 2], aux_all.reshape(group_rows, 128)[:, ROT // 2 : ROT]
-    zeros = jnp.zeros((group_rows, HD - ROT), F32)
-    tables = (
-        jnp.tile(jnp.concatenate([cosine, cosine, zeros + 1.0], axis=1), (1, heads)),
-        jnp.tile(jnp.concatenate([-sine_part, jnp.zeros_like(sine_part), zeros], axis=1), (1, heads)),
-        jnp.tile(jnp.concatenate([jnp.zeros_like(sine_part), sine_part, zeros], axis=1), (1, heads)),
+    wq, wo, wg, wd, h1, h2, cot, aux_all, row_all, qkv, att, hidden, slopes, resid, norms = forward(
+        count, small, aux, row, tokens_in[0], d_out[0], *weights
     )
-    seg_col = aux_all.reshape(group_rows, 128)[:, ROT : ROT + 1].astype(jnp.int32)
-    seg_row = row_all[:, 0:1, :].astype(jnp.int32)
-    tokens_own = own_half(tokens_in[0]).astype(F32)
-    _, scaled_two, inverse_two = layer_norm(residual, norm_rows[2], norm_rows[3])
-
-    grad_down = dot(cotangent, hidden, 0, 0).astype(BF16)
-    down_sum = links.line_scatter_sum(grad_down.reshape(links.lines, TP * rows, hid))
-    grad_hidden = dot(cotangent, down_matrix, 1, 0)
-    grad_gate = (grad_hidden * slope.astype(F32)).astype(BF16)
-    grad_up = (grad_hidden * gain.astype(F32)).astype(BF16)
-    grad_gated = jnp.concatenate(
-        [grad_gate[:, :full], grad_up[:, :full], grad_gate[:, full:], grad_up[:, full:]], axis=1
+    cot = cot.reshape(TP * seq_len, D)
+    rs_q, rs_o, rs_g, rs_d, block_out, input_grad, norm_sum, bias_sum = backward(
+        count, aux_all, row_all, tokens_in[0], resid, norms, hidden, cot, slopes, wd, wg, wo, wq, h2, h1, qkv, att
     )
-    normed_grad_two = links.scatter_sum(to_parts(dot(grad_gated, gating_matrix, 1, 1)))
-    grad_gating = dot(normed_two, grad_gated, 0, 0).astype(BF16)
-    gating_sum = links.line_scatter_sum(grad_gating.reshape(links.lines, TP * rows, 2 * hid))
-
-    residual_part, gain_two, shift_two = norm_back(
-        normed_grad_two, scaled_two, inverse_two, norm_rows[2]
-    )
-    residual_grad = own_half(d_out[0]).astype(F32) + residual_part
-    residual_low = links.gather(residual_grad.astype(BF16)).reshape(group_rows, D)
-    grad_attended = dot(residual_low, out_matrix, 1, 0).astype(BF16)
-    grad_out = dot(residual_low, attended, 0, 0).astype(BF16)
-    out_sum = links.line_scatter_sum(grad_out.reshape(links.lines, TP * rows, wide))
-
-    feedforward_term = links.scatter_sum(to_parts(dot(hidden, down_matrix, 1, 1)))
-    block_own = residual + feedforward_term
-    block_out = links.pair(block_own, links.swap(block_own), links.tensor == 1).reshape(seq_len, D)
-
-    grad_projected, bias_sums = attend_back(
-        qkv_rot, grad_attended, tables, seg_col, seg_row, TP, seq_len, wide
-    )
-    grad_qkv = dot(normed_one, grad_projected, 0, 0).astype(BF16)
-    qkv_sum = links.line_scatter_sum(grad_qkv.reshape(links.lines, TP * rows, 3 * wide))
-    normed_grad_one = links.scatter_sum(to_parts(dot(grad_projected, qkv_matrix, 1, 1)))
-    _, scaled_one, inverse_one = layer_norm(tokens_own, norm_rows[0], norm_rows[1])
-    input_part, gain_one, shift_one = norm_back(
-        normed_grad_one, scaled_one, inverse_one, norm_rows[0]
-    )
-    input_own = residual_grad + input_part
-    input_grad = links.pair(input_own, links.swap(input_own), links.tensor == 1).reshape(seq_len, D)
-
-    norm_small = jnp.concatenate([gain_one, shift_one, gain_two, shift_two])
-    norm_small = norm_small + links.swap(norm_small)
-    bias_small = jnp.sum(bias_sums, axis=0).reshape(3, 1, wide)
-    bias_small = jnp.where(
-        lax.broadcasted_iota(jnp.int32, (3, TP, wide), 1) == links.j, bias_small, 0.0
-    ).reshape(-1)
-    small_grad = jnp.concatenate([norm_small, bias_small])
-    small_grad = small_grad + links.flip(small_grad, 1)
-    small_grad = small_grad + links.flip(small_grad, 2)
-    small_grad = links.line_sum(small_grad)
-    norm_grad = lax.dynamic_slice_in_dim(small_grad[: 4 * D].reshape(4, D), links.place * rows, rows, 1)
-    bias_grad = lax.dynamic_slice_in_dim(
-        small_grad[4 * D :].reshape(1, -1), links.place * bias_here, bias_here, 1
-    )
-
-    def to_owner(total):
-        blocks = total.astype(BF16).reshape(TP, rows, total.shape[1])
-        return links.group_swap(blocks).transpose(1, 0, 2).astype(F32)
-
-    down_shard = to_owner(down_sum).reshape(rows, hidden_local).T
-    gating_parts = to_owner(gating_sum)
+
+    lines = count // TP
+    line = place // TP
+
+    def total(parts):
+        summed = 0.0
+        for u in range(lines):
+            piece = parts[u].astype(F32)
+            if lines == 4 and u in (0, 3):
+                piece = jnp.where(line == 3 - u, 0.0, piece)
+            summed = summed + piece
+        return summed.transpose(1, 0, 2)
+
+    gating_parts = total(rs_g)
     gate_parts = jnp.concatenate([gating_parts[..., :full], gating_parts[..., 2 * full : full + hid]], axis=2)
     up_parts = jnp.concatenate([gating_parts[..., full : 2 * full], gating_parts[..., full + hid :]], axis=2)
     gating_shard = jnp.stack([gate_parts, up_parts], axis=1).reshape(gating_weight.shape)
-    out_shard = to_owner(out_sum).reshape(rows, head_local).T
-    qkv_shard = (
-        to_owner(qkv_sum).reshape(rows, TP, 3, wide).transpose(0, 2, 1, 3).reshape(qkv_weight.shape)
-    )
+    qkv_shard = total(rs_q).reshape(rows, TP, 3, wide).transpose(0, 2, 1, 3).reshape(qkv_weight.shape)
+    out_shard = total(rs_o).reshape(rows, head_local).T
+    down_shard = total(rs_d)[..., :hid].reshape(rows, hidden_local).T
+    norm_grad = lax.dynamic_slice_in_dim(norm_sum[:4], (place * rows) % 128, rows, 1)
+    bias_grad = bias_sum[:, 0].reshape(TP, 3, wide).transpose(1, 0, 2).reshape(1, 3 * head_local)
+    bias_grad = lax.dynamic_slice_in_dim(bias_grad, place * bias_here, bias_here, 1)
     return (
         block_out[None],
         input_grad[None],

time: 870 us -> 687 us (0.79); the launches traced: 860 us -> 686 us
  Pallas kernels: 297 us -> 582 us
  waiting for transfers between devices: 204 us -> 0 us
  local copies, waits for them, and re-layouts: 151 us -> 72.3 us
  starting transfers between devices: 75.2 us -> 0 us
  matrix products: 51.5 us -> 0 us
  other arithmetic: 78.8 us -> 30.7 us
    pallas_call x1, Pallas kernels: 11.4 us -> 299 us  [backward(): pl.pallas_call(functools.partial(backward_kernel, count), in_specs=[vmem]...]
    ppermute x56 -> x0, waiting for transfers between devices: 204 us -> none  [the longest x19 117 us: along(): lax.ppermute(values, 'dp', [(a * TP + r, b * TP + r) for a, b in pairs fo...]
    ppermute x56 -> x0, starting transfers between devices: 75.2 us -> none  [the longest x19 41.7 us: along(): lax.ppermute(values, 'dp', [(a * TP + r, b * TP + r) for a, b in pairs fo...]
    dot_general x9 -> x0, matrix products: 51.5 us -> none  [dot(): lax.dot_general(a, b, (((ca,), (cb,)), ((), ())), preferred_element_type=...]
    dynamic_slice x7 -> x0, local copies, waits for them, and re-layouts: 17.4 us -> none  [the longest x1 11.1 us: block(): return lax.dynamic_index_in_dim(blocks, (self.u + k) % n, 0, False)]
    convert_element_type x12 -> x0, other arithmetic: 17.1 us -> none  [the longest x4 7.17 us: to_owner(): blocks = total.astype(BF16).reshape(TP, rows, total.shape[1])]
    unnamed x130 -> x66, local copies, waits for them, and re-layouts: 64.1 us -> 51.1 us
    add x20 -> x0, other arithmetic: 12.3 us -> none  [the longest x3 8.55 us: scatter_sum(): here = take(partial, 1, self.c) + other.astype(F32)]
  transfers between devices with their start and end apart: 56 -> 0, of which waited for: 29 -> 0; matrix products, arithmetic and copies ran while one was open for 23% -> 0% of each run, Pallas kernels for 1% -> 0%
where the time goes in v3:
time: 687 us; the launch traced here: 686 us
  Pallas kernels  582 us (85%)
  local copies, waits for them, and re-layouts  72.3 us (11%)
  other arithmetic  30.7 us (4%)
    pallas_call x1, Pallas kernels, backward(): pl.pallas_call(functools.partial(backward_kernel, count), in_specs=[vmem]...  299 us
    pallas_call x1, Pallas kernels, forward(): pl.pallas_call(functools.partial(forward_kernel, count), in_specs=[vmem,...  283 us
    unnamed x66, local copies, waits for them, and re-layouts  51.1 us
    sub x6, other arithmetic, adamw_update(): weight_old - step_rate * (corrected + decay_rate * weight_old)  21.1 us

profile of v3, /device:TPU:0, one launch (start us, length us, event | category | flops | bytes accessed | tf_op | source)
XLA Modules:
  0.0 686.3 jit_solution(11452550164310451199)
XLA Ops:
  0.7 0.9 dynamic_update_slice.8
  1.6 0.7 convert.15
  2.2 0.6 fusion.8.small_src
  2.8 4.1 copy.135
  7.2 1.4 copy-done
  8.6 1.1 copy-done.8
  9.8 0.3 copy.162
  10.1 0.3 copy.163
  10.4 0.9 fusion.22
  11.5 2.2 concatenate.19
  14.2 0.7 pad.11.aux_src
  14.9 0.5 copy.131
  15.5 0.9 copy.132
  16.4 0.3 copy-done.2
  16.7 2.3 copy.133
  19.0 0.6 broadcast_in_dim.39.row_src
  20.0 0.9 pad_bitcast_fusion.wd_src
  21.0 0.9 copy.134
  21.8 283.0 %forward.1 = (bf16[2048,768]{1,0:T(8,128)(2,1)}, bf16[2048,256]{1,0:T(8,128)(2,1)}, bf16[2048,1408]{1,0:T(8,128)(2,1)}, bf16[2048,768]{1,0:T(8,128)(2,1)}, bf16[...) custom-call(bf16[40,128]{1,0:T(8,128)(2,1)} %fusion.8.small_src, ...), custom_call_target="tpu_custom_call" | custom-call | flops 12000000000 | bytes 80000000 | tf_op jit(solution)/shard_map/forward/pallas_call | solution.py:583
  304.8 299.3 %backward.1 = (bf16[4,4,128,768]{3,2,1,0:T(8,128)(2,1)}, bf16[4,4,128,256]{3,2,1,0:T(8,128)(2,1)}, bf16[4,4,128,1408]{3,2,1,0:T(8,128)(2,1)}, bf16[4,4,128,768]{...) custom-call(f32[4,256,128]{2,1,0:T(8,128)} %get-tuple-element.43.aux, ...), custom_call_target="tpu_custom_call" | custom-call | flops 27000000512 | bytes 120000000 | tf_op jit(solution)/shard_map/backward/pallas_call | solution.py:968
  604.1 3.5 add_bitcast_fusion
  608.3 1.6 copy.150
  609.8 1.6 copy.151
  611.4 5.6 copy.149
  617.0 5.7 copy.152
  622.7 6.7 multiply_subtract_fusion
  629.4 5.6 copy.159
  635.0 5.7 copy.160
  640.7 3.3 copy.161
  644.0 3.7 add_bitcast_fusion.1
  647.7 1.6 copy.142
  649.3 2.8 copy.143
  652.1 1.6 copy.141
  653.7 3.1 copy.144
  656.9 5.3 multiply_subtract_fusion.1
  662.1 3.0 copy.156
  665.2 3.1 copy.157
  668.3 1.6 copy.158
  669.9 1.6 copy.155
  671.5 5.0 multiply_subtract_fusion.2
  676.9 0.7 copy-done.10
  677.6 2.8 multiply_subtract_fusion.3
  680.4 0.9 slice.89
  681.4 0.7 multiply_subtract_fusion.5
  682.0 0.6 multiply_subtract_fusion.4
  682.7 1.3 copy.169
  684.0 1.0 copy-done.11
  685.0 1.3 copy.170
  (66 shorter events, 2.5 us)
Async XLA Ops:
  7.0 1.6 copy-start
  8.6 1.1 copy-start.8
  11.4 2.3 copy-start.16
  11.5 3.3 copy-start.13
  15.3 1.4 copy-start.2
  15.5 4.2 copy-start.6
  19.7 1.3 copy-start.9
  617.0 5.7 copy-start.1
  635.0 5.7 copy-start.4
  649.3 2.8 copy-start.14
  653.7 3.1 copy-start.3
  665.2 3.1 copy-start.5
  669.9 1.6 copy-start.7
  671.5 5.0 copy-start.15
  676.5 1.0 copy-start.10
  677.6 3.8 copy-start.18
  677.6 3.8 copy-start.22
  677.6 3.8 copy-start.23
  677.6 4.5 copy-start.17
  677.6 4.5 copy-start.19
  677.6 4.4 copy-start.20
  677.6 4.4 copy-start.21
  677.6 5.0 copy-start.12
  682.7 2.3 copy-start.11

commit v4 on v3

v4 whole, which is shorter than its diff:
```python
import functools

import jax
import jax.numpy as jnp
from jax import lax
from jax.experimental import pallas as pl
from jax.experimental.pallas import tpu as pltpu
from jax.sharding import PartitionSpec as P

D = 2048
H = 32
HD = 64
ROT = 16
FF = 5632
STEP = 10
TP = 4

F32 = jnp.float32
BF16 = jnp.bfloat16


def layer_norm(values, scale_row, shift_row):
    centre = values - jnp.mean(values, axis=-1, keepdims=True)
    spread = jnp.mean(centre * centre, axis=-1, keepdims=True)
    inverse = lax.rsqrt(spread + 1e-05)
    scaled = centre * inverse
    return (scaled * scale_row + shift_row, scaled, inverse)


def norm_back(grad_in, scaled, inverse, scale_row):
    grad_scaled = grad_in * scale_row
    mean_first = jnp.mean(grad_scaled, axis=-1, keepdims=True)
    mean_second = jnp.mean(grad_scaled * scaled, axis=-1, keepdims=True)
    grad_values = inverse * (grad_scaled - mean_first - scaled * mean_second)
    return (grad_values, jnp.sum(grad_in * scaled, axis=0), jnp.sum(grad_in, axis=0))


def adamw_update(weight_old, gradient, first_old, second_old, step_rate, decay_rate):
    first_new = 0.9 * first_old + 0.1 * gradient
    second_new = 0.95 * second_old + 0.05 * gradient * gradient
    corrected = first_new / (1.0 - 0.9**STEP) / (jnp.sqrt(second_new / (1.0 - 0.95**STEP)) + 1e-08)
    return (weight_old - step_rate * (corrected + decay_rate * weight_old), first_new, second_new)


def dot(a, b, ca, cb):
    return lax.dot_general(a, b, (((ca,), (cb,)), ((), ())), preferred_element_type=F32)


def spin(values, cos_t, lower_t, upper_t):
    wide = values.shape[1]
    return (
        values * cos_t
        + pltpu.roll(values, wide - ROT // 2, 1) * lower_t
        + pltpu.roll(values, ROT // 2, 1) * upper_t
    )


def spin_back(values, cos_t, lower_t, upper_t):
    wide = values.shape[1]
    return (
        values * cos_t
        + pltpu.roll(values * lower_t, ROT // 2, 1)
        + pltpu.roll(values * upper_t, wide - ROT // 2, 1)
    )


def mask_of(seg_col, seg_row, size):
    rows = lax.broadcasted_iota(jnp.int32, (size, size), 0)
    cols = lax.broadcasted_iota(jnp.int32, (size, size), 1)
    return (seg_col == seg_row) & (cols <= rows)


def attend_back_values(query, key, value, grad, allowed, tables):
    head_of = lax.broadcasted_iota(jnp.int32, query.shape, 1) // HD
    zero = jnp.zeros_like(query)
    dq = jnp.zeros(query.shape, F32)
    dk = jnp.zeros(query.shape, F32)
    dv = jnp.zeros(query.shape, F32)
    for head in range(query.shape[1] // HD):
        mine = head_of == head
        query_h = jnp.where(mine, query, zero)
        grad_h = jnp.where(mine, grad, zero)
        scores = dot(query_h, key, 1, 1) * HD ** (-0.5)
        scores = jnp.where(allowed, scores, -1e30)
        weights = jnp.exp(scores - jnp.max(scores, axis=1, keepdims=True))
        prob = weights / jnp.sum(weights, axis=1, keepdims=True)
        dv = dv + dot(prob.astype(BF16), grad_h, 0, 0)
        dprob = dot(grad_h, value, 1, 1)
        delta = jnp.sum(prob * dprob, axis=1, keepdims=True)
        dscore = (prob * (dprob - delta)).astype(BF16)
        dq = jnp.where(mine, dot(dscore, key, 1, 0), dq)
        dk = dk + dot(dscore, query_h, 0, 0)
    dq = spin_back(dq * HD ** (-0.5), *tables).astype(BF16)
    dk = spin_back(dk * HD ** (-0.5), *tables).astype(BF16)
    return dq, dk, dv.astype(BF16)


class Place:
    def __init__(self, count):
        self.count = count
        self.lines = count // TP
        self.me = lax.axis_index("dp")
        self.t = lax.axis_index("tensor")
        self.u = self.me // TP
        self.j = self.me % TP
        self.x = self.j // 2
        self.c = self.j % 2
        self.core_peer = self.me + 1 - 2 * self.c
        self.x_peer = self.me + 2 - 4 * self.x

    def group(self, k):
        x = (self.x + k // 2) % 2
        return self.u * TP + x * 2 + self.c, (self.t + k % 2) % 2, x


def remote(src, dst, send_sem, recv_sem, dp, t):
    return pltpu.make_async_remote_copy(
        src_ref=src,
        dst_ref=dst,
        send_sem=send_sem,
        recv_sem=recv_sem,
        device_id=(dp, t),
        device_id_type=pl.DeviceIdType.MESH,
    )


def wait_bytes(ref, sem):
    pltpu.make_async_copy(ref, ref, sem).wait()


def greet(place):
    barrier = pltpu.get_barrier_semaphore()

    @pl.loop(1, place.count)
    def _(k):
        pl.semaphore_signal(
            barrier,
            inc=1,
            device_id=((place.me + k) % place.count, place.t),
            device_id_type=pl.DeviceIdType.MESH,
        )

    for k in (1, 3):
        dp, t, _ = place.group(k)
        pl.semaphore_signal(barrier, inc=1, device_id=(dp, t), device_id_type=pl.DeviceIdType.MESH)
    pl.semaphore_wait(barrier, place.count + 1)


def each_dest(place, act):
    if place.lines == 4:

        @pl.loop(1, TP)
        def _(q):
            j = (place.j + q) % TP
            act(place.u * TP + j, place.u, j)

        @pl.loop(0, TP)
        def _(q):
            j = (place.j + q) % TP
            for dz in (2, 1, 3):
                u = (place.u + dz) % 4
                act(u * TP + j, u, j)

    else:

        @pl.loop(1, place.count)
        def _(k):
            dest = (place.me + k) % place.count
            act(dest, dest // TP, dest % TP)


class WeightGather:
    def __init__(self, place, index, src, dst, send_sem, recv_sem):
        self.place, self.src, self.dst = place, src, dst
        self.send_sem, self.recv_sem = send_sem.at[index], recv_sem.at[index]
        self.rows = src.shape[1]

    def group_copy(self, q):
        p = self.place
        j = (p.j + q) % TP
        mine = self.dst.at[pl.ds(p.me * self.rows, self.rows)]
        return remote(self.src.at[j], mine, self.send_sem.at[q], self.recv_sem.at[2], p.u * TP + j, p.t)

    def chunk(self, u):
        size = TP * self.rows
        return self.dst.at[pl.ds(u * size, size)]

    def line_copy(self, k):
        p = self.place
        u = (p.u + k) % p.lines
        far = 0
        if p.lines == 4:
            far = (((p.u == 0) & (u == 2)) | ((p.u == 3) & (u == 1))).astype(jnp.int32)
        mine = self.chunk(p.u)
        return remote(mine, mine, self.send_sem.at[TP + k], self.recv_sem.at[far], u * TP + p.j, p.t)

    def line_each(self, act):
        p = self.place
        if p.lines == 4:
            for k in (2, 1, 3):
                pl.when(jnp.abs(p.u - (p.u + k) % 4) < 3)(lambda k=k: act(k))
        else:
            for k in range(1, p.lines):
                act(k)

    def start(self):
        p = self.place
        for q in (2, 3, 1):
            self.group_copy(q).start()
        mine = self.dst.at[pl.ds(p.me * self.rows, self.rows)]
        pltpu.make_async_copy(self.src.at[p.j], mine, self.recv_sem.at[2]).start()

    def pass_on(self):
        wait_bytes(self.chunk(0), self.recv_sem.at[2])
        self.line_each(lambda k: self.line_copy(k).start())

    def middle(self):
        return (self.place.u == 1) | (self.place.u == 2)

    def forward(self):
        p = self.place
        chunk = self.chunk(jnp.where(p.u == 2, 0, 3))
        dest = p.me + jnp.where(p.u == 2, TP, -TP)
        return remote(chunk, chunk, self.send_sem.at[TP], self.recv_sem.at[1], dest, p.t)

    def relay(self):
        if self.place.lines == 4:

            @pl.when(self.middle())
            def _():
                wait_bytes(self.chunk(0), self.recv_sem.at[1])
                self.forward().start()

    def arrive(self):
        p = self.place
        size = TP * self.rows
        wait_bytes(self.dst.at[pl.ds(0, size * (2 if p.lines == 4 else p.lines - 1))], self.recv_sem.at[0])
        if p.lines == 4:
            pl.when(~self.middle())(lambda: wait_bytes(self.chunk(0), self.recv_sem.at[1]))

    def finish(self):
        for q in range(1, TP):
            self.group_copy(q).wait_send()
        self.line_each(lambda k: self.line_copy(k).wait_send())
        if self.place.lines == 4:
            pl.when(self.middle())(lambda: self.forward().wait_send())


class GroupSum:
    def __init__(self, place, to_core, from_core, low, own, parts, core_sem, part_sem, free_sem=None):
        self.place = place
        self.to_core, self.from_core, self.low, self.own, self.parts = to_core, from_core, low, own, parts
        self.core_sem, self.part_sem, self.free_sem = core_sem, part_sem, free_sem

    def core_copy(self, i):
        p = self.place
        return remote(
            self.to_core.at[i], self.from_core.at[i], self.core_sem.at[0, i], self.core_sem.at[1, i], p.core_peer, p.t
        )

    def part_copy(self, k):
        p = self.place
        half = self.parts.shape[1]
        dp, t, _ = p.group(k)
        block = self.low.at[0 if k >= 2 else 1, pl.ds(pl.multiple_of(t * half, half), half)]
        return remote(block, self.parts.at[k - 1], self.part_sem.at[0, k], self.part_sem.at[1, k], dp, t)

    def start(self, product):
        p = self.place
        step = min(512, D)
        other = [(p.x + 1) % 2, p.x]
        for i in range(2):

            @pl.loop(0, D // step)
            def _(n):
                at = pl.ds(pl.multiple_of(n * step, step), step)
                self.to_core[i, :, at] = product(other[i] * 2 + 1 - p.c, n, step).astype(BF16)

            self.core_copy(i).start()
        for i in range(2):
            self.core_copy(i).wait_recv()

            @pl.loop(0, D // step)
            def _(n):
                at = pl.ds(pl.multiple_of(n * step, step), step)
                total = product(other[i] * 2 + p.c, n, step) + self.from_core[i, :, at].astype(F32)
                self.low[i, :, at] = total.astype(BF16)
                if i == 1:
                    half = self.own.shape[0]

                    @pl.when(p.t == 0)
                    def _():
                        self.own[:, at] = total[:half]

                    @pl.when(p.t == 1)
                    def _():
                        self.own[:, at] = total[half:]

            for k in (3, 2) if i == 0 else (1,):
                self.part_copy(k).start()

    def arrive(self):
        for k in (3, 2, 1):
            self.part_copy(k).wait_recv()

    def total(self, at, rows):
        value = self.own[pl.ds(pl.multiple_of(at, 32), rows), :]
        for k in range(3):
            value = value + self.parts[k, pl.ds(pl.multiple_of(at, 32), rows), :].astype(F32)
        return value

    def finish(self):
        for i in range(2):
            self.core_copy(i).wait_send()
        for k in (1, 2, 3):
            self.part_copy(k).wait_send()

    def release(self):
        p = self.place
        pl.semaphore_signal(
            self.free_sem.at[0], inc=1, device_id=(p.core_peer, p.t), device_id_type=pl.DeviceIdType.MESH
        )
        for k in (1, 2, 3):
            dp, t, _ = p.group(k)
            pl.semaphore_signal(
                self.free_sem.at[k], inc=1, device_id=(dp, t), device_id_type=pl.DeviceIdType.MESH
            )

    def acquire(self):
        self.finish()
        for k in range(4):
            pl.semaphore_wait(self.free_sem.at[k], 1)


class GroupGather:
    def __init__(self, place, out, size, part_sem, core_sem):
        self.place, self.out, self.half = place, out, size // 2
        self.part_sem, self.core_sem = part_sem, core_sem

    def block(self, x, t):
        p = self.place
        start = ((x * 2 + p.c) * 2 + t) * self.half
        return self.out.at[pl.ds(pl.multiple_of(start, self.half), self.half)]

    def part_copy(self, k):
        p = self.place
        dp, t, _ = p.group(k)
        mine = self.block(p.x, p.t)
        return remote(mine, mine, self.part_sem.at[0, k], self.part_sem.at[1, k], dp, t)

    def core_copy(self, k):
        p = self.place
        _, t, x = p.group(k)
        block = self.block(x, t)
        return remote(block, block, self.core_sem.at[0, k], self.core_sem.at[1, k], p.core_peer, p.t)

    def start(self):
        for k in (3, 2, 1):
            self.part_copy(k).start()
        self.core_copy(0).start()

    def arrive(self):
        for k in (1, 2, 3):
            self.part_copy(k).wait_recv()
            self.core_copy(k).start()
        for k in range(4):
            self.core_copy(k).wait_recv()

    def finish(self):
        for k in (1, 2, 3):
            self.part_copy(k).wait_send()
        for k in range(4):
            self.core_copy(k).wait_send()


class GroupPieces:
    def __init__(self, place, src, out, sem, size=0):
        self.place, self.src, self.out, self.sem, self.size = place, src, out, sem, size

    def at(self, j):
        if self.size:
            return self.out.at[pl.ds(pl.multiple_of(j * self.size, self.size), self.size)]
        return self.out.at[j]

    def own(self):
        return pltpu.make_async_copy(self.src, self.at(self.place.j), self.sem.at[0, 0])

    def near(self, k):
        p = self.place
        dest = p.core_peer if k == 1 else p.x_peer
        return remote(self.src, self.at(p.j), self.sem.at[0, k], self.sem.at[1, k], dest, p.t)

    def relay(self):
        p = self.place
        block = self.at((p.j + 2) % TP)
        return remote(block, block, self.sem.at[0, 3], self.sem.at[1, 3], p.core_peer, p.t)

    def start(self):
        self.near(2).start()
        self.near(1).start()
        self.own().start()

    def pass_on(self):
        self.near(2).wait_recv()
        self.relay().start()

    def arrive(self):
        self.near(1).wait_recv()
        self.relay().wait_recv()
        self.own().wait()

    def finish(self):
        self.near(1).wait_send()
        self.near(2).wait_send()
        self.relay().wait_send()


def tables_of(aux, wide):
    half = ROT // 2
    line = lax.broadcasted_iota(jnp.int32, (aux.shape[1], wide), 0)
    lane = lax.broadcasted_iota(jnp.int32, (aux.shape[1], wide), 1) % HD
    first = lane < half
    second = (lane >= half) & (lane < ROT)

    def spread(pick, sign):
        table = jnp.where(pick, sign, 0.0).astype(F32)
        return lax.dot_general(
            aux, table, (((1,), (0,)), ((), ())), precision=lax.Precision.HIGHEST, preferred_element_type=F32
        )

    rest = lax.broadcasted_iota(jnp.int32, (aux.shape[0], wide), 1) % HD >= ROT
    cos_t = spread((line == lane % half) & (first | second), 1.0) + jnp.where(rest, 1.0, 0.0)
    low_t = spread((line == lane + half) & first, -1.0)
    upp_t = spread((line == lane) & second, 1.0)
    return cos_t, low_t, upp_t


def attend_values(query, key, value, allowed):
    head_of = lax.broadcasted_iota(jnp.int32, query.shape, 1) // HD
    total = jnp.zeros(query.shape, F32)
    for head in range(query.shape[1] // HD):
        mine = head_of == head
        scores = dot(jnp.where(mine, query, jnp.zeros_like(query)), key, 1, 1) * HD ** (-0.5)
        scores = jnp.where(allowed, scores, -1e30)
        weights = jnp.exp(scores - jnp.max(scores, axis=1, keepdims=True))
        prob = weights / jnp.sum(weights, axis=1, keepdims=True)
        total = jnp.where(mine, dot(prob.astype(BF16), value, 1, 0), total)
    return total


class GradScatter:
    def __init__(self, place, index, grad, slots, out, send_sem, recv_sem, free_sem=None):
        self.place, self.grad, self.slots, self.out = place, grad, slots, out
        self.send_sem, self.recv_sem, self.free_sem = send_sem.at[index], recv_sem.at[index], free_sem
        self.rows = out.shape[1]
        self.size = TP * self.rows

    def chunk(self, ref, u):
        return ref.at[pl.ds(u * self.size, self.size)]

    def near(self, u):
        return jnp.abs(self.place.u - u) < 3 if self.place.lines == 4 else None

    def line_each(self, act, picked=lambda u: True):
        p = self.place
        for k in (2, 1, 3) if p.lines == 4 else range(1, p.lines):
            u = (p.u + k) % p.lines
            if p.lines == 4:
                pl.when(self.near(u) & picked(u))(lambda k=k, u=u: act(k, u))
            else:
                act(k, u)

    def line_copy(self, k, u):
        p = self.place
        far = 0
        if p.lines == 4:
            far = (((p.u == 0) & (u == 2)) | ((p.u == 3) & (u == 1))).astype(jnp.int32)
        return remote(
            self.chunk(self.grad, u), self.chunk(self.slots, p.u), self.send_sem.at[TP + k], self.recv_sem.at[far],
            u * TP + p.j, p.t,
        )

    def outer(self):
        p = self.place
        first = p.u == 0
        src, dst = self.chunk(self.grad, jnp.where(first, 3, 0)), self.chunk(self.slots, jnp.where(first, 1, 2))
        return remote(src, dst, self.send_sem.at[TP], self.recv_sem.at[2], p.me + jnp.where(first, TP, -TP), p.t)

    def ends(self):
        return (self.place.u == 0) | (self.place.u == 3)

    def later(self, u):
        p = self.place
        return ((p.u == 1) & (u == 3)) | ((p.u == 2) & (u == 0))

    def allow(self):
        p = self.place
        self.line_each(
            lambda k, u: pl.semaphore_signal(
                self.free_sem.at[p.u], inc=1, device_id=(u * TP + p.j, p.t), device_id_type=pl.DeviceIdType.MESH
            )
        )

    def start(self):
        if self.free_sem is not None:
            self.line_each(lambda k, u: pl.semaphore_wait(self.free_sem.at[u], 1))
        if self.place.lines == 4:
            pl.when(self.ends())(lambda: self.outer().start())
            self.line_each(lambda k, u: self.line_copy(k, u).start(), lambda u: ~self.later(u))
        else:
            self.line_each(lambda k, u: self.line_copy(k, u).start())

    def add(self, u, sources):
        p = self.place

        @pl.loop(0, self.size // 32)
        def _(i):
            at = pl.ds(pl.multiple_of(u * self.size + i * 32, 32), 32)
            total = self.grad[at, :].astype(F32)
            for slot in sources:
                here = pl.ds(pl.multiple_of(slot * self.size + i * 32, 32), 32)
                total = total + self.slots[here, :].astype(F32)
            self.grad[at, :] = total.astype(BF16)

    def combine(self):
        p = self.place
        if p.lines != 4:
            return

        @pl.when(~self.ends())
        def _():
            wait_bytes(self.chunk(self.slots, 0), self.recv_sem.at[2])
            self.add(jnp.where(p.u == 1, 3, 0), [p.u])
            self.line_each(lambda k, u: self.line_copy(k, u).start(), self.later)

    def group_copy(self, q):
        p = self.place
        j = (p.j + q) % TP
        block = self.grad.at[pl.ds((p.u * TP + j) * self.rows, self.rows)]
        return remote(block, self.out.at[p.j], self.send_sem.at[q], self.recv_sem.at[3], p.u * TP + j, p.t)

    def reduce(self):
        p = self.place
        if p.lines == 4:
            wait_bytes(self.slots.at[pl.ds(0, 2 * self.size)], self.recv_sem.at[0])
            pl.when(~self.ends())(lambda: wait_bytes(self.chunk(self.slots, 0), self.recv_sem.at[1]))
            pl.when(self.ends())(lambda: self.add(p.u, [1, 2]))
            pl.when(p.u == 1)(lambda: self.add(p.u, [0, 2, 3]))
            pl.when(p.u == 2)(lambda: self.add(p.u, [0, 1, 3]))
        else:
            wait_bytes(self.slots.at[pl.ds(0, (p.lines - 1) * self.size)], self.recv_sem.at[0])
            for k in range(1, p.lines):
                self.add(p.u, [(p.u + k) % p.lines])
        for q in (2, 3, 1):
            self.group_copy(q).start()
        own = self.grad.at[pl.ds(p.me * self.rows, self.rows)]
        pltpu.make_async_copy(own, self.out.at[p.j], self.recv_sem.at[3]).start()

    def finish(self):
        wait_bytes(self.out, self.recv_sem.at[3])
        for q in range(1, TP):
            self.group_copy(q).wait_send()
        self.line_each(lambda k, u: self.line_copy(k, u).wait_send())
        if self.place.lines == 4:
            pl.when(self.ends())(lambda: self.outer().wait_send())


def norm_stats(values):
    centre = values - jnp.mean(values, axis=-1, keepdims=True)
    inverse = lax.rsqrt(jnp.mean(centre * centre, axis=-1, keepdims=True) + 1e-05)
    return centre * inverse, inverse


def layer_kernel(
    count,
    small_src, aux_src, row_src, tok_src, cot_src, wq_src, wo_src, wg_src, wd_src,
    rs_q, rs_o, rs_g, rs_d, block_out, input_out, h1_out, norm_out, bias_out,
    wq, wo, wg, wd, cot, hh, qkv, att, hid, slopes, dgate, gd, gg, go, slots_d, slots_o,
    to_core, from_core, low, own, parts, grad, resid, block, gains, biases, norms,
    small, aux_all, row_all, small_all, bias_all, small_t,
    w_send, w_recv, small_sem, aux_sem, row_sem, tok_sem, cot_sem, h1_sem,
    rs_send, rs_recv, free_g, free_d, core_sem, part_sem, free_sem, part2_sem, core2_sem, part3_sem, core3_sem,
    swap_sem, gain_sem, bias_sem, rank_sem, t_sem,
):
    p = Place(count)
    size = tok_src.shape[0]
    half = size // 2
    group = TP * size
    wide = att.shape[1]
    rows = wq_src.shape[1]
    full = hid.shape[1] - 128
    greet(p)

    def rows_of(s):
        return pl.ds(pl.multiple_of(s * size, size), size)

    def columns(n, step):
        return pl.ds(pl.multiple_of(n * step, step), step)

    gathers = [
        WeightGather(p, i, src, dst, w_send, w_recv)
        for i, (src, dst) in enumerate(((wq_src, wq), (wo_src, wo), (wg_src, wg), (wd_src, wd)))
    ]
    gather_q, gather_o, gather_g, gather_d = gathers
    tok = cot
    auxes = GroupPieces(p, aux_src, aux_all, aux_sem)
    rowses = GroupPieces(p, row_src, row_all, row_sem)
    tokens = GroupPieces(p, tok_src, tok, tok_sem, size)
    cots = GroupPieces(p, cot_src, cot, cot_sem, size)
    sums = GroupSum(p, to_core, from_core, low, own, parts, core_sem, part_sem, free_sem)
    spread_h = GroupGather(p, hh, size, part2_sem, core2_sem)
    spread_r = GroupGather(p, cot, size, part3_sem, core3_sem)
    gq = slopes.at[:D, : 3 * wide]
    scatter_q, scatter_o, scatter_g, scatter_d = [
        GradScatter(p, i, g, slots, out, rs_send, rs_recv, free)
        for i, (g, slots, out, free) in enumerate(
            (
                (gq, slots_d.at[:, : 3 * wide], rs_q, free_d),
                (go, slots_o, rs_o, None),
                (gg, wg, rs_g, free_g),
                (gd, slots_d.at[:, : hid.shape[1]], rs_d, None),
            )
        )
    ]

    def small_copy(dest):
        return remote(small_src, small.at[p.me], small_sem.at[dest], small_sem.at[count], dest, p.t)

    gather_q.start()
    auxes.start()
    rowses.start()
    gather_o.start()
    gather_g.start()
    gather_d.start()
    tokens.start()
    pltpu.make_async_copy(small_src, small.at[p.me], small_sem.at[count]).start()
    gather_q.pass_on()
    each_dest(p, lambda dest, u, j: small_copy(dest).start())
    gather_o.pass_on()
    gather_g.pass_on()
    auxes.pass_on()
    rowses.pass_on()
    gather_d.pass_on()
    tokens.pass_on()

    wait_bytes(small, small_sem.at[count])
    per_tile = 128 // rows
    for m in range(D // 128):
        tile = jnp.zeros((8, 128), F32)
        for i in range(per_tile):
            tile = tile + small[m * per_tile + i].astype(F32)[0:8]
        norms[0:8, m * 128 : (m + 1) * 128] = tile
    bias_rows = small.shape[1] - 16
    total = jnp.zeros((bias_rows, 128), F32)
    for d in range(count):
        total = total + small[d].astype(F32)[16:]
    for i in range(bias_rows):
        norms[8:9, i * 128 : (i + 1) * 128] = total[i : i + 1]
    auxes.arrive()
    rowses.arrive()
    gather_q.relay()
    tokens.arrive()

    @pl.loop(0, group // 32)
    def _(i):
        at = pl.ds(pl.multiple_of(i * 32, 32), 32)
        normed, _, _ = layer_norm(tok[at, :].astype(F32), norms[0:1, :D], norms[1:2, :D])
        hh[at, :] = normed.astype(BF16)

    tokens.finish()
    keep_h1 = pltpu.make_async_copy(hh, h1_out, h1_sem.at[0])
    keep_h1.start()
    gather_q.arrive()
    gather_o.relay()
    head_wide = (bias_rows * 128) // 3

    @pl.loop(0, TP)
    def _(s):
        at = rows_of(s)
        proj = dot(hh[at, :], wq[...], 1, 0)
        tables = tables_of(aux_all[s], wide)

        def part(k):
            lanes = pl.ds(pl.multiple_of(k * head_wide + p.j * wide, 128), wide)
            return proj[:, k * wide : (k + 1) * wide] + norms[8:9, lanes]

        query = spin(part(0), *tables).astype(BF16)
        key = spin(part(1), *tables).astype(BF16)
        value = part(2).astype(BF16)
        qkv[at, :wide] = query
        qkv[at, wide : 2 * wide] = key
        qkv[at, 2 * wide :] = value
        allowed = mask_of(aux_all[s][:, ROT : ROT + 1], row_all[s, 0:1, :], size)
        att[at, :] = attend_values(query, key, value, allowed).astype(BF16)

    gather_o.arrive()
    keep_h1.wait()
    sums.start(lambda s, n, step: dot(att[rows_of(s), :], wo[columns(n, step), :], 1, 1))
    gather_g.relay()
    sums.arrive()

    @pl.loop(0, half // 32)
    def _(i):
        at = pl.multiple_of(i * 32, 32)
        values = tok_src[pl.ds(pl.multiple_of(p.t * half + at, 32), 32), :].astype(F32)
        values = values + sums.total(at, 32)
        resid[pl.ds(at, 32), :] = values
        normed, _, _ = layer_norm(values, norms[2:3, :D], norms[3:4, :D])
        start = (p.j * 2 + p.t) * half + at
        hh[pl.ds(pl.multiple_of(start, 32), 32), :] = normed.astype(BF16)

    sums.release()
    spread_h.start()
    cots.start()
    spread_h.arrive()
    cots.pass_on()
    gather_g.arrive()
    gather_d.relay()

    @pl.loop(0, TP)
    def _(s):
        at = rows_of(s)
        late = pl.ds(pl.multiple_of(group + s * size, size), size)
        rows_in = hh[at, :]
        gate = dot(rows_in, wg[:, :full], 1, 0)
        up = dot(rows_in, wg[:, full : 2 * full], 1, 0)
        sig = jax.nn.sigmoid(gate)
        hid[at, :full] = (gate * sig * up).astype(BF16)
        slopes[at, :full] = (up * sig * (1.0 + gate * (1.0 - sig))).astype(BF16)
        slopes[late, :full] = (gate * sig).astype(BF16)
        gate = dot(rows_in, wg[:, 2 * full :], 1, 0)
        up = pltpu.roll(gate, 64, 1)
        sig = jax.nn.sigmoid(gate)
        first = lax.broadcasted_iota(jnp.int32, gate.shape, 1) < 64
        tail = slice(full, full + 128)
        hid[at, tail] = jnp.where(first, gate * sig * up, 0.0).astype(BF16)
        slopes[at, tail] = jnp.where(first, up * sig * (1.0 + gate * (1.0 - sig)), 0.0).astype(BF16)
        slopes[late, tail] = jnp.where(first, gate * sig, 0.0).astype(BF16)

    cots.arrive()
    step = min(256, D)

    def weight_grad(left, right, out):
        @pl.loop(0, D // step)
        def _(n):
            at = columns(n, step)
            out[at, :] = dot(left[:, at], right[...], 0, 0).astype(BF16)

    weight_grad(cot, hid, gd)
    scatter_d.start()

    gather_d.arrive()

    @pl.loop(0, TP)
    def _(s):
        at = rows_of(s)
        late = pl.ds(pl.multiple_of(group + s * size, size), size)
        dhid = dot(cot[at, :], wd[...], 1, 0)
        slope = dhid * slopes[at, : hid.shape[1]].astype(F32)
        gain = dhid * slopes[late, : hid.shape[1]].astype(F32)
        dgate[at, :full] = slope[:, :full].astype(BF16)
        dgate[at, full : 2 * full] = gain[:, :full].astype(BF16)
        last = slope[:, full:] + pltpu.roll(gain[:, full:], 64, 1)
        dgate[at, 2 * full :] = last.astype(BF16)

    cots.finish()
    sums.acquire()
    sums.start(lambda s, n, step: dot(dgate[rows_of(s), :], wg[columns(n, step), :], 1, 1))
    gather_g.finish()
    scatter_g.allow()
    weight_grad(hh, dgate, gg)
    scatter_g.start()
    spread_h.finish()
    load_h1 = pltpu.make_async_copy(h1_out, hh, h1_sem.at[1])
    load_h1.start()
    scatter_d.combine()
    sums.arrive()

    gains[...] = jnp.zeros_like(gains)

    @pl.loop(0, half // 32)
    def _(i):
        at = pl.multiple_of(i * 32, 32)
        scaled, inverse = norm_stats(resid[pl.ds(at, 32), :])
        part, gain, shift = norm_back(sums.total(at, 32), scaled, inverse, norms[2:3, :D])
        gains[2:3, :] += gain[None]
        gains[3:4, :] += shift[None]
        mine = pl.ds(pl.multiple_of((p.j * 2 + p.t) * half + at, 32), 32)
        total = cot[mine, :].astype(F32) + part
        grad[pl.ds(at, 32), :] = total
        cot[mine, :] = total.astype(BF16)

    sums.release()
    spread_r.start()
    scatter_g.combine()
    scatter_d.reduce()
    scatter_q.allow()
    spread_r.arrive()

    biases[...] = jnp.zeros_like(biases)

    @pl.loop(0, TP)
    def _(s):
        at = rows_of(s)
        grad_out = dot(cot[at, :], wo[...], 1, 0).astype(BF16)
        allowed = mask_of(aux_all[s][:, ROT : ROT + 1], row_all[s, 0:1, :], size)
        tables = tables_of(aux_all[s], wide)
        three = attend_back_values(
            qkv[at, :wide], qkv[at, wide : 2 * wide], qkv[at, 2 * wide :], grad_out, allowed, tables
        )
        for k, value in enumerate(three):
            lanes = slice(k * wide, (k + 1) * wide)
            qkv[at, lanes] = value
            biases[0:1, lanes] += jnp.sum(value.astype(F32), axis=0, keepdims=True)

    load_h1.wait()
    weight_grad(hh, qkv, gq)
    scatter_q.start()
    weight_grad(cot, att, go)
    scatter_o.start()

    bias_all[p.u] = biases[...]

    def bias_copy(k):
        u = (p.u + k) % p.lines
        return remote(biases, bias_all.at[p.u], bias_sem.at[k], bias_sem.at[p.lines + k], u * TP + p.j, p.t)

    for k in range(1, p.lines):
        bias_copy(k).start()

    sums.acquire()
    sums.start(lambda s, n, step: dot(qkv[rows_of(s), :], wq[columns(n, step), :], 1, 1))
    scatter_q.combine()
    scatter_o.combine()
    sums.arrive()

    @pl.loop(0, half // 32)
    def _(i):
        at = pl.multiple_of(i * 32, 32)
        values = tok_src[pl.ds(pl.multiple_of(p.t * half + at, 32), 32), :].astype(F32)
        scaled, inverse = norm_stats(values)
        part, gain, shift = norm_back(sums.total(at, 32), scaled, inverse, norms[0:1, :D])
        gains[0:1, :] += gain[None]
        gains[1:2, :] += shift[None]
        grad[pl.ds(at, 32), :] += part

    sums.release()
    mine = pl.ds(pl.multiple_of(p.t * half, half), half)

    def give(index, value, out):
        here = pltpu.make_async_copy(value, out.at[mine], swap_sem.at[index, 0])
        there = remote(value, out.at[mine], swap_sem.at[index, 1], swap_sem.at[index, 2], p.me, 1 - p.t)
        here.start()
        there.start()
        return here, there

    gives = [*give(0, grad, input_out)]

    def tile_of(d):
        return pl.ds(pl.multiple_of(d * rows // 128 * 128, 128), 128)

    def gain_copy(dest):
        return remote(gains.at[:, tile_of(dest)], small_all.at[p.me], gain_sem.at[dest], gain_sem.at[count], dest, p.t)

    pltpu.make_async_copy(gains.at[:, tile_of(p.me)], small_all.at[p.me], gain_sem.at[count]).start()
    each_dest(p, lambda dest, u, j: gain_copy(dest).start())

    for k in range(1, p.lines):
        bias_copy(k).wait_recv()
    total = bias_all[0]
    for k in range(1, p.lines):
        total = total + bias_all[k]
    bias_out[p.j] = total

    def rank_copy(q):
        j = (p.j + q) % TP
        return remote(bias_out.at[p.j], bias_out.at[p.j], rank_sem.at[q], rank_sem.at[TP + q], p.u * TP + j, p.t)

    for q in range(1, TP):
        rank_copy(q).start()

    sums.acquire()
    sums.start(lambda s, n, step: dot(hid[rows_of(s), :], wd[columns(n, step), :], 1, 1))
    sums.arrive()

    @pl.loop(0, half // 32)
    def _(i):
        at = pl.multiple_of(i * 32, 32)
        block[pl.ds(at, 32), :] = resid[pl.ds(at, 32), :] + sums.total(at, 32)

    gives += give(1, block, block_out)
    scatter_g.reduce()

    wait_bytes(small_all, gain_sem.at[count])
    total = small_all[0]
    for d in range(1, count):
        total = total + small_all[d]
    small_t[0] = total
    swap = remote(small_t.at[0], small_t.at[1], t_sem.at[0], t_sem.at[1], p.me, 1 - p.t)
    swap.start()
    scatter_q.reduce()
    scatter_o.reduce()
    swap.wait()
    norm_out[...] = small_t[0] + small_t[1]
    for q in range(1, TP):
        rank_copy(q).wait()
    for k in range(1, p.lines):
        bias_copy(k).wait_send()
    each_dest(p, lambda dest, u, j: small_copy(dest).wait_send())
    each_dest(p, lambda dest, u, j: gain_copy(dest).wait_send())
    for copy in gives:
        copy.wait()
    for part in (auxes, rowses, sums, spread_r, gather_q, gather_o, gather_d):
        part.finish()
    for scatter in (scatter_d, scatter_g, scatter_q, scatter_o):
        scatter.finish()


def layer(count, small, aux, row, tokens, cot, wq, wo, wg, wd):
    size = tokens.shape[0]
    half = size // 2
    group = TP * size
    lines, rows = count // TP, wq.shape[1]
    wide, pad, gates = wo.shape[2], wd.shape[2], wg.shape[2]
    any_spec = pl.BlockSpec(memory_space=pl.ANY)
    vmem = pl.BlockSpec(memory_space=pltpu.VMEM)
    dma = pltpu.SemaphoreType.DMA
    regular = pltpu.SemaphoreType.REGULAR

    def out(*shape, dtype=BF16):
        return jax.ShapeDtypeStruct(shape, dtype)

    return pl.pallas_call(
        functools.partial(layer_kernel, count),
        in_specs=[vmem, vmem, vmem, vmem] + [any_spec] * 5,
        out_specs=[any_spec] * 7 + [vmem] * 2,
        out_shape=[
            out(TP, rows, 3 * wide),
            out(TP, rows, wide),
            out(TP, rows, gates),
            out(TP, rows, pad),
            out(size, D, dtype=F32),
            out(size, D, dtype=F32),
            out(group, D),
            out(8, 128, dtype=F32),
            out(TP, 8, 3 * wide, dtype=F32),
        ],
        scratch_shapes=[
            pltpu.VMEM((D, 3 * wide), BF16),
            pltpu.VMEM((D, wide), BF16),
            pltpu.VMEM((D, gates), BF16),
            pltpu.VMEM((D, pad), BF16),
            pltpu.VMEM((group, D), BF16),
            pltpu.VMEM((group, D), BF16),
            pltpu.VMEM((group, 3 * wide), BF16),
            pltpu.VMEM((group, wide), BF16),
            pltpu.VMEM((group, pad), BF16),
            pltpu.VMEM((max(2 * group, D), max(pad, 3 * wide)), BF16),
            pltpu.VMEM((group, gates), BF16),
            pltpu.VMEM((D, pad), BF16),
            pltpu.VMEM((D, gates), BF16),
            pltpu.VMEM((D, wide), BF16),
            pltpu.VMEM((D, max(pad, 3 * wide)), BF16),
            pltpu.VMEM((D, wide), BF16),
            pltpu.VMEM((2, size, D), BF16),
            pltpu.VMEM((2, size, D), BF16),
            pltpu.VMEM((2, size, D), BF16),
            pltpu.VMEM((half, D), F32),
            pltpu.VMEM((3, half, D), BF16),
            pltpu.VMEM((half, D), F32),
            pltpu.VMEM((half, D), F32),
            pltpu.VMEM((half, D), F32),
            pltpu.VMEM((8, D), F32),
            pltpu.VMEM((8, 3 * wide), F32),
            pltpu.VMEM((16, max(D, 128 * (small.shape[0] - 16))), F32),
            pltpu.VMEM((count,) + small.shape, BF16),
            pltpu.VMEM((TP, size, 128), F32),
            pltpu.VMEM((TP, 8, size), F32),
            pltpu.VMEM((count, 8, 128), F32),
            pltpu.VMEM((lines, 8, 3 * wide), F32),
            pltpu.VMEM((2, 8, 128), F32),
            dma((4, TP + lines)),
            dma((4, 3)),
            dma((count + 1,)),
            dma((2, 4)),
            dma((2, 4)),
            dma((2, 4)),
            dma((2, 4)),
            dma((2,)),
            dma((4, TP + lines)),
            dma((4, 4)),
            regular((lines,)),
            regular((lines,)),
            dma((2, 2)),
            dma((2, 4)),
            regular((4,)),
            dma((2, 4)),
            dma((2, 4)),
            dma((2, 4)),
            dma((2, 4)),
            dma((2, 3)),
            dma((count + 1,)),
            dma((2 * lines,)),
            dma((2 * TP,)),
            dma((2,)),
        ],
        compiler_params=pltpu.CompilerParams(
            collective_id=0, has_side_effects=True, vmem_limit_bytes=63 * 1024 * 1024
        ),
        cost_estimate=pl.CostEstimate(flops=40 * 10**9, bytes_accessed=60 * 10**6, transcendentals=10**7),
        name="layer",
    )(small, aux, row, tokens, cot, wq, wo, wg, wd)


def per_device(
    count,
    tokens_in,
    segment_ids,
    d_out,
    qkv_weight,
    qkv_bias,
    out_weight,
    gating_weight,
    down_weight,
    norm_params,
    qkv_first,
    qkv_second,
    bias_first,
    bias_second,
    out_first,
    out_second,
    gating_first,
    gating_second,
    down_first,
    down_second,
    norm_first,
    norm_second,
):
    place = lax.axis_index("dp")
    rows = norm_params.shape[1]
    seq_len = tokens_in.shape[1]
    head_local = qkv_weight.shape[2]
    hidden_local = gating_weight.shape[2]
    wide = head_local // TP
    hid = hidden_local // TP
    full = hid // 128 * 128

    def cut(shard):
        return shard.astype(BF16).transpose(1, 0, 2)

    gates = gating_weight.astype(BF16).reshape(rows, 2, TP, hid)
    gates = jnp.concatenate(
        [gates[:, 0, :, :full], gates[:, 1, :, :full], gates[:, 0, :, full:], gates[:, 1, :, full:]], axis=2
    )
    downs = jnp.pad(down_weight.T.reshape(rows, TP, hid), ((0, 0), (0, 0), (0, -hid % 128)))
    weights = (
        cut(qkv_weight.reshape(rows, 3, TP, wide).transpose(0, 2, 1, 3).reshape(rows, TP, 3 * wide)),
        cut(out_weight.T.reshape(rows, TP, wide)),
        gates.transpose(1, 0, 2),
        cut(downs),
    )
    bias_here = qkv_bias.shape[1]
    small_norm = lax.dynamic_update_slice(jnp.zeros((16, 128), F32), norm_params, (0, (place * rows) % 128))
    small_bias = lax.dynamic_update_slice(jnp.zeros((3 * head_local,), F32), qkv_bias[0], (place * bias_here,))
    small = jnp.concatenate([small_norm, small_bias.reshape(-1, 128)]).astype(BF16)
    segments = segment_ids[0]
    earlier = jnp.sum((segments[None, :] < segments[:, None]).astype(jnp.int32), axis=1)
    positions = (jnp.arange(seq_len, dtype=jnp.int32) - earlier).astype(F32)
    frequency = 10000.0 ** (-2.0 * jnp.arange(ROT // 2, dtype=F32) / ROT)
    angles = positions[:, None] * frequency[None, :]
    aux = jnp.concatenate([jnp.cos(angles), jnp.sin(angles), segments[:, None].astype(F32)], axis=1)
    aux = jnp.pad(aux, ((0, 0), (0, 128 - aux.shape[1])))
    row = jnp.broadcast_to(segments.astype(F32)[None], (8, seq_len))

    rs_q, rs_o, rs_g, rs_d, block_out, input_grad, _, norm_sum, bias_sum = layer(
        count, small, aux, row, tokens_in[0], d_out[0], *weights
    )

    def total(parts):
        return parts.transpose(1, 0, 2).astype(F32)

    gating_parts = total(rs_g)
    gate_parts = jnp.concatenate([gating_parts[..., :full], gating_parts[..., 2 * full : full + hid]], axis=2)
    up_parts = jnp.concatenate([gating_parts[..., full : 2 * full], gating_parts[..., full + hid :]], axis=2)
    gating_shard = jnp.stack([gate_parts, up_parts], axis=1).reshape(gating_weight.shape)
    qkv_shard = total(rs_q).reshape(rows, TP, 3, wide).transpose(0, 2, 1, 3).reshape(qkv_weight.shape)
    out_shard = total(rs_o).reshape(rows, head_local).T
    down_shard = total(rs_d)[..., :hid].reshape(rows, hidden_local).T
    norm_grad = lax.dynamic_slice_in_dim(norm_sum[:4], (place * rows) % 128, rows, 1)
    bias_grad = bias_sum[:, 0].reshape(TP, 3, wide).transpose(1, 0, 2).reshape(1, 3 * head_local)
    bias_grad = lax.dynamic_slice_in_dim(bias_grad, place * bias_here, bias_here, 1)
    return (
        block_out[None],
        input_grad[None],
        *adamw_update(qkv_weight, qkv_shard, qkv_first, qkv_second, D ** (-0.5), 0.1),
        *adamw_update(qkv_bias, bias_grad, bias_first, bias_second, 0.3, 0.0),
        *adamw_update(out_weight, out_shard, out_first, out_second, (H * HD // 16) ** (-0.5), 0.1),
        *adamw_update(gating_weight, gating_shard, gating_first, gating_second, D ** (-0.5), 0.1),
        *adamw_update(down_weight, down_shard, down_first, down_second, FF ** (-0.5), 0.1),
        *adamw_update(norm_params, norm_grad, norm_first, norm_second, 0.25, 0.0),
    )


def solution(mesh):
    tokens = P("dp", None, None)
    qkv = P("dp", None, "tensor")
    rest = P("tensor", "dp")
    norm = P(None, "dp")
    weights = (qkv, rest, rest, qkv, rest, norm)
    states = (qkv, qkv, rest, rest, rest, rest, qkv, qkv, rest, rest, norm, norm)
    return jax.shard_map(
        functools.partial(per_device, mesh.shape["dp"]),
        mesh=mesh,
        in_specs=(tokens, P("dp", None), tokens, *weights, *states),
        out_specs=(tokens, tokens, *(spec for spec in weights for _ in range(3))),
        check_vma=False,
    )
```

time: 687 us -> 616 us (0.90)
  Pallas kernels: 582 us -> 520 us
    pallas_call x2 -> x1, Pallas kernels: 582 us -> 520 us  [layer(): pl.pallas_call(functools.partial(layer_kernel, count), in_specs=[vmem, vm...]
    unnamed x66 -> x70, local copies, waits for them, and re-layouts: 51.1 us -> 50.8 us
where the time goes in v4:
time: 616 us; the launch traced here: 615 us
  Pallas kernels  520 us (84%)
  local copies, waits for them, and re-layouts  67.4 us (11%)
  other arithmetic  26.1 us (4%)
    pallas_call x1, Pallas kernels, layer(): pl.pallas_call(functools.partial(layer_kernel, count), in_specs=[vmem, vm...  520 us
    unnamed x70, local copies, waits for them, and re-layouts  50.8 us
    sub x6, other arithmetic, adamw_update(): weight_old - step_rate * (corrected + decay_rate * weight_old)  19.7 us

profile of v4, /device:TPU:0, one launch (start us, length us, event | category | flops | bytes accessed | tf_op | source)
XLA Modules:
  0.0 615.0 jit_solution(992347150553668669)
XLA Ops:
  0.7 0.7 convert.27
  1.3 0.9 dynamic_update_slice.8
  2.2 0.6 fusion.8.small_src
  2.8 0.7 fusion.24
  3.5 0.9 convert_reduce_fusion
  4.7 0.7 pad.11.aux_src
  5.4 0.6 broadcast_in_dim.22.row_src
  6.0 1.9 copy.163
  8.0 1.0 copy-done.2
  9.0 1.2 copy.165
  10.2 0.9 copy.166
  11.0 4.1 copy.167
  15.4 1.4 copy-done
  16.8 1.1 copy-done.8
  18.3 0.3 copy.195
  18.6 0.9 fusion.22
  19.7 2.2 concatenate.19
  22.3 0.9 pad_bitcast_fusion.wd_src
  23.2 520.4 %layer.1 = (bf16[4,128,768]{2,1,0:T(8,128)(2,1)}, bf16[4,128,256]{2,1,0:T(8,128)(2,1)}, bf16[4,128,1408]{2,1,0:T(8,128)(2,1)}, bf16[4,128,768]{2,1,0:T(8,128)(2,...) custom-call(bf16[40,128]{1,0:T(8,128)(2,1)} %fusion.8.small_src, ...), custom_call_target="tpu_custom_call" | custom-call | flops 40000000000 | bytes 60000000 | tf_op jit(solution)/shard_map/layer/pallas_call | solution.py:933
  543.7 1.3 convert_bitcast_fusion.1
  544.9 0.5 copy.174
  545.4 1.3 copy.175
  546.7 0.7 copy-done.13
  547.4 1.6 copy.173
  549.0 1.6 copy.176
  550.6 5.2 multiply_subtract_fusion.1
  555.8 3.1 copy.188
  559.0 1.6 copy.189
  560.6 1.6 copy.190
  562.2 1.0 slice.38
  563.3 0.7 multiply_subtract_fusion.5
  564.2 1.4 multiply_subtract_fusion.3
  565.6 0.5 copy-done.15
  567.0 1.6 copy.183
  568.5 1.6 copy.182
  570.1 5.6 copy.181
  575.7 5.7 copy.184
  581.4 6.7 %multiply_subtract_fusion = (f32[128,2,2816]{0,2,1:T(8,128)}, f32[128,2,2816]{0,2,1:T(8,128)}, f32[128,2,2816]{0,2,1:T(8,128)}) fusion(f32[128,2,2816]{0,2,1:T(8,128)S(1)} %copy-done.1, f32[128,1,2816]{0,2,1:T(8,128)} %bitcast.75, f32[128,1,2816]{0,2,1:T(8,128)} %bitcast.76, f32[128,2,2816]{0,2,1:T(8,128)} %copy.181, f32[128,2,2816]{0,2,1:T(8,128)} %copy.184), kind=kLoop, calls=%fused_computation.4 | loop fusion | flops 11534336 | bytes 20185088 | tf_op jit(solution)/shard_map/sub | solution.py:42
  588.1 5.6 copy.191
  593.7 5.7 copy.192
  599.4 3.3 copy.193
  602.7 1.3 slice_convert_fusion
  604.0 1.6 copy.187
  605.6 5.1 multiply_subtract_fusion.2
  610.7 0.6 multiply_subtract_fusion.4
  611.3 1.3 copy.201
  612.6 1.0 copy-done.11
  613.7 1.3 copy.202
  (70 shorter events, 2.8 us)
Async XLA Ops:
  7.8 1.1 copy-start.2
  8.0 2.2 copy-start.9
  15.2 1.6 copy-start
  16.8 1.1 copy-start.8
  19.6 2.3 copy-start.6
  545.4 2.0 copy-start.13
  547.4 1.6 copy-start.14
  549.0 1.6 copy-start.3
  555.8 3.1 copy-start.5
  560.6 2.7 copy-start.20
  560.6 2.7 copy-start.24
  560.6 2.7 copy-start.25
  560.6 3.4 copy-start.18
  562.2 2.0 copy-start.10
  562.2 2.0 copy-start.16
  562.2 2.0 copy-start.17
  564.2 1.9 copy-start.15
  575.7 5.7 copy-start.1
  593.7 5.7 copy-start.4
  604.0 1.6 copy-start.7
  605.6 5.1 copy-start.19
  605.6 5.1 copy-start.21
  605.6 5.1 copy-start.22
  605.6 5.1 copy-start.23
  605.6 5.7 copy-start.12
  611.3 2.3 copy-start.11

commit v5 on v4

--- a/solution.py
+++ b/solution.py
@@ -4,6 +4,7 @@
 import jax.numpy as jnp
 from jax import lax
 from jax.experimental import pallas as pl
+from jax.experimental.layout import Layout, with_layout_constraint
 from jax.experimental.pallas import tpu as pltpu
 from jax.sharding import PartitionSpec as P
 
@@ -502,10 +503,17 @@
         )
 
     def start(self):
+        self.start_outer()
+        self.start_rest()
+
+    def start_outer(self):
         if self.free_sem is not None:
             self.line_each(lambda k, u: pl.semaphore_wait(self.free_sem.at[u], 1))
         if self.place.lines == 4:
             pl.when(self.ends())(lambda: self.outer().start())
+
+    def start_rest(self):
+        if self.place.lines == 4:
             self.line_each(lambda k, u: self.line_copy(k, u).start(), lambda u: ~self.later(u))
         else:
             self.line_each(lambda k, u: self.line_copy(k, u).start())
@@ -626,6 +634,8 @@
     def small_copy(dest):
         return remote(small_src, small.at[p.me], small_sem.at[dest], small_sem.at[count], dest, p.t)
 
+    pltpu.make_async_copy(small_src, small.at[p.me], small_sem.at[count]).start()
+    each_dest(p, lambda dest, u, j: small_copy(dest).start())
     gather_q.start()
     auxes.start()
     rowses.start()
@@ -633,14 +643,11 @@
     gather_g.start()
     gather_d.start()
     tokens.start()
-    pltpu.make_async_copy(small_src, small.at[p.me], small_sem.at[count]).start()
     gather_q.pass_on()
-    each_dest(p, lambda dest, u, j: small_copy(dest).start())
     gather_o.pass_on()
     gather_g.pass_on()
     auxes.pass_on()
     rowses.pass_on()
-    gather_d.pass_on()
     tokens.pass_on()
 
     wait_bytes(small, small_sem.at[count])
@@ -671,6 +678,7 @@
     keep_h1 = pltpu.make_async_copy(hh, h1_out, h1_sem.at[0])
     keep_h1.start()
     gather_q.arrive()
+    gather_d.pass_on()
     gather_o.relay()
     head_wide = (bias_rows * 128) // 3
 
@@ -792,9 +800,6 @@
 
     sums.release()
     spread_r.start()
-    scatter_g.combine()
-    scatter_d.reduce()
-    scatter_q.allow()
     spread_r.arrive()
 
     biases[...] = jnp.zeros_like(biases)
@@ -813,12 +818,6 @@
             qkv[at, lanes] = value
             biases[0:1, lanes] += jnp.sum(value.astype(F32), axis=0, keepdims=True)
 
-    load_h1.wait()
-    weight_grad(hh, qkv, gq)
-    scatter_q.start()
-    weight_grad(cot, att, go)
-    scatter_o.start()
-
     bias_all[p.u] = biases[...]
 
     def bias_copy(k):
@@ -828,10 +827,19 @@
     for k in range(1, p.lines):
         bias_copy(k).start()
 
+    scatter_d.reduce()
+    scatter_q.allow()
+    load_h1.wait()
+    weight_grad(hh, qkv, gq)
+    scatter_q.start_outer()
+    weight_grad(cot, att, go)
+    scatter_o.start_outer()
+    scatter_q.start_rest()
+    scatter_o.start_rest()
+    scatter_g.combine()
+
     sums.acquire()
     sums.start(lambda s, n, step: dot(qkv[rows_of(s), :], wq[columns(n, step), :], 1, 1))
-    scatter_q.combine()
-    scatter_o.combine()
     sums.arrive()
 
     @pl.loop(0, half // 32)
@@ -865,6 +873,20 @@
     pltpu.make_async_copy(gains.at[:, tile_of(p.me)], small_all.at[p.me], gain_sem.at[count]).start()
     each_dest(p, lambda dest, u, j: gain_copy(dest).start())
 
+    sums.acquire()
+    sums.start(lambda s, n, step: dot(hid[rows_of(s), :], wd[columns(n, step), :], 1, 1))
+    sums.arrive()
+
+    @pl.loop(0, half // 32)
+    def _(i):
+        at = pl.multiple_of(i * 32, 32)
+        block[pl.ds(at, 32), :] = resid[pl.ds(at, 32), :] + sums.total(at, 32)
+
+    gives += give(1, block, block_out)
+    scatter_g.reduce()
+    scatter_q.combine()
+    scatter_o.combine()
+
     for k in range(1, p.lines):
         bias_copy(k).wait_recv()
     total = bias_all[0]
@@ -878,18 +900,6 @@
 
     for q in range(1, TP):
         rank_copy(q).start()
-
-    sums.acquire()
-    sums.start(lambda s, n, step: dot(hid[rows_of(s), :], wd[columns(n, step), :], 1, 1))
-    sums.arrive()
-
-    @pl.loop(0, half // 32)
-    def _(i):
-        at = pl.multiple_of(i * 32, 32)
-        block[pl.ds(at, 32), :] = resid[pl.ds(at, 32), :] + sums.total(at, 32)
-
-    gives += give(1, block, block_out)
-    scatter_g.reduce()
 
     wait_bytes(small_all, gain_sem.at[count])
     total = small_all[0]
@@ -1012,6 +1022,10 @@
     )(small, aux, row, tokens, cot, wq, wo, wg, wd)
 
 
+def laid_out(values):
+    return with_layout_constraint(values, Layout(tuple(range(values.ndim))))
+
+
 def per_device(
     count,
     tokens_in,
@@ -1045,19 +1059,35 @@
     hid = hidden_local // TP
     full = hid // 128 * 128
 
-    def cut(shard):
-        return shard.astype(BF16).transpose(1, 0, 2)
-
-    gates = gating_weight.astype(BF16).reshape(rows, 2, TP, hid)
-    gates = jnp.concatenate(
-        [gates[:, 0, :, :full], gates[:, 1, :, :full], gates[:, 0, :, full:], gates[:, 1, :, full:]], axis=2
-    )
-    downs = jnp.pad(down_weight.T.reshape(rows, TP, hid), ((0, 0), (0, 0), (0, -hid % 128)))
+    low_gates = laid_out(gating_weight.astype(BF16))
+    heads_part, tails_part = low_gates[:, :, : TP * full], low_gates[:, :, TP * full :]
+    spare = hid - full
     weights = (
-        cut(qkv_weight.reshape(rows, 3, TP, wide).transpose(0, 2, 1, 3).reshape(rows, TP, 3 * wide)),
-        cut(out_weight.T.reshape(rows, TP, wide)),
-        gates.transpose(1, 0, 2),
-        cut(downs),
+        jnp.stack(
+            [
+                jnp.concatenate([qkv_weight[:, k, j * wide : (j + 1) * wide] for k in range(3)], axis=1)
+                for j in range(TP)
+            ]
+        ).astype(BF16),
+        out_weight.astype(BF16).reshape(TP, wide, rows).transpose(0, 2, 1),
+        jnp.stack(
+            [
+                jnp.concatenate(
+                    [heads_part[:, k, j * full : (j + 1) * full] for k in range(2)]
+                    + [tails_part[:, k, j * spare : (j + 1) * spare] for k in range(2)],
+                    axis=1,
+                )
+                for j in range(TP)
+            ]
+        ),
+        jnp.concatenate(
+            [
+                down_weight[: TP * full].astype(BF16).reshape(TP, full, rows),
+                down_weight[TP * full :].astype(BF16).reshape(TP, spare, rows),
+                jnp.zeros((TP, -hid % 128, rows), BF16),
+            ],
+            axis=1,
+        ).transpose(0, 2, 1),
     )
     bias_here = qkv_bias.shape[1]
     small_norm = lax.dynamic_update_slice(jnp.zeros((16, 128), F32), norm_params, (0, (place * rows) % 128))
@@ -1076,16 +1106,29 @@
         count, small, aux, row, tokens_in[0], d_out[0], *weights
     )
 
-    def total(parts):
-        return parts.transpose(1, 0, 2).astype(F32)
-
-    gating_parts = total(rs_g)
-    gate_parts = jnp.concatenate([gating_parts[..., :full], gating_parts[..., 2 * full : full + hid]], axis=2)
-    up_parts = jnp.concatenate([gating_parts[..., full : 2 * full], gating_parts[..., full + hid :]], axis=2)
-    gating_shard = jnp.stack([gate_parts, up_parts], axis=1).reshape(gating_weight.shape)
-    qkv_shard = total(rs_q).reshape(rows, TP, 3, wide).transpose(0, 2, 1, 3).reshape(qkv_weight.shape)
-    out_shard = total(rs_o).reshape(rows, head_local).T
-    down_shard = total(rs_d)[..., :hid].reshape(rows, hidden_local).T
+    gate_parts = [
+        jnp.concatenate(
+            [rs_g[j, :, k * full : (k + 1) * full] for j in range(TP)]
+            + [rs_g[j, :, 2 * full + k * spare : 2 * full + (k + 1) * spare] for j in range(TP)],
+            axis=1,
+        )
+        for k in range(2)
+    ]
+    gating_shard = lax.optimization_barrier(laid_out(jnp.stack(gate_parts, axis=1))).astype(F32)
+    qkv_shard = jnp.stack(
+        [
+            jnp.concatenate([rs_q[j, :, k * wide : (k + 1) * wide] for j in range(TP)], axis=1)
+            for k in range(3)
+        ],
+        axis=1,
+    ).astype(F32)
+    out_shard = laid_out(rs_o.transpose(0, 2, 1).reshape(head_local, rows)).astype(F32)
+    down_parts = rs_d.transpose(0, 2, 1)
+    down_shard = laid_out(
+        jnp.concatenate(
+            [down_parts[:, :full].reshape(TP * full, rows), down_parts[:, full:hid].reshape(TP * spare, rows)]
+        )
+    ).astype(F32)
     norm_grad = lax.dynamic_slice_in_dim(norm_sum[:4], (place * rows) % 128, rows, 1)
     bias_grad = bias_sum[:, 0].reshape(TP, 3, wide).transpose(1, 0, 2).reshape(1, 3 * head_local)
     bias_grad = lax.dynamic_slice_in_dim(bias_grad, place * bias_here, bias_here, 1)

time: 616 us -> 541 us (0.88); the launches traced: 615 us -> 532 us
  Pallas kernels: 520 us -> 470 us
  local copies, waits for them, and re-layouts: 67.4 us -> 23.2 us
  other arithmetic: 26.1 us -> 37.3 us
    pallas_call x1, Pallas kernels: 520 us -> 470 us  [layer(): pl.pallas_call(functools.partial(layer_kernel, count), in_specs=[vmem, vm...]
    unnamed x70 -> x50, local copies, waits for them, and re-layouts: 50.8 us -> 5.77 us
    another operation x2 -> x11, other arithmetic: 0.76 us -> 7.96 us  [the longest x1 3.27 us: per_device(): jnp.stack(gate_parts, axis=1)]
where the time goes in v5:
time: 541 us; the launch traced here: 532 us
  Pallas kernels  470 us (87%)
  other arithmetic  37.3 us (7%)
  local copies, waits for them, and re-layouts  23.2 us (4%)
    pallas_call x1, Pallas kernels, layer(): pl.pallas_call(functools.partial(layer_kernel, count), in_specs=[vmem, vm...  470 us
    sub x6, other arithmetic, adamw_update(): weight_old - step_rate * (corrected + decay_rate * weight_old)  24.2 us

profile of v5, /device:TPU:0, one launch (start us, length us, event | category | flops | bytes accessed | tf_op | source)
XLA Modules:
  0.0 532.5 jit_solution(13263381944203262982)
XLA Ops:
  0.7 0.7 convert.59
  1.3 0.9 dynamic_update_slice.8
  2.2 0.6 fusion.9.small_src
  2.8 0.7 fusion.24
  3.5 0.9 convert_reduce_fusion
  4.4 0.1 multiply_cosine_fusion
  4.7 0.7 pad.6.aux_src
  5.4 0.6 broadcast_in_dim.25.row_src
  6.0 1.5 convert.61
  7.7 1.0 pad_maximum_fusion.2.wq_src
  8.7 0.7 convert_element_type.54
  9.4 1.8 copy.140
  11.2 1.0 convert_element_type.55
  12.2 1.9 fusion.23
  14.0 0.7 copy_bitcast_fusion
  14.7 1.1 fusion.22
  15.9 1.0 concatenate.65
  17.0 0.9 copy_bitcast_fusion.10
  18.4 1.3 pad_maximum_fusion.wg_src
  19.7 0.5 copy-done.3
  20.3 0.1 copy.158
  20.5 0.3 copy.157
  20.9 1.0 maximum_bitcast_fusion.wd_src
  21.9 470.4 %layer.1 = (bf16[4,128,768]{2,1,0:T(8,128)(2,1)}, bf16[4,128,256]{2,1,0:T(8,128)(2,1)}, bf16[4,128,1408]{2,1,0:T(8,128)(2,1)}, bf16[4,128,768]{2,1,0:T(8,128)(2,...) custom-call(bf16[40,128]{1,0:T(8,128)(2,1)} %fusion.9.small_src, ...), custom_call_target="tpu_custom_call" | custom-call | flops 40000000000 | bytes 60000000 | tf_op jit(solution)/shard_map/layer/pallas_call | solution.py:943
  492.4 1.4 slice_bitcast_fusion.31
  493.8 0.3 copy-done.2
  494.1 0.5 copy-done.10
  494.6 4.7 multiply_subtract_fusion.1
  499.3 0.9 slice.260
  500.2 0.7 multiply_subtract_fusion.5
  500.9 0.2 copy.160
  501.1 1.4 multiply_subtract_fusion.3
  502.5 0.5 copy-done.9
  503.0 0.1 slice_bitcast_fusion.4
  503.3 0.3 concatenate.71
  503.6 1.1 copy.163
  504.7 0.3 concatenate.70
  505.0 1.1 copy.162
  506.1 3.3 pad_maximum_fusion.1
  509.4 12.1 %multiply_subtract_fusion = (f32[128,2,2816]{2,1,0:T(2,128)}, f32[128,2,2816]{2,1,0:T(2,128)}, f32[128,2,2816]{2,1,0:T(2,128)}) fusion(f32[128,2,2816]{2,1,0:T(2,128)S(1)} %copy-done.1, bf16[128,2,2816]{2,1,0:T(2,128)(2,1)S(1)} %pad_maximum_fusion.1, f32[128,2,2816]{2,1,0:T(2,128)S(1)} %copy-done.5, f32[128,2,2816]{2,1,0:T(2,128)} %param.37), kind=kLoop, calls=%fused_computation.4 | loop fusion | flops 11534336 | bytes 18743296 | tf_op jit(solution)/shard_map/sub | solution.py:43
  521.6 0.7 copy.165
  522.4 0.3 copy.164
  522.7 0.2 copy-done.4
  523.0 4.7 multiply_subtract_fusion.2
  527.8 0.6 multiply_subtract_fusion.4
  528.4 1.3 copy.201
  529.7 1.0 copy-done.6
  530.7 1.3 copy.202
  (72 shorter events, 1.3 us)
Async XLA Ops:
  7.6 1.1 copy-start.8
  7.7 3.5 copy-start
  16.9 1.1 copy-start.14
  16.9 1.1 copy-start.15
  18.4 1.8 copy-start.3
  492.3 1.8 copy-start.2
  492.4 2.2 copy-start.10
  494.6 5.6 %copy-start.18 = (f32[1,192]{1,0:T(1,128)S(1)}, f32[1,192]{1,0:T(1,128)}, u32[]{:S(2)}) copy-start(f32[1,192]{1,0:T(1,128)} %param.25) | copy-start | bytes 2308
  494.6 5.7 %copy-start.22 = (f32[1,192]{1,0:T(1,128)S(1)}, f32[1,192]{1,0:T(1,128)}, u32[]{:S(2)}) copy-start(f32[1,192]{1,0:T(1,128)} %param.32) | copy-start | bytes 2308
  494.6 5.7 %copy-start.23 = (f32[1,192]{1,0:T(1,128)S(1)}, f32[1,192]{1,0:T(1,128)}, u32[]{:S(2)}) copy-start(f32[1,192]{1,0:T(1,128)} %param.33) | copy-start | bytes 2308
  494.6 6.3 %copy-start.16 = (bf16[4,128,256]{2,1,0:T(8,128)(2,1)S(1)}, bf16[4,128,256]{2,1,0:T(8,128)(2,1)}, u32[]{:S(2)}) copy-start(bf16[4,128,256]{2,1,0:T(8,128)(2,1)} %get-tuple-element.32) | copy-start | bytes 786436
  494.6 6.5 %copy-start.12 = (f32[1024,128]{1,0:T(8,128)S(1)}, f32[1024,128]{1,0:T(8,128)}, u32[]{:S(2)}) copy-start(f32[1024,128]{1,0:T(8,128)} %param.34) | copy-start | bytes 1572868
  494.6 6.5 %copy-start.13 = (f32[1024,128]{1,0:T(8,128)S(1)}, f32[1024,128]{1,0:T(8,128)}, u32[]{:S(2)}) copy-start(f32[1024,128]{1,0:T(8,128)} %param.35) | copy-start | bytes 1572868
  501.1 1.9 copy-start.9
  505.0 4.4 copy-start.5
  506.1 3.3 copy-start.1
  509.4 12.2 %copy-start.11 = (bf16[4,128,768]{2,1,0:T(8,128)(2,1)S(1)}, bf16[4,128,768]{2,1,0:T(8,128)(2,1)}, u32[]{:S(2)}) copy-start(bf16[4,128,768]{2,1,0:T(8,128)(2,1)} %get-tuple-element.34) | copy-start | bytes 2359300
  521.6 1.4 copy-start.4
  523.0 4.8 copy-start.17
  523.0 4.8 copy-start.19
  523.0 4.8 copy-start.20
  523.0 4.8 copy-start.21
  523.0 5.4 %copy-start.7 = (f32[256,2048]{1,0:T(8,128)S(1)}, f32[256,2048]{1,0:T(8,128)}, u32[]{:S(2)}) copy-start(f32[256,2048]{1,0:T(8,128)} %get-tuple-element.28) | copy-start | bytes 6291460
  528.4 2.3 copy-start.6

commit v6 on v5

--- a/solution.py
+++ b/solution.py
@@ -189,17 +189,18 @@
     def line_copy(self, k):
         p = self.place
         u = (p.u + k) % p.lines
-        far = 0
+        sem = 0
         if p.lines == 4:
-            far = (((p.u == 0) & (u == 2)) | ((p.u == 3) & (u == 1))).astype(jnp.int32)
+            sem = jnp.where(self.middle(), jnp.where(p.u + u == 3, 3, 0), jnp.where(jnp.abs(p.u - u) == 2, 1, 0))
         mine = self.chunk(p.u)
-        return remote(mine, mine, self.send_sem.at[TP + k], self.recv_sem.at[far], u * TP + p.j, p.t)
+        return remote(mine, mine, self.send_sem.at[TP + k], self.recv_sem.at[sem], u * TP + p.j, p.t)
 
     def line_each(self, act):
         p = self.place
         if p.lines == 4:
             for k in (2, 1, 3):
-                pl.when(jnp.abs(p.u - (p.u + k) % 4) < 3)(lambda k=k: act(k))
+                gap = jnp.abs(p.u - (p.u + k) % 4)
+                pl.when((gap == 1) | ((gap == 2) & ~self.middle()))(lambda k=k: act(k))
         else:
             for k in range(1, p.lines):
                 act(k)
@@ -218,33 +219,42 @@
     def middle(self):
         return (self.place.u == 1) | (self.place.u == 2)
 
-    def forward(self):
-        p = self.place
-        chunk = self.chunk(jnp.where(p.u == 2, 0, 3))
-        dest = p.me + jnp.where(p.u == 2, TP, -TP)
-        return remote(chunk, chunk, self.send_sem.at[TP], self.recv_sem.at[1], dest, p.t)
+    def forward(self, which):
+        p = self.place
+        up = p.u == 2
+        chunk = self.chunk(jnp.where(up, which, 3 - which))
+        sem = self.send_sem.at[TP + 2 * which]
+        return remote(chunk, chunk, sem, self.recv_sem.at[1], p.me + jnp.where(up, TP, -TP), p.t)
 
     def relay(self):
         if self.place.lines == 4:
 
             @pl.when(self.middle())
             def _():
+                wait_bytes(self.chunk(0), self.recv_sem.at[3])
+                self.forward(1).start()
                 wait_bytes(self.chunk(0), self.recv_sem.at[1])
-                self.forward().start()
+                self.forward(0).start()
 
     def arrive(self):
         p = self.place
         size = TP * self.rows
-        wait_bytes(self.dst.at[pl.ds(0, size * (2 if p.lines == 4 else p.lines - 1))], self.recv_sem.at[0])
         if p.lines == 4:
-            pl.when(~self.middle())(lambda: wait_bytes(self.chunk(0), self.recv_sem.at[1]))
+            wait_bytes(self.chunk(0), self.recv_sem.at[0])
+            pl.when(~self.middle())(lambda: wait_bytes(self.dst.at[pl.ds(0, 2 * size)], self.recv_sem.at[1]))
+        else:
+            wait_bytes(self.dst.at[pl.ds(0, size * (p.lines - 1))], self.recv_sem.at[0])
 
     def finish(self):
         for q in range(1, TP):
             self.group_copy(q).wait_send()
         self.line_each(lambda k: self.line_copy(k).wait_send())
         if self.place.lines == 4:
-            pl.when(self.middle())(lambda: self.forward().wait_send())
+
+            @pl.when(self.middle())
+            def _():
+                self.forward(1).wait_send()
+                self.forward(0).wait_send()
 
 
 class GroupSum:
@@ -581,13 +591,14 @@
 
 def layer_kernel(
     count,
-    small_src, aux_src, row_src, tok_src, cot_src, wq_src, wo_src, wg_src, wd_src,
-    rs_q, rs_o, rs_g, rs_d, block_out, input_out, h1_out, norm_out, bias_out,
-    wq, wo, wg, wd, cot, hh, qkv, att, hid, slopes, dgate, gd, gg, go, slots_d, slots_o,
-    to_core, from_core, low, own, parts, grad, resid, block, gains, biases, norms,
-    small, aux_all, row_all, small_all, bias_all, small_t,
+    small_src, aux_src, row_src, tok_src, cot_src, wq_src, wo_src, wga_src, wda_src, wgb_src, wdb_src,
+    rs_q, rs_o, rs_ga, rs_da, rs_gb, rs_db, block_out, input_out, h1_out, norm_out, bias_out,
+    wq, wo, wga, wda, wgb, wdb, cot, hh, qkv, att, hid, slopes, dga, dgb, gda, gga, gdb, ggb, go,
+    slots_ga, slots_da, slots_db, slots_o,
+    to_core, from_core, low, own, parts, grad, resid, gains, biases, norms,
+    small, aux_all, row_all, small_all, bias_all, gains_t,
     w_send, w_recv, small_sem, aux_sem, row_sem, tok_sem, cot_sem, h1_sem,
-    rs_send, rs_recv, free_g, free_d, core_sem, part_sem, free_sem, part2_sem, core2_sem, part3_sem, core3_sem,
+    rs_send, rs_recv, free_g, free_q, core_sem, part_sem, free_sem, part2_sem, core2_sem, part3_sem, core3_sem,
     swap_sem, gain_sem, bias_sem, rank_sem, t_sem,
 ):
     p = Place(count)
@@ -596,7 +607,8 @@
     group = TP * size
     wide = att.shape[1]
     rows = wq_src.shape[1]
-    full = hid.shape[1] - 128
+    first = wda.shape[1]
+    second = hid.shape[1] - 128 - first
     greet(p)
 
     def rows_of(s):
@@ -607,9 +619,11 @@
 
     gathers = [
         WeightGather(p, i, src, dst, w_send, w_recv)
-        for i, (src, dst) in enumerate(((wq_src, wq), (wo_src, wo), (wg_src, wg), (wd_src, wd)))
+        for i, (src, dst) in enumerate(
+            ((wq_src, wq), (wo_src, wo), (wga_src, wga), (wda_src, wda), (wgb_src, wgb), (wdb_src, wdb))
+        )
     ]
-    gather_q, gather_o, gather_g, gather_d = gathers
+    gather_q, gather_o, gather_ga, gather_da, gather_gb, gather_db = gathers
     tok = cot
     auxes = GroupPieces(p, aux_src, aux_all, aux_sem)
     rowses = GroupPieces(p, row_src, row_all, row_sem)
@@ -619,17 +633,20 @@
     spread_h = GroupGather(p, hh, size, part2_sem, core2_sem)
     spread_r = GroupGather(p, cot, size, part3_sem, core3_sem)
     gq = slopes.at[:D, : 3 * wide]
-    scatter_q, scatter_o, scatter_g, scatter_d = [
+    scatters = [
         GradScatter(p, i, g, slots, out, rs_send, rs_recv, free)
         for i, (g, slots, out, free) in enumerate(
             (
-                (gq, slots_d.at[:, : 3 * wide], rs_q, free_d),
+                (gq, wga.at[:, : 3 * wide], rs_q, free_q),
                 (go, slots_o, rs_o, None),
-                (gg, wg, rs_g, free_g),
-                (gd, slots_d.at[:, : hid.shape[1]], rs_d, None),
+                (gga, slots_ga, rs_ga, None),
+                (gda, slots_da, rs_da, None),
+                (ggb, wgb, rs_gb, free_g),
+                (gdb, slots_db, rs_db, None),
             )
         )
     ]
+    scatter_q, scatter_o, scatter_ga, scatter_da, scatter_gb, scatter_db = scatters
 
     def small_copy(dest):
         return remote(small_src, small.at[p.me], small_sem.at[dest], small_sem.at[count], dest, p.t)
@@ -640,12 +657,13 @@
     auxes.start()
     rowses.start()
     gather_o.start()
-    gather_g.start()
-    gather_d.start()
+    for part in gathers[2:4]:
+        part.start()
     tokens.start()
-    gather_q.pass_on()
-    gather_o.pass_on()
-    gather_g.pass_on()
+    for part in gathers[4:]:
+        part.start()
+    for part in gathers[:4]:
+        part.pass_on()
     auxes.pass_on()
     rowses.pass_on()
     tokens.pass_on()
@@ -678,7 +696,8 @@
     keep_h1 = pltpu.make_async_copy(hh, h1_out, h1_sem.at[0])
     keep_h1.start()
     gather_q.arrive()
-    gather_d.pass_on()
+    gather_gb.pass_on()
+    gather_db.pass_on()
     gather_o.relay()
     head_wide = (bias_rows * 128) // 3
 
@@ -704,7 +723,7 @@
     gather_o.arrive()
     keep_h1.wait()
     sums.start(lambda s, n, step: dot(att[rows_of(s), :], wo[columns(n, step), :], 1, 1))
-    gather_g.relay()
+    gather_ga.relay()
     sums.arrive()
 
     @pl.loop(0, half // 32)
@@ -722,66 +741,89 @@
     cots.start()
     spread_h.arrive()
     cots.pass_on()
-    gather_g.arrive()
-    gather_d.relay()
-
-    @pl.loop(0, TP)
-    def _(s):
-        at = rows_of(s)
-        late = pl.ds(pl.multiple_of(group + s * size, size), size)
-        rows_in = hh[at, :]
-        gate = dot(rows_in, wg[:, :full], 1, 0)
-        up = dot(rows_in, wg[:, full : 2 * full], 1, 0)
-        sig = jax.nn.sigmoid(gate)
-        hid[at, :full] = (gate * sig * up).astype(BF16)
-        slopes[at, :full] = (up * sig * (1.0 + gate * (1.0 - sig))).astype(BF16)
-        slopes[late, :full] = (gate * sig).astype(BF16)
-        gate = dot(rows_in, wg[:, 2 * full :], 1, 0)
-        up = pltpu.roll(gate, 64, 1)
-        sig = jax.nn.sigmoid(gate)
-        first = lax.broadcasted_iota(jnp.int32, gate.shape, 1) < 64
-        tail = slice(full, full + 128)
-        hid[at, tail] = jnp.where(first, gate * sig * up, 0.0).astype(BF16)
-        slopes[at, tail] = jnp.where(first, up * sig * (1.0 + gate * (1.0 - sig)), 0.0).astype(BF16)
-        slopes[late, tail] = jnp.where(first, gate * sig, 0.0).astype(BF16)
-
-    cots.arrive()
+    gather_da.relay()
+    gather_gb.relay()
+    gather_db.relay()
     step = min(256, D)
 
     def weight_grad(left, right, out):
         @pl.loop(0, D // step)
         def _(n):
             at = columns(n, step)
-            out[at, :] = dot(left[:, at], right[...], 0, 0).astype(BF16)
-
-    weight_grad(cot, hid, gd)
-    scatter_d.start()
-
-    gather_d.arrive()
-
-    @pl.loop(0, TP)
-    def _(s):
-        at = rows_of(s)
-        late = pl.ds(pl.multiple_of(group + s * size, size), size)
-        dhid = dot(cot[at, :], wd[...], 1, 0)
-        slope = dhid * slopes[at, : hid.shape[1]].astype(F32)
-        gain = dhid * slopes[late, : hid.shape[1]].astype(F32)
-        dgate[at, :full] = slope[:, :full].astype(BF16)
-        dgate[at, full : 2 * full] = gain[:, :full].astype(BF16)
-        last = slope[:, full:] + pltpu.roll(gain[:, full:], 64, 1)
-        dgate[at, 2 * full :] = last.astype(BF16)
+            out[at, :] = dot(left[:, at], right, 0, 0).astype(BF16)
+
+    def late_rows(s):
+        return pl.ds(pl.multiple_of(group + s * size, size), size)
+
+    def hidden_part(weights, base, width, mixed):
+        @pl.loop(0, TP)
+        def _(s):
+            at, late = rows_of(s), late_rows(s)
+            rows_in = hh[at, :]
+            lanes = slice(base, base + width)
+            gate = dot(rows_in, weights[:, :width], 1, 0)
+            up = dot(rows_in, weights[:, width : 2 * width], 1, 0)
+            sig = jax.nn.sigmoid(gate)
+            hid[at, lanes] = (gate * sig * up).astype(BF16)
+            slopes[at, lanes] = (up * sig * (1.0 + gate * (1.0 - sig))).astype(BF16)
+            slopes[late, lanes] = (gate * sig).astype(BF16)
+            if mixed:
+                gate = dot(rows_in, weights[:, 2 * width :], 1, 0)
+                up = pltpu.roll(gate, 64, 1)
+                sig = jax.nn.sigmoid(gate)
+                left = lax.broadcasted_iota(jnp.int32, gate.shape, 1) < 64
+                lanes = slice(base + width, base + width + 128)
+                hid[at, lanes] = jnp.where(left, gate * sig * up, 0.0).astype(BF16)
+                slopes[at, lanes] = jnp.where(left, up * sig * (1.0 + gate * (1.0 - sig)), 0.0).astype(BF16)
+                slopes[late, lanes] = jnp.where(left, gate * sig, 0.0).astype(BF16)
+
+    def gates_part(weights, base, width, mixed, out):
+        @pl.loop(0, TP)
+        def _(s):
+            at, late = rows_of(s), late_rows(s)
+            lanes = slice(base, base + weights.shape[1])
+            dhid = dot(cot[at, :], weights[...], 1, 0)
+            slope = dhid * slopes[at, lanes].astype(F32)
+            gain = dhid * slopes[late, lanes].astype(F32)
+            out[at, :width] = slope[:, :width].astype(BF16)
+            out[at, width : 2 * width] = gain[:, :width].astype(BF16)
+            if mixed:
+                last = slope[:, width:] + pltpu.roll(gain[:, width:], 64, 1)
+                out[at, 2 * width :] = last.astype(BF16)
+
+    gather_ga.arrive()
+    hidden_part(wga, 0, first, False)
+    cots.arrive()
+    weight_grad(cot, hid[:, :first], gda)
+    scatter_da.start()
+    gather_da.arrive()
+    gates_part(wda, 0, first, False, dga)
+    weight_grad(hh, dga[...], gga)
+    scatter_ga.start()
+    gather_gb.arrive()
+    hidden_part(wgb, first, second, True)
+    weight_grad(cot, hid[:, first:], gdb)
+    scatter_db.start()
+    gather_db.arrive()
+    gates_part(wdb, first, second, True, dgb)
 
     cots.finish()
     sums.acquire()
-    sums.start(lambda s, n, step: dot(dgate[rows_of(s), :], wg[columns(n, step), :], 1, 1))
-    gather_g.finish()
-    scatter_g.allow()
-    weight_grad(hh, dgate, gg)
-    scatter_g.start()
+    sums.start(
+        lambda s, n, step: dot(dga[rows_of(s), :], wga[columns(n, step), :], 1, 1)
+        + dot(dgb[rows_of(s), :], wgb[columns(n, step), :], 1, 1)
+    )
+    gather_gb.finish()
+    gather_ga.finish()
+    scatter_gb.allow()
+    scatter_q.allow()
+    weight_grad(hh, dgb[...], ggb)
+    scatter_gb.start()
     spread_h.finish()
     load_h1 = pltpu.make_async_copy(h1_out, hh, h1_sem.at[1])
     load_h1.start()
-    scatter_d.combine()
+    scatter_da.combine()
+    scatter_ga.combine()
     sums.arrive()
 
     gains[...] = jnp.zeros_like(gains)
@@ -801,6 +843,12 @@
     sums.release()
     spread_r.start()
     spread_r.arrive()
+
+    sums.acquire()
+    sums.start(
+        lambda s, n, step: dot(hid[rows_of(s), :first], wda[columns(n, step), :], 1, 1)
+        + dot(hid[rows_of(s), first:], wdb[columns(n, step), :], 1, 1)
+    )
 
     biases[...] = jnp.zeros_like(biases)
 
@@ -827,16 +875,34 @@
     for k in range(1, p.lines):
         bias_copy(k).start()
 
-    scatter_d.reduce()
-    scatter_q.allow()
     load_h1.wait()
-    weight_grad(hh, qkv, gq)
+    weight_grad(hh, qkv[...], gq)
     scatter_q.start_outer()
-    weight_grad(cot, att, go)
+    weight_grad(cot, att[...], go)
     scatter_o.start_outer()
     scatter_q.start_rest()
     scatter_o.start_rest()
-    scatter_g.combine()
+    scatter_db.combine()
+    scatter_gb.combine()
+
+    sums.arrive()
+
+    @pl.loop(0, half // 32)
+    def _(i):
+        at = pl.multiple_of(i * 32, 32)
+        resid[pl.ds(at, 32), :] += sums.total(at, 32)
+
+    sums.release()
+    mine = pl.ds(pl.multiple_of(p.t * half, half), half)
+
+    def give(index, value, out):
+        here = pltpu.make_async_copy(value, out.at[mine], swap_sem.at[index, 0])
+        there = remote(value, out.at[mine], swap_sem.at[index, 1], swap_sem.at[index, 2], p.me, 1 - p.t)
+        here.start()
+        there.start()
+        return here, there
+
+    gives = [*give(1, resid, block_out)]
 
     sums.acquire()
     sums.start(lambda s, n, step: dot(qkv[rows_of(s), :], wq[columns(n, step), :], 1, 1))
@@ -852,17 +918,7 @@
         gains[1:2, :] += shift[None]
         grad[pl.ds(at, 32), :] += part
 
-    sums.release()
-    mine = pl.ds(pl.multiple_of(p.t * half, half), half)
-
-    def give(index, value, out):
-        here = pltpu.make_async_copy(value, out.at[mine], swap_sem.at[index, 0])
-        there = remote(value, out.at[mine], swap_sem.at[index, 1], swap_sem.at[index, 2], p.me, 1 - p.t)
-        here.start()
-        there.start()
-        return here, there
-
-    gives = [*give(0, grad, input_out)]
+    gives += give(0, grad, input_out)
 
     def tile_of(d):
         return pl.ds(pl.multiple_of(d * rows // 128 * 128, 128), 128)
@@ -870,20 +926,17 @@
     def gain_copy(dest):
         return remote(gains.at[:, tile_of(dest)], small_all.at[p.me], gain_sem.at[dest], gain_sem.at[count], dest, p.t)
 
+    swap = remote(gains, gains_t, t_sem.at[0], t_sem.at[1], p.me, 1 - p.t)
+    swap.start()
+    swap.wait()
+    gains[...] = gains[...] + gains_t[...]
     pltpu.make_async_copy(gains.at[:, tile_of(p.me)], small_all.at[p.me], gain_sem.at[count]).start()
     each_dest(p, lambda dest, u, j: gain_copy(dest).start())
 
-    sums.acquire()
-    sums.start(lambda s, n, step: dot(hid[rows_of(s), :], wd[columns(n, step), :], 1, 1))
-    sums.arrive()
-
-    @pl.loop(0, half // 32)
-    def _(i):
-        at = pl.multiple_of(i * 32, 32)
-        block[pl.ds(at, 32), :] = resid[pl.ds(at, 32), :] + sums.total(at, 32)
-
-    gives += give(1, block, block_out)
-    scatter_g.reduce()
+    scatter_da.reduce()
+    scatter_ga.reduce()
+    scatter_db.reduce()
+    scatter_gb.reduce()
     scatter_q.combine()
     scatter_o.combine()
 
@@ -901,17 +954,13 @@
     for q in range(1, TP):
         rank_copy(q).start()
 
+    scatter_q.reduce()
+    scatter_o.reduce()
     wait_bytes(small_all, gain_sem.at[count])
     total = small_all[0]
     for d in range(1, count):
         total = total + small_all[d]
-    small_t[0] = total
-    swap = remote(small_t.at[0], small_t.at[1], t_sem.at[0], t_sem.at[1], p.me, 1 - p.t)
-    swap.start()
-    scatter_q.reduce()
-    scatter_o.reduce()
-    swap.wait()
-    norm_out[...] = small_t[0] + small_t[1]
+    norm_out[...] = total
     for q in range(1, TP):
         rank_copy(q).wait()
     for k in range(1, p.lines):
@@ -920,18 +969,19 @@
     each_dest(p, lambda dest, u, j: gain_copy(dest).wait_send())
     for copy in gives:
         copy.wait()
-    for part in (auxes, rowses, sums, spread_r, gather_q, gather_o, gather_d):
+    for part in (auxes, rowses, sums, spread_r, gather_q, gather_o, gather_da, gather_db):
         part.finish()
-    for scatter in (scatter_d, scatter_g, scatter_q, scatter_o):
+    for scatter in scatters:
         scatter.finish()
 
 
-def layer(count, small, aux, row, tokens, cot, wq, wo, wg, wd):
+def layer(count, small, aux, row, tokens, cot, *weights):
     size = tokens.shape[0]
     half = size // 2
     group = TP * size
-    lines, rows = count // TP, wq.shape[1]
-    wide, pad, gates = wo.shape[2], wd.shape[2], wg.shape[2]
+    lines, rows = count // TP, weights[0].shape[1]
+    _, wide, gates_a, hid_a, gates_b, hid_b = [w.shape[2] for w in weights]
+    pad = hid_a + hid_b
     any_spec = pl.BlockSpec(memory_space=pl.ANY)
     vmem = pl.BlockSpec(memory_space=pltpu.VMEM)
     dma = pltpu.SemaphoreType.DMA
@@ -942,13 +992,10 @@
 
     return pl.pallas_call(
         functools.partial(layer_kernel, count),
-        in_specs=[vmem, vmem, vmem, vmem] + [any_spec] * 5,
-        out_specs=[any_spec] * 7 + [vmem] * 2,
+        in_specs=[vmem, vmem, vmem, vmem] + [any_spec] * 7,
+        out_specs=[any_spec] * 9 + [vmem] * 2,
         out_shape=[
-            out(TP, rows, 3 * wide),
-            out(TP, rows, wide),
-            out(TP, rows, gates),
-            out(TP, rows, pad),
+            *[out(TP, rows, w.shape[2]) for w in weights],
             out(size, D, dtype=F32),
             out(size, D, dtype=F32),
             out(group, D),
@@ -956,28 +1003,29 @@
             out(TP, 8, 3 * wide, dtype=F32),
         ],
         scratch_shapes=[
-            pltpu.VMEM((D, 3 * wide), BF16),
-            pltpu.VMEM((D, wide), BF16),
-            pltpu.VMEM((D, gates), BF16),
-            pltpu.VMEM((D, pad), BF16),
+            *[pltpu.VMEM((D, w.shape[2]), BF16) for w in weights],
             pltpu.VMEM((group, D), BF16),
             pltpu.VMEM((group, D), BF16),
             pltpu.VMEM((group, 3 * wide), BF16),
             pltpu.VMEM((group, wide), BF16),
             pltpu.VMEM((group, pad), BF16),
             pltpu.VMEM((max(2 * group, D), max(pad, 3 * wide)), BF16),
-            pltpu.VMEM((group, gates), BF16),
-            pltpu.VMEM((D, pad), BF16),
-            pltpu.VMEM((D, gates), BF16),
+            pltpu.VMEM((group, gates_a), BF16),
+            pltpu.VMEM((group, gates_b), BF16),
+            pltpu.VMEM((D, hid_a), BF16),
+            pltpu.VMEM((D, gates_a), BF16),
+            pltpu.VMEM((D, hid_b), BF16),
+            pltpu.VMEM((D, gates_b), BF16),
             pltpu.VMEM((D, wide), BF16),
-            pltpu.VMEM((D, max(pad, 3 * wide)), BF16),
+            pltpu.VMEM((D, gates_a), BF16),
+            pltpu.VMEM((D, hid_a), BF16),
+            pltpu.VMEM((D, hid_b), BF16),
             pltpu.VMEM((D, wide), BF16),
             pltpu.VMEM((2, size, D), BF16),
             pltpu.VMEM((2, size, D), BF16),
             pltpu.VMEM((2, size, D), BF16),
             pltpu.VMEM((half, D), F32),
             pltpu.VMEM((3, half, D), BF16),
-            pltpu.VMEM((half, D), F32),
             pltpu.VMEM((half, D), F32),
             pltpu.VMEM((half, D), F32),
             pltpu.VMEM((8, D), F32),
@@ -988,17 +1036,17 @@
             pltpu.VMEM((TP, 8, size), F32),
             pltpu.VMEM((count, 8, 128), F32),
             pltpu.VMEM((lines, 8, 3 * wide), F32),
-            pltpu.VMEM((2, 8, 128), F32),
-            dma((4, TP + lines)),
-            dma((4, 3)),
+            pltpu.VMEM((8, D), F32),
+            dma((6, TP + lines)),
+            dma((6, 4)),
             dma((count + 1,)),
             dma((2, 4)),
             dma((2, 4)),
             dma((2, 4)),
             dma((2, 4)),
             dma((2,)),
-            dma((4, TP + lines)),
-            dma((4, 4)),
+            dma((6, TP + lines)),
+            dma((6, 4)),
             regular((lines,)),
             regular((lines,)),
             dma((2, 2)),
@@ -1019,7 +1067,7 @@
         ),
         cost_estimate=pl.CostEstimate(flops=40 * 10**9, bytes_accessed=60 * 10**6, transcendentals=10**7),
         name="layer",
-    )(small, aux, row, tokens, cot, wq, wo, wg, wd)
+    )(small, aux, row, tokens, cot, *weights)
 
 
 def laid_out(values):
@@ -1060,30 +1108,28 @@
     full = hid // 128 * 128
 
     low_gates = laid_out(gating_weight.astype(BF16))
-    heads_part, tails_part = low_gates[:, :, : TP * full], low_gates[:, :, TP * full :]
+    first = -(-(full // 2) // 128) * 128
     spare = hid - full
+
+    def gate_cut(k, start, width):
+        return [low_gates[:, k, j * width + start : (j + 1) * width + start] for j in range(TP)]
+
+    def ranks(parts):
+        return jnp.stack([jnp.concatenate(one, axis=1) for one in zip(*parts, strict=True)])
+
+    low_down = down_weight.astype(BF16)
+    down_full = low_down[: TP * full].reshape(TP, full, rows)
+    gate_full = [[low_gates[:, k, j * full : (j + 1) * full] for j in range(TP)] for k in range(2)]
     weights = (
-        jnp.stack(
-            [
-                jnp.concatenate([qkv_weight[:, k, j * wide : (j + 1) * wide] for k in range(3)], axis=1)
-                for j in range(TP)
-            ]
-        ).astype(BF16),
+        ranks([[qkv_weight[:, k, j * wide : (j + 1) * wide] for j in range(TP)] for k in range(3)]).astype(BF16),
         out_weight.astype(BF16).reshape(TP, wide, rows).transpose(0, 2, 1),
-        jnp.stack(
-            [
-                jnp.concatenate(
-                    [heads_part[:, k, j * full : (j + 1) * full] for k in range(2)]
-                    + [tails_part[:, k, j * spare : (j + 1) * spare] for k in range(2)],
-                    axis=1,
-                )
-                for j in range(TP)
-            ]
-        ),
+        ranks([[part[:, :first] for part in gate_full[k]] for k in range(2)]),
+        down_full[:, :first].transpose(0, 2, 1),
+        ranks([[part[:, first:] for part in gate_full[k]] for k in range(2)] + [gate_cut(k, TP * full, spare) for k in range(2)]),
         jnp.concatenate(
             [
-                down_weight[: TP * full].astype(BF16).reshape(TP, full, rows),
-                down_weight[TP * full :].astype(BF16).reshape(TP, spare, rows),
+                down_full[:, first:],
+                low_down[TP * full :].reshape(TP, spare, rows),
                 jnp.zeros((TP, -hid % 128, rows), BF16),
             ],
             axis=1,
@@ -1102,14 +1148,22 @@
     aux = jnp.pad(aux, ((0, 0), (0, 128 - aux.shape[1])))
     row = jnp.broadcast_to(segments.astype(F32)[None], (8, seq_len))
 
-    rs_q, rs_o, rs_g, rs_d, block_out, input_grad, _, norm_sum, bias_sum = layer(
+    rs_q, rs_o, rs_ga, rs_da, rs_gb, rs_db, block_out, input_grad, _, norm_sum, bias_sum = layer(
         count, small, aux, row, tokens_in[0], d_out[0], *weights
     )
 
+    second = full - first
     gate_parts = [
         jnp.concatenate(
-            [rs_g[j, :, k * full : (k + 1) * full] for j in range(TP)]
-            + [rs_g[j, :, 2 * full + k * spare : 2 * full + (k + 1) * spare] for j in range(TP)],
+            [
+                part
+                for j in range(TP)
+                for part in (
+                    rs_ga[j, :, k * first : (k + 1) * first],
+                    rs_gb[j, :, k * second : (k + 1) * second],
+                )
+            ]
+            + [rs_gb[j, :, 2 * second + k * spare : 2 * second + (k + 1) * spare] for j in range(TP)],
             axis=1,
         )
         for k in range(2)
@@ -1123,7 +1177,7 @@
         axis=1,
     ).astype(F32)
     out_shard = laid_out(rs_o.transpose(0, 2, 1).reshape(head_local, rows)).astype(F32)
-    down_parts = rs_d.transpose(0, 2, 1)
+    down_parts = jnp.concatenate([rs_da, rs_db], axis=2).transpose(0, 2, 1)
     down_shard = laid_out(
         jnp.concatenate(
             [down_parts[:, :full].reshape(TP * full, rows), down_parts[:, full:hid].reshape(TP * spare, rows)]

time: 541 us -> 529 us (0.978)
  Pallas kernels: 470 us -> 449 us
  local copies, waits for them, and re-layouts: 23.2 us -> 29.2 us
    pallas_call x1, Pallas kernels: 470 us -> 449 us  [layer(): pl.pallas_call(functools.partial(layer_kernel, count), in_specs=[vmem, vm...]
    slice x4 -> x22, local copies, waits for them, and re-layouts: 3.05 us -> 9.26 us  [the longest x8 5.93 us: per_device(): part[:, first:]]
where the time goes in v6:
time: 529 us; the launch traced here: 520 us
  Pallas kernels  449 us (85%)
  other arithmetic  39.3 us (7%)
  local copies, waits for them, and re-layouts  29.2 us (6%)
    pallas_call x1, Pallas kernels, layer(): pl.pallas_call(functools.partial(layer_kernel, count), in_specs=[vmem, vm...  449 us
    sub x6, other arithmetic, adamw_update(): weight_old - step_rate * (corrected + decay_rate * weight_old)  24.2 us

profile of v6, /device:TPU:0, one launch (start us, length us, event | category | flops | bytes accessed | tf_op | source)
XLA Modules:
  0.0 519.7 jit_solution(13632064604090327875)
XLA Ops:
  0.7 0.7 convert.55
  1.3 0.9 dynamic_update_slice.8
  2.2 0.6 fusion.9.small_src
  2.8 0.7 fusion.24
  3.5 0.9 convert_reduce_fusion
  4.7 0.7 pad.6.aux_src
  5.4 0.6 broadcast_in_dim.25.row_src
  6.0 1.5 convert.57
  7.7 1.0 pad_maximum_fusion.1.wq_src
  8.7 0.9 copy.143
  9.5 2.8 convert_element_type.56
  12.3 1.9 fusion.23
  14.4 0.6 copy-done.16
  15.2 0.6 copy-done.14
  16.0 0.6 copy-done.11
  16.7 1.0 pad_maximum_fusion.2.wga_src
  17.8 0.8 slice.393
  18.6 1.9 copy.178
  20.5 0.5 fusion.22
  21.0 0.8 slice.407
  21.9 0.8 slice.406
  22.8 0.8 slice.403
  23.7 0.8 slice.402
  24.6 0.8 slice.399
  25.5 0.8 slice.398
  26.4 0.8 slice.395
  27.4 0.9 pad_maximum_fusion.5.wgb_src
  28.7 0.8 maximum_bitcast_fusion.1.wdb_src
  29.6 449.4 %layer.1 = (bf16[4,128,768]{2,1,0:T(8,128)(2,1)}, bf16[4,128,256]{2,1,0:T(8,128)(2,1)}, bf16[4,128,768]{2,1,0:T(8,128)(2,1)}, bf16[4,128,384]{2,1,0:T(8,128)(2,1...) custom-call(bf16[40,128]{1,0:T(8,128)(2,1)} %fusion.9.small_src, ...), custom_call_target="tpu_custom_call" | custom-call | flops 40000000000 | bytes 60000000 | tf_op jit(solution)/shard_map/layer/pallas_call | solution.py:993
  479.0 1.4 slice_bitcast_fusion.39
  480.8 0.5 copy-done.8
  481.3 4.7 multiply_subtract_fusion.1
  485.9 0.9 slice.336
  486.9 0.7 multiply_subtract_fusion.5
  487.8 1.4 multiply_subtract_fusion.3
  489.3 1.0 copy-done.9
  490.4 0.3 concatenate.90
  490.7 1.1 copy.167
  492.2 1.1 copy.166
  493.3 3.3 pad_maximum_fusion
  496.6 12.1 %multiply_subtract_fusion = (f32[128,2,2816]{2,1,0:T(2,128)}, f32[128,2,2816]{2,1,0:T(2,128)}, f32[128,2,2816]{2,1,0:T(2,128)}) fusion(f32[128,2,2816]{2,1,0:T(2,128)S(1)} %copy-done, bf16[128,2,2816]{2,1,0:T(2,128)(2,1)S(1)} %pad_maximum_fusion, f32[128,2,2816]{2,1,0:T(2,128)S(1)} %copy-done.4, f32[128,2,2816]{2,1,0:T(2,128)} %param.37), kind=kLoop, calls=%fused_computation.4 | loop fusion | flops 11534336 | bytes 18743296 | tf_op jit(solution)/shard_map/sub | solution.py:43
  509.1 0.3 copy.168
  509.4 0.8 copy-done.3
  510.2 4.7 multiply_subtract_fusion.2
  515.0 0.6 multiply_subtract_fusion.4
  515.6 1.3 copy.207
  516.9 1.0 copy-done.5
  517.9 1.3 copy.208
  (110 shorter events, 3.2 us)
Async XLA Ops:
  7.6 1.1 copy-start.7
  14.3 0.7 copy-start.16
  14.3 0.7 copy-start.17
  15.1 0.7 copy-start.14
  15.1 0.7 copy-start.15
  15.8 0.8 copy-start.12
  15.8 0.8 copy-start.13
  15.9 1.8 copy-start.2
  16.0 0.7 copy-start.11
  479.0 1.8 copy-start.1
  479.0 2.2 copy-start.8
  481.2 5.6 %copy-start.24 = (f32[1,192]{1,0:T(1,128)S(1)}, f32[1,192]{1,0:T(1,128)}, u32[]{:S(2)}) copy-start(f32[1,192]{1,0:T(1,128)} %param.25) | copy-start | bytes 2308
  481.2 5.7 %copy-start.28 = (f32[1,192]{1,0:T(1,128)S(1)}, f32[1,192]{1,0:T(1,128)}, u32[]{:S(2)}) copy-start(f32[1,192]{1,0:T(1,128)} %param.32) | copy-start | bytes 2308
  481.2 5.7 %copy-start.29 = (f32[1,192]{1,0:T(1,128)S(1)}, f32[1,192]{1,0:T(1,128)}, u32[]{:S(2)}) copy-start(f32[1,192]{1,0:T(1,128)} %param.33) | copy-start | bytes 2308
  481.2 6.3 %copy-start.22 = (bf16[4,128,256]{2,1,0:T(8,128)(2,1)S(1)}, bf16[4,128,256]{2,1,0:T(8,128)(2,1)}, u32[]{:S(2)}) copy-start(bf16[4,128,256]{2,1,0:T(8,128)(2,1)} %get-tuple-element.34) | copy-start | bytes 786436
  481.2 6.5 %copy-start.18 = (f32[1024,128]{1,0:T(8,128)S(1)}, f32[1024,128]{1,0:T(8,128)}, u32[]{:S(2)}) copy-start(f32[1024,128]{1,0:T(8,128)} %param.34) | copy-start | bytes 1572868
  481.3 6.5 %copy-start.19 = (f32[1024,128]{1,0:T(8,128)S(1)}, f32[1024,128]{1,0:T(8,128)}, u32[]{:S(2)}) copy-start(f32[1024,128]{1,0:T(8,128)} %param.35) | copy-start | bytes 1572868
  487.8 1.4 copy-start.10
  489.2 1.1 copy-start.9
  492.2 4.4 copy-start.4
  493.3 3.3 copy-start
  496.6 12.2 %copy-start.20 = (bf16[4,128,384]{2,1,0:T(8,128)(2,1)S(1)}, bf16[4,128,384]{2,1,0:T(8,128)(2,1)}, u32[]{:S(2)}) copy-start(bf16[4,128,384]{2,1,0:T(8,128)(2,1)} %get-tuple-element.37) | copy-start | bytes 1179652
  496.6 12.2 %copy-start.21 = (bf16[4,128,384]{2,1,0:T(8,128)(2,1)S(1)}, bf16[4,128,384]{2,1,0:T(8,128)(2,1)}, u32[]{:S(2)}) copy-start(bf16[4,128,384]{2,1,0:T(8,128)(2,1)} %get-tuple-element.38) | copy-start | bytes 1179652
  508.8 1.4 copy-start.3
  510.2 4.7 copy-start.23
  510.2 4.7 copy-start.25
  510.2 4.7 copy-start.26
  510.2 4.7 copy-start.27
  510.2 5.4 %copy-start.6 = (f32[256,2048]{1,0:T(8,128)S(1)}, f32[256,2048]{1,0:T(8,128)}, u32[]{:S(2)}) copy-start(f32[256,2048]{1,0:T(8,128)} %get-tuple-element.30) | copy-start | bytes 6291460
  515.6 2.3 copy-start.5

commit v7 on v6

--- a/solution.py
+++ b/solution.py
@@ -1070,6 +1070,217 @@
     )(small, aux, row, tokens, cot, *weights)
 
 
+def prepare_kernel(
+    first, *refs,
+):
+    ins, outs = refs[:7], refs[7:16]
+    held, made = refs[16:23], refs[23:32]
+    lines, in_sem, out_sem = refs[32:]
+    loads = [pltpu.make_async_copy(ref, here, in_sem.at[i]) for i, (ref, here) in enumerate(zip(ins, held))]
+    stores = [pltpu.make_async_copy(here, ref, out_sem.at[i]) for i, (here, ref) in enumerate(zip(made, outs))]
+    for copy in loads:
+        copy.start()
+    seg_ref, norm_ref, bias_ref, qkv_ref, out_ref, gates_ref, down_ref = held
+    small, aux, row, wq, wo, wga, wda, wgb, wdb = made
+    for copy in loads[:3]:
+        copy.wait()
+    size = seg_ref.shape[1]
+    wide, second = wo.shape[2], (wgb.shape[2] - 128) // 2
+    full = first + second
+    me = lax.axis_index("dp")
+
+    start = me * bias_ref.shape[1]
+    wrapped = jnp.concatenate([bias_ref[...], jnp.zeros((1, 256 - bias_ref.shape[1]), F32)], axis=1)
+    wrapped = pltpu.roll(jnp.broadcast_to(wrapped, (8, 256)), start % 128, 1)
+    lines[...] = jnp.zeros_like(lines)
+    lines[0:4, :] = norm_ref[...]
+    lines[pl.ds(16 + start // 128, 1), :] = wrapped[0:1, :128]
+    lines[pl.ds(17 + start // 128, 1), :] = wrapped[0:1, 128:]
+    small[...] = lines[...].astype(BF16)
+
+    seg = seg_ref[...].astype(F32)
+    row[...] = jnp.broadcast_to(seg, row.shape)
+    column = jnp.transpose(jnp.broadcast_to(seg, (128, size)))
+    earlier = jnp.sum((seg < column[:, 0:1]).astype(F32), axis=1, keepdims=True)
+    position = lax.broadcasted_iota(jnp.int32, (size, 128), 0).astype(F32) - earlier
+    lane = lax.broadcasted_iota(jnp.int32, (size, 128), 1)
+    half = ROT // 2
+    frequency = jnp.zeros((size, 128), F32)
+    for k in range(half):
+        frequency = jnp.where(lane % half == k, 10000.0 ** (-2.0 * k / ROT), frequency)
+    angles = position * frequency
+    turned = jnp.where(lane < half, jnp.cos(angles), jnp.sin(angles))
+    aux[...] = jnp.where(lane < ROT, turned, jnp.where(lane == ROT, column, 0.0))
+
+    left = lax.broadcasted_iota(jnp.int32, (wq.shape[1], 128), 1) < 64
+    for copy in stores[:3]:
+        copy.start()
+    loads[3].wait()
+    for j in range(TP):
+        for k in range(3):
+            wq[j, :, k * wide : (k + 1) * wide] = qkv_ref[k, :, j * wide : (j + 1) * wide].astype(BF16)
+    stores[3].start()
+    loads[4].wait()
+    for j in range(TP):
+        wo[j] = jnp.transpose(out_ref[j * wide : (j + 1) * wide, :]).astype(BF16)
+    stores[4].start()
+    loads[5].wait()
+    for j in range(TP):
+        for k in range(2):
+            begin = j * full
+            wga[j, :, k * first : (k + 1) * first] = gates_ref[:, k, begin : begin + first].astype(BF16)
+            wgb[j, :, k * second : (k + 1) * second] = gates_ref[:, k, begin + first : begin + full].astype(BF16)
+        tile = slice(TP * full + j // 2 * 128, TP * full + j // 2 * 128 + 128)
+        gate, up = gates_ref[:, 0, tile], gates_ref[:, 1, tile]
+        if j % 2:
+            gate = pltpu.roll(gate, 64, 1)
+        else:
+            up = pltpu.roll(up, 64, 1)
+        wgb[j, :, 2 * second :] = jnp.where(left, gate, up).astype(BF16)
+    stores[5].start()
+    stores[7].start()
+    loads[6].wait()
+    for j in range(TP):
+        wda[j] = jnp.transpose(down_ref[j * full : j * full + first, :]).astype(BF16)
+        wdb[j, :, :second] = jnp.transpose(down_ref[j * full + first : (j + 1) * full, :]).astype(BF16)
+        tile = slice(TP * full + j // 2 * 128, TP * full + j // 2 * 128 + 128)
+        tail = jnp.transpose(down_ref[tile, :])
+        if j % 2:
+            tail = pltpu.roll(tail, 64, 1)
+        wdb[j, :, second:] = jnp.where(left, tail, 0.0).astype(BF16)
+    stores[6].start()
+    stores[8].start()
+    for copy in stores:
+        copy.wait()
+
+
+def prepare(first, seg, norm, bias, qkv, out, gates, down):
+    rows, size = norm.shape[1], seg.shape[1]
+    wide, hid = qkv.shape[2] // TP, down.shape[0] // TP
+    second = hid // 128 * 128 - first
+    lines = 16 + 3 * qkv.shape[2] // 128
+
+    def shape(*dims, dtype=BF16):
+        return jax.ShapeDtypeStruct(dims, dtype)
+
+    given = (seg, norm, bias, qkv, out, gates, down)
+    shapes = [
+        shape(lines, 128),
+        shape(size, 128, dtype=F32),
+        shape(8, size, dtype=F32),
+        shape(TP, rows, 3 * wide),
+        shape(TP, rows, wide),
+        shape(TP, rows, 2 * first),
+        shape(TP, rows, first),
+        shape(TP, rows, 2 * second + 128),
+        shape(TP, rows, second + 128),
+    ]
+    return pl.pallas_call(
+        functools.partial(prepare_kernel, first),
+        in_specs=[pl.BlockSpec(memory_space=pl.ANY)] * 7,
+        out_specs=[pl.BlockSpec(memory_space=pl.ANY)] * 9,
+        out_shape=shapes,
+        scratch_shapes=[pltpu.VMEM(x.shape, x.dtype) for x in (*given, *shapes)]
+        + [pltpu.VMEM((lines, 128), F32), pltpu.SemaphoreType.DMA((7,)), pltpu.SemaphoreType.DMA((9,))],
+        compiler_params=pltpu.CompilerParams(vmem_limit_bytes=60 * 1024 * 1024),
+        name="prepare",
+    )(*given)
+
+
+def step_weights(weight, first, second, gradient, step_rate, decay_rate):
+    first = 0.9 * first + 0.1 * gradient
+    second = 0.95 * second + 0.05 * gradient * gradient
+    corrected = first * (1.0 / (1.0 - 0.9**STEP)) / (jnp.sqrt(second * (1.0 / (1.0 - 0.95**STEP))) + 1e-08)
+    return weight - step_rate * (corrected + decay_rate * weight), first, second
+
+
+def update_kernel(*refs):
+    ins, outs = refs[:18], refs[18:30]
+    held = refs[30:48]
+    in_sem, out_sem = refs[48:]
+    loads = [pltpu.make_async_copy(ref, here, in_sem.at[i]) for i, (ref, here) in enumerate(zip(ins, held))]
+    for copy in loads:
+        copy.start()
+    rs_q, rs_o, rs_ga, rs_gb, rs_da, rs_db = held[:6]
+    states = [held[6 + 3 * i : 9 + 3 * i] for i in range(4)]
+    stores = [
+        pltpu.make_async_copy(here, ref, out_sem.at[i]) for i, (here, ref) in enumerate(zip(held[6:], outs))
+    ]
+
+    def ready(index, *gradients):
+        for i in (*gradients, *range(6 + 3 * index, 9 + 3 * index)):
+            loads[i].wait()
+
+    def done(index):
+        for copy in stores[3 * index : 3 * index + 3]:
+            copy.start()
+
+    def change(index, at, gradient, rate):
+        new = step_weights(*(ref[at] for ref in states[index]), gradient, rate, 0.1)
+        for ref, value in zip(states[index], new):
+            ref[at] = value
+
+    every = slice(None)
+    wide = rs_o.shape[2]
+    first, second = rs_da.shape[2], rs_db.shape[2] - 128
+    full = first + second
+    left = lax.broadcasted_iota(jnp.int32, (rs_gb.shape[1], 128), 1) < 64
+
+    ready(0, 0)
+    for k in range(3):
+        for j in range(TP):
+            gradient = rs_q[j, :, k * wide : (k + 1) * wide].astype(F32)
+            change(0, (k, every, slice(j * wide, (j + 1) * wide)), gradient, D ** (-0.5))
+    done(0)
+    ready(2, 2, 3)
+    for j in range(TP):
+        for k in range(2):
+            begin = j * full
+            gradient = rs_ga[j, :, k * first : (k + 1) * first].astype(F32)
+            change(2, (every, k, slice(begin, begin + first)), gradient, D ** (-0.5))
+            gradient = rs_gb[j, :, k * second : (k + 1) * second].astype(F32)
+            change(2, (every, k, slice(begin + first, begin + full)), gradient, D ** (-0.5))
+    for i in range(TP // 2):
+        even = rs_gb[2 * i, :, 2 * second :].astype(F32)
+        odd = rs_gb[2 * i + 1, :, 2 * second :].astype(F32)
+        tile = slice(TP * full + i * 128, TP * full + (i + 1) * 128)
+        change(2, (every, 0, tile), jnp.where(left, even, pltpu.roll(odd, 64, 1)), D ** (-0.5))
+        change(2, (every, 1, tile), jnp.where(left, pltpu.roll(even, 64, 1), odd), D ** (-0.5))
+    done(2)
+    ready(3, 4, 5)
+    for j in range(TP):
+        begin = j * full
+        gradient = jnp.transpose(rs_da[j].astype(F32))
+        change(3, (slice(begin, begin + first), every), gradient, FF ** (-0.5))
+        gradient = jnp.transpose(rs_db[j].astype(F32))
+        change(3, (slice(begin + first, begin + full), every), gradient[:second], FF ** (-0.5))
+        begin = TP * full + j * 64
+        change(3, (slice(begin, begin + 64), every), gradient[second : second + 64], FF ** (-0.5))
+    done(3)
+    ready(1, 1)
+    for j in range(TP):
+        gradient = jnp.transpose(rs_o[j].astype(F32))
+        change(1, (slice(j * wide, (j + 1) * wide), every), gradient, (H * HD // 16) ** (-0.5))
+    done(1)
+    for copy in stores:
+        copy.wait()
+
+
+def update(gradients, states):
+    given = (*gradients, *states)
+    any_spec = pl.BlockSpec(memory_space=pl.ANY)
+    return pl.pallas_call(
+        update_kernel,
+        in_specs=[any_spec] * 18,
+        out_specs=[any_spec] * 12,
+        out_shape=[jax.ShapeDtypeStruct(x.shape, x.dtype) for x in states],
+        scratch_shapes=[pltpu.VMEM(x.shape, x.dtype) for x in given]
+        + [pltpu.SemaphoreType.DMA((18,)), pltpu.SemaphoreType.DMA((12,))],
+        compiler_params=pltpu.CompilerParams(vmem_limit_bytes=60 * 1024 * 1024),
+        name="update",
+    )(*given)
+
+
 def laid_out(values):
     return with_layout_constraint(values, Layout(tuple(range(values.ndim))))
 
@@ -1107,93 +1318,111 @@
     hid = hidden_local // TP
     full = hid // 128 * 128
 
-    low_gates = laid_out(gating_weight.astype(BF16))
     first = -(-(full // 2) // 128) * 128
     spare = hid - full
-
-    def gate_cut(k, start, width):
-        return [low_gates[:, k, j * width + start : (j + 1) * width + start] for j in range(TP)]
-
-    def ranks(parts):
-        return jnp.stack([jnp.concatenate(one, axis=1) for one in zip(*parts, strict=True)])
-
-    low_down = down_weight.astype(BF16)
-    down_full = low_down[: TP * full].reshape(TP, full, rows)
-    gate_full = [[low_gates[:, k, j * full : (j + 1) * full] for j in range(TP)] for k in range(2)]
-    weights = (
-        ranks([[qkv_weight[:, k, j * wide : (j + 1) * wide] for j in range(TP)] for k in range(3)]).astype(BF16),
-        out_weight.astype(BF16).reshape(TP, wide, rows).transpose(0, 2, 1),
-        ranks([[part[:, :first] for part in gate_full[k]] for k in range(2)]),
-        down_full[:, :first].transpose(0, 2, 1),
-        ranks([[part[:, first:] for part in gate_full[k]] for k in range(2)] + [gate_cut(k, TP * full, spare) for k in range(2)]),
-        jnp.concatenate(
-            [
-                down_full[:, first:],
-                low_down[TP * full :].reshape(TP, spare, rows),
-                jnp.zeros((TP, -hid % 128, rows), BF16),
-            ],
-            axis=1,
-        ).transpose(0, 2, 1),
-    )
     bias_here = qkv_bias.shape[1]
-    small_norm = lax.dynamic_update_slice(jnp.zeros((16, 128), F32), norm_params, (0, (place * rows) % 128))
-    small_bias = lax.dynamic_update_slice(jnp.zeros((3 * head_local,), F32), qkv_bias[0], (place * bias_here,))
-    small = jnp.concatenate([small_norm, small_bias.reshape(-1, 128)]).astype(BF16)
-    segments = segment_ids[0]
-    earlier = jnp.sum((segments[None, :] < segments[:, None]).astype(jnp.int32), axis=1)
-    positions = (jnp.arange(seq_len, dtype=jnp.int32) - earlier).astype(F32)
-    frequency = 10000.0 ** (-2.0 * jnp.arange(ROT // 2, dtype=F32) / ROT)
-    angles = positions[:, None] * frequency[None, :]
-    aux = jnp.concatenate([jnp.cos(angles), jnp.sin(angles), segments[:, None].astype(F32)], axis=1)
-    aux = jnp.pad(aux, ((0, 0), (0, 128 - aux.shape[1])))
-    row = jnp.broadcast_to(segments.astype(F32)[None], (8, seq_len))
+    if rows % 128 == 0 and spare == 64 and bias_here <= 192:
+        small, aux, row, *weights = prepare(
+            first, segment_ids, norm_params, qkv_bias, qkv_weight.transpose(1, 0, 2), out_weight, gating_weight, down_weight
+        )
+    else:
+        low_gates = laid_out(gating_weight.astype(BF16))
+
+        def gate_cut(k, start, width):
+            return [low_gates[:, k, j * width + start : (j + 1) * width + start] for j in range(TP)]
+
+        def ranks(parts):
+            return jnp.stack([jnp.concatenate(one, axis=1) for one in zip(*parts, strict=True)])
+
+        low_down = down_weight.astype(BF16)
+        down_full = low_down[: TP * full].reshape(TP, full, rows)
+        gate_full = [[low_gates[:, k, j * full : (j + 1) * full] for j in range(TP)] for k in range(2)]
+        weights = (
+            ranks([[qkv_weight[:, k, j * wide : (j + 1) * wide] for j in range(TP)] for k in range(3)]).astype(BF16),
+            out_weight.astype(BF16).reshape(TP, wide, rows).transpose(0, 2, 1),
+            ranks([[part[:, :first] for part in gate_full[k]] for k in range(2)]),
+            down_full[:, :first].transpose(0, 2, 1),
+            ranks([[part[:, first:] for part in gate_full[k]] for k in range(2)] + [gate_cut(k, TP * full, spare) for k in range(2)]),
+            jnp.concatenate(
+                [
+                    down_full[:, first:],
+                    low_down[TP * full :].reshape(TP, spare, rows),
+                    jnp.zeros((TP, -hid % 128, rows), BF16),
+                ],
+                axis=1,
+            ).transpose(0, 2, 1),
+        )
+        small_norm = lax.dynamic_update_slice(jnp.zeros((16, 128), F32), norm_params, (0, (place * rows) % 128))
+        small_bias = lax.dynamic_update_slice(jnp.zeros((3 * head_local,), F32), qkv_bias[0], (place * bias_here,))
+        small = jnp.concatenate([small_norm, small_bias.reshape(-1, 128)]).astype(BF16)
+        segments = segment_ids[0]
+        earlier = jnp.sum((segments[None, :] < segments[:, None]).astype(jnp.int32), axis=1)
+        positions = (jnp.arange(seq_len, dtype=jnp.int32) - earlier).astype(F32)
+        frequency = 10000.0 ** (-2.0 * jnp.arange(ROT // 2, dtype=F32) / ROT)
+        angles = positions[:, None] * frequency[None, :]
+        aux = jnp.concatenate([jnp.cos(angles), jnp.sin(angles), segments[:, None].astype(F32)], axis=1)
+        aux = jnp.pad(aux, ((0, 0), (0, 128 - aux.shape[1])))
+        row = jnp.broadcast_to(segments.astype(F32)[None], (8, seq_len))
 
     rs_q, rs_o, rs_ga, rs_da, rs_gb, rs_db, block_out, input_grad, _, norm_sum, bias_sum = layer(
         count, small, aux, row, tokens_in[0], d_out[0], *weights
     )
 
-    second = full - first
-    gate_parts = [
-        jnp.concatenate(
-            [
-                part
-                for j in range(TP)
-                for part in (
-                    rs_ga[j, :, k * first : (k + 1) * first],
-                    rs_gb[j, :, k * second : (k + 1) * second],
-                )
-            ]
-            + [rs_gb[j, :, 2 * second + k * spare : 2 * second + (k + 1) * spare] for j in range(TP)],
-            axis=1,
-        )
-        for k in range(2)
-    ]
-    gating_shard = lax.optimization_barrier(laid_out(jnp.stack(gate_parts, axis=1))).astype(F32)
-    qkv_shard = jnp.stack(
-        [
-            jnp.concatenate([rs_q[j, :, k * wide : (k + 1) * wide] for j in range(TP)], axis=1)
-            for k in range(3)
-        ],
-        axis=1,
-    ).astype(F32)
-    out_shard = laid_out(rs_o.transpose(0, 2, 1).reshape(head_local, rows)).astype(F32)
-    down_parts = jnp.concatenate([rs_da, rs_db], axis=2).transpose(0, 2, 1)
-    down_shard = laid_out(
-        jnp.concatenate(
-            [down_parts[:, :full].reshape(TP * full, rows), down_parts[:, full:hid].reshape(TP * spare, rows)]
-        )
-    ).astype(F32)
     norm_grad = lax.dynamic_slice_in_dim(norm_sum[:4], (place * rows) % 128, rows, 1)
     bias_grad = bias_sum[:, 0].reshape(TP, 3, wide).transpose(1, 0, 2).reshape(1, 3 * head_local)
     bias_grad = lax.dynamic_slice_in_dim(bias_grad, place * bias_here, bias_here, 1)
+    if rows % 128 == 0 and spare == 64 and bias_here <= 192:
+        planes = [x.transpose(1, 0, 2) for x in (qkv_weight, qkv_first, qkv_second)]
+        new = update(
+            (rs_q, rs_o, rs_ga, rs_gb, rs_da, rs_db),
+            (*planes, out_weight, out_first, out_second, gating_weight, gating_first, gating_second)
+            + (down_weight, down_first, down_second),
+        )
+        new_qkv, new_out, new_gating, new_down = [x.transpose(1, 0, 2) for x in new[:3]], new[3:6], new[6:9], new[9:]
+    else:
+        second = full - first
+        gate_parts = [
+            jnp.concatenate(
+                [
+                    part
+                    for j in range(TP)
+                    for part in (
+                        rs_ga[j, :, k * first : (k + 1) * first],
+                        rs_gb[j, :, k * second : (k + 1) * second],
+                    )
+                ]
+                + [rs_gb[j, :, 2 * second + k * spare : 2 * second + (k + 1) * spare] for j in range(TP)],
+                axis=1,
+            )
+            for k in range(2)
+        ]
+        gating_shard = lax.optimization_barrier(laid_out(jnp.stack(gate_parts, axis=1))).astype(F32)
+        qkv_shard = jnp.stack(
+            [
+                jnp.concatenate([rs_q[j, :, k * wide : (k + 1) * wide] for j in range(TP)], axis=1)
+                for k in range(3)
+            ],
+            axis=1,
+        ).astype(F32)
+        out_shard = laid_out(rs_o.transpose(0, 2, 1).reshape(head_local, rows)).astype(F32)
+        down_parts = jnp.concatenate([rs_da, rs_db], axis=2).transpose(0, 2, 1)
+        down_shard = laid_out(
+            jnp.concatenate(
+                [down_parts[:, :full].reshape(TP * full, rows), down_parts[:, full:hid].reshape(TP * spare, rows)]
+            )
+        ).astype(F32)
+        new_qkv = adamw_update(qkv_weight, qkv_shard, qkv_first, qkv_second, D ** (-0.5), 0.1)
+        new_out = adamw_update(out_weight, out_shard, out_first, out_second, (H * HD // 16) ** (-0.5), 0.1)
+        new_gating = adamw_update(gating_weight, gating_shard, gating_first, gating_second, D ** (-0.5), 0.1)
+        new_down = adamw_update(down_weight, down_shard, down_first, down_second, FF ** (-0.5), 0.1)
     return (
         block_out[None],
         input_grad[None],
-        *adamw_update(qkv_weight, qkv_shard, qkv_first, qkv_second, D ** (-0.5), 0.1),
+        *new_qkv,
         *adamw_update(qkv_bias, bias_grad, bias_first, bias_second, 0.3, 0.0),
-        *adamw_update(out_weight, out_shard, out_first, out_second, (H * HD // 16) ** (-0.5), 0.1),
-        *adamw_update(gating_weight, gating_shard, gating_first, gating_second, D ** (-0.5), 0.1),
-        *adamw_update(down_weight, down_shard, down_first, down_second, FF ** (-0.5), 0.1),
+        *new_out,
+        *new_gating,
+        *new_down,
         *adamw_update(norm_params, norm_grad, norm_first, norm_second, 0.25, 0.0),
     )
 

time: 529 us -> 496 us (0.938)
  other arithmetic: 39.3 us -> 1.95 us
  Pallas kernels: 449 us -> 484 us
  local copies, waits for them, and re-layouts: 29.2 us -> 4.63 us
    pallas_call x0 -> x2, Pallas kernels: none -> 34 us  [the longest x1 26.3 us: update(): pl.pallas_call(update_kernel, in_specs=[any_spec] * 18, out_specs=[any_sp...]
    sub x6 -> x2, other arithmetic: 24.2 us -> 1.95 us  [adamw_update(): weight_old - step_rate * (corrected + decay_rate * weight_old)]
    slice x26 -> x0, local copies, waits for them, and re-layouts: 9.78 us -> none  [the longest x8 5.93 us: per_device(): part[:, first:]]
    another operation x19 -> x0, other arithmetic: 8.91 us -> none  [the longest x13 3.38 us: ranks(): jnp.stack([jnp.concatenate(one, axis=1) for one in zip(*parts, strict=Tru...]
    unnamed x64 -> x18, local copies, waits for them, and re-layouts: 10.3 us -> 3.7 us
where the time goes in v7:
time: 496 us; the launch traced here: 492 us
  Pallas kernels  484 us (98%)
    pallas_call x1, Pallas kernels, layer(): pl.pallas_call(functools.partial(layer_kernel, count), in_specs=[vmem, vm...  450 us
    pallas_call x1, Pallas kernels, update(): pl.pallas_call(update_kernel, in_specs=[any_spec] * 18, out_specs=[any_sp...  26.3 us

profile of v7, /device:TPU:0, one launch (start us, length us, event | category | flops | bytes accessed | tf_op | source)
XLA Modules:
  0.0 491.5 jit_solution(179409818829031635)
XLA Ops:
  0.7 7.6 %prepare.1 = (bf16[40,128]{1,0:T(8,128)(2,1)}, f32[256,128]{1,0:T(8,128)}, f32[8,256]{1,0:T(8,128)}, bf16[4,128,768]{2,1,0:T(8,128)(2,1)}, bf16[4,128,256]{2,1,0...) custom-call(s32[1,256]{1,0:T(1,128)} %refs_0_.1, ...), custom_call_target="tpu_custom_call" | custom-call | tf_op jit(solution)/shard_map/prepare/pallas_call | solution.py:1178
  8.3 0.0 copy-start.2
  8.3 0.0 copy-start.4
  8.3 0.0 copy-start.5
  8.3 0.0 copy-start.3
  8.4 0.0 copy-start.6
  8.4 0.0 copy-start.7
  8.4 449.9 %layer.1 = (bf16[4,128,768]{2,1,0:T(8,128)(2,1)}, bf16[4,128,256]{2,1,0:T(8,128)(2,1)}, bf16[4,128,768]{2,1,0:T(8,128)(2,1)}, bf16[4,128,384]{2,1,0:T(8,128)(2,1...) custom-call(bf16[40,128]{1,0:T(8,128)(2,1)} %get-tuple-element.51.sm, ...), custom_call_target="tpu_custom_call" | custom-call | flops 40000000000 | bytes 60000000 | tf_op jit(solution)/shard_map/layer/pallas_call | solution.py:993
  458.3 0.0 copy-done.2
  458.3 0.0 copy-done.4
  458.3 0.0 copy-done.5
  458.3 1.3 multiply_subtract_fusion
  459.6 0.9 slice.6
  460.6 0.0 copy-done.3
  460.6 0.0 copy-done.6
  460.6 0.0 copy-done.7
  460.6 0.7 multiply_subtract_fusion.1
  461.3 0.0 copy-start.1
  461.3 26.3 %update.1 = (f32[3,128,1024]{2,1,0:T(8,128)}, f32[3,128,1024]{2,1,0:T(8,128)}, f32[3,128,1024]{2,1,0:T(8,128)}, f32[1024,128]{1,0:T(8,128)}, f32[1024,128]{1,0:T...) custom-call(bf16[4,128,768]{2,1,0:T(8,128)(2,1)} %get-tuple-element., ...), custom_call_target="tpu_custom_call" | custom-call | tf_op jit(solution)/shard_map/update/pallas_call | solution.py:1272
  487.6 0.0 copy-done.1
  487.6 0.0 copy-start
  487.6 1.3 copy.45
  488.9 1.0 copy-done
  489.9 1.3 copy.46
  (2 shorter events, 0.0 us)
Async XLA Ops:
  8.3 450.0 %copy-start.2 = (f32[4,128]{1,0:T(4,128)S(1)}, f32[4,128]{1,0:T(4,128)}, u32[]{:S(2)}) copy-start(f32[4,128]{1,0:T(4,128)} %refs_1_.1) | copy-start | bytes 6148
  8.3 450.0 %copy-start.4 = (f32[4,128]{1,0:T(4,128)S(1)}, f32[4,128]{1,0:T(4,128)}, u32[]{:S(2)}) copy-start(f32[4,128]{1,0:T(4,128)} %param.40) | copy-start | bytes 6148
  8.3 450.0 %copy-start.5 = (f32[4,128]{1,0:T(4,128)S(1)}, f32[4,128]{1,0:T(4,128)}, u32[]{:S(2)}) copy-start(f32[4,128]{1,0:T(4,128)} %param.41) | copy-start | bytes 6148
  8.3 452.2 %copy-start.3 = (f32[1,192]{1,0:T(1,128)S(1)}, f32[1,192]{1,0:T(1,128)}, u32[]{:S(2)}) copy-start(f32[1,192]{1,0:T(1,128)} %refs_2_.1) | copy-start | bytes 2308
  8.4 452.2 %copy-start.6 = (f32[1,192]{1,0:T(1,128)S(1)}, f32[1,192]{1,0:T(1,128)}, u32[]{:S(2)}) copy-start(f32[1,192]{1,0:T(1,128)} %param.32) | copy-start | bytes 2308
  8.4 452.2 %copy-start.7 = (f32[1,192]{1,0:T(1,128)S(1)}, f32[1,192]{1,0:T(1,128)}, u32[]{:S(2)}) copy-start(f32[1,192]{1,0:T(1,128)} %param.33) | copy-start | bytes 2308
  461.3 26.3 %copy-start.1 = (f32[256,2048]{1,0:T(8,128)S(1)}, f32[256,2048]{1,0:T(8,128)}, u32[]{:S(2)}) copy-start(f32[256,2048]{1,0:T(8,128)} %get-tuple-element.60) | copy-start | bytes 6291460
  487.6 2.3 copy-start

commit v8 on v7

--- a/solution.py
+++ b/solution.py
@@ -935,10 +935,10 @@
 
     scatter_da.reduce()
     scatter_ga.reduce()
+    scatter_q.combine()
+    scatter_o.combine()
     scatter_db.reduce()
     scatter_gb.reduce()
-    scatter_q.combine()
-    scatter_o.combine()
 
     for k in range(1, p.lines):
         bias_copy(k).wait_recv()

time: 496 us -> 496 us (level)
  no operation moved by 1% of the time
where the time goes in v8:
time: 496 us; the launch traced here: 492 us
  Pallas kernels  484 us (98%)
    pallas_call x1, Pallas kernels, layer(): pl.pallas_call(functools.partial(layer_kernel, count), in_specs=[vmem, vm...  450 us
    pallas_call x1, Pallas kernels, update(): pl.pallas_call(update_kernel, in_specs=[any_spec] * 18, out_specs=[any_sp...  26.3 us

profile of v8, /device:TPU:0, one launch (start us, length us, event | category | flops | bytes accessed | tf_op | source)
XLA Modules:
  0.0 491.5 jit_solution(9249507807924800695)
XLA Ops:
  0.7 7.6 %prepare.1 = (bf16[40,128]{1,0:T(8,128)(2,1)}, f32[256,128]{1,0:T(8,128)}, f32[8,256]{1,0:T(8,128)}, bf16[4,128,768]{2,1,0:T(8,128)(2,1)}, bf16[4,128,256]{2,1,0...) custom-call(s32[1,256]{1,0:T(1,128)} %refs_0_.1, ...), custom_call_target="tpu_custom_call" | custom-call | tf_op jit(solution)/shard_map/prepare/pallas_call | solution.py:1178
  8.3 0.0 copy-start.2
  8.3 0.0 copy-start.4
  8.3 0.0 copy-start.5
  8.3 0.0 copy-start.3
  8.4 0.0 copy-start.6
  8.4 0.0 copy-start.7
  8.4 449.9 %layer.1 = (bf16[4,128,768]{2,1,0:T(8,128)(2,1)}, bf16[4,128,256]{2,1,0:T(8,128)(2,1)}, bf16[4,128,768]{2,1,0:T(8,128)(2,1)}, bf16[4,128,384]{2,1,0:T(8,128)(2,1...) custom-call(bf16[40,128]{1,0:T(8,128)(2,1)} %get-tuple-element.51.sm, ...), custom_call_target="tpu_custom_call" | custom-call | flops 40000000000 | bytes 60000000 | tf_op jit(solution)/shard_map/layer/pallas_call | solution.py:993
  458.3 0.0 copy-done.2
  458.3 0.0 copy-done.4
  458.3 0.0 copy-done.5
  458.3 1.3 multiply_subtract_fusion
  459.6 0.9 slice.6
  460.6 0.0 copy-done.3
  460.6 0.0 copy-done.6
  460.6 0.0 copy-done.7
  460.6 0.7 multiply_subtract_fusion.1
  461.3 0.0 copy-start.1
  461.3 26.3 %update.1 = (f32[3,128,1024]{2,1,0:T(8,128)}, f32[3,128,1024]{2,1,0:T(8,128)}, f32[3,128,1024]{2,1,0:T(8,128)}, f32[1024,128]{1,0:T(8,128)}, f32[1024,128]{1,0:T...) custom-call(bf16[4,128,768]{2,1,0:T(8,128)(2,1)} %get-tuple-element., ...), custom_call_target="tpu_custom_call" | custom-call | tf_op jit(solution)/shard_map/update/pallas_call | solution.py:1272
  487.6 0.0 copy-done.1
  487.6 0.0 copy-start
  487.6 1.3 copy.45
  488.9 1.0 copy-done
  489.9 1.3 copy.46
  (2 shorter events, 0.0 us)
Async XLA Ops:
  8.3 450.0 %copy-start.2 = (f32[4,128]{1,0:T(4,128)S(1)}, f32[4,128]{1,0:T(4,128)}, u32[]{:S(2)}) copy-start(f32[4,128]{1,0:T(4,128)} %refs_1_.1) | copy-start | bytes 6148
  8.3 450.0 %copy-start.4 = (f32[4,128]{1,0:T(4,128)S(1)}, f32[4,128]{1,0:T(4,128)}, u32[]{:S(2)}) copy-start(f32[4,128]{1,0:T(4,128)} %param.40) | copy-start | bytes 6148
  8.3 450.0 %copy-start.5 = (f32[4,128]{1,0:T(4,128)S(1)}, f32[4,128]{1,0:T(4,128)}, u32[]{:S(2)}) copy-start(f32[4,128]{1,0:T(4,128)} %param.41) | copy-start | bytes 6148
  8.3 452.2 %copy-start.3 = (f32[1,192]{1,0:T(1,128)S(1)}, f32[1,192]{1,0:T(1,128)}, u32[]{:S(2)}) copy-start(f32[1,192]{1,0:T(1,128)} %refs_2_.1) | copy-start | bytes 2308
  8.4 452.2 %copy-start.6 = (f32[1,192]{1,0:T(1,128)S(1)}, f32[1,192]{1,0:T(1,128)}, u32[]{:S(2)}) copy-start(f32[1,192]{1,0:T(1,128)} %param.32) | copy-start | bytes 2308
  8.4 452.2 %copy-start.7 = (f32[1,192]{1,0:T(1,128)S(1)}, f32[1,192]{1,0:T(1,128)}, u32[]{:S(2)}) copy-start(f32[1,192]{1,0:T(1,128)} %param.33) | copy-start | bytes 2308
  461.3 26.3 %copy-start.1 = (f32[256,2048]{1,0:T(8,128)S(1)}, f32[256,2048]{1,0:T(8,128)}, u32[]{:S(2)}) copy-start(f32[256,2048]{1,0:T(8,128)} %get-tuple-element.60) | copy-start | bytes 6291460
  487.6 2.3 copy-start
